TPU v7x, 256 devices: a whole 4x4x8 slice. The times are simulated.
256 devices in a mesh: frame: 8 (over x, y_lo), patch: 32 (over y_hi, z, core).
Axes of the slice: x: 4, y: 4 (y_hi: 2, y_lo: 2; y = y_hi * 2 + y_lo), z: 8, core: 2. Of those that a mesh axis runs over, the one named last changes fastest.
Arguments:
- queries: bfloat16 [8, 4096, 1024], P('frame', 'patch'), may hold values from -8 to 8
- key_states: bfloat16 [8, 4096, 1024], P('frame', 'patch'), may hold values from -8 to 8
- value_states: bfloat16 [8, 4096, 1024], P('frame', 'patch'), may hold values from -6 to 6
- out_grad: bfloat16 [8, 4096, 1024], P('frame', 'patch'), may hold values from -6 to 6
Outputs:
- grad_queries: bfloat16 [8, 4096, 1024], P('frame', 'patch')
- grad_keys: bfloat16 [8, 4096, 1024], P('frame', 'patch')
- grad_values: bfloat16 [8, 4096, 1024], P('frame', 'patch')
All inputs are finite; a program needn't handle non-finite values.
Results may differ from a plain program's by a relative error of at most 0.0076.
Values may be sent and summed in bfloat16 or wider, within the bound.
No kernel may reach another device: no remote copies, remote signals or barrier semaphores. Data moves between devices by JAX's collectives and lax.ppermute only.
A program may use at most 64 MiB of HBM per device.

v0:
```python
import math

import jax
import jax.numpy as jnp
from jax import lax
from jax.sharding import PartitionSpec as P

HEADS = 8
HD = 128


def with_halo(block, sides, width):
    for axis, dim in sides:
        count = lax.axis_size(axis)
        forward = [(i, i + 1) for i in range(count - 1)]
        forward.append((count - 1, 0))
        backward = [(target, source) for source, target in forward]
        low = lax.ppermute(
            lax.slice_in_dim(block, block.shape[dim] - width, None, axis=dim), axis, forward
        )
        high = lax.ppermute(lax.slice_in_dim(block, 0, width, axis=dim), axis, backward)
        block = jnp.concatenate([low, block, high], axis=dim)
    return block


def shifted(value, axis, steps):
    count = lax.axis_size(axis)
    pairs = [(source, (source + steps) % count) for source in range(count)]
    return lax.ppermute(value, axis, pairs)


def head_split(tensor, tok_rows):
    return tensor.reshape(tok_rows, HEADS, HD)


def score_tile(query_part, key_part, scale_factor):
    return (
        jnp.einsum("thd,shd->hts", query_part, key_part, preferred_element_type=jnp.float32)
        * scale_factor
    )


def tile_grads(query_part, grad_part, key_part, value_part, total_part, delta_part, scale_factor):
    scores = score_tile(query_part, key_part, scale_factor)
    prob_full = jnp.exp(scores - total_part[:, :, None])
    grad_prob = jnp.einsum(
        "thd,shd->hts", grad_part, value_part, preferred_element_type=jnp.float32
    )
    dscore = (prob_full * (grad_prob - delta_part[:, :, None])).astype(jnp.bfloat16)
    return (prob_full.astype(jnp.bfloat16), dscore)


def on_device(queries, key_states, value_states, out_grad):
    frames_dev, patches_dev, channels = queries.shape
    tok_rows = frames_dev * patches_dev
    scale_factor = 1.0 / math.sqrt(HD)
    query_loc = head_split(queries, tok_rows)
    key_loc = head_split(key_states, tok_rows)
    value_loc = head_split(value_states, tok_rows)
    grad_loc = head_split(out_grad, tok_rows)
    steps_three = (-1, 0, 1)
    kv_local = jnp.concatenate(
        [key_states.reshape(tok_rows, channels), value_states.reshape(tok_rows, channels)], axis=1
    )
    kv_column = with_halo(kv_local[None], (("patch", 0),), 1)
    kv_rows = {0: kv_column}
    for frame_step in (-1, 1):
        kv_rows[frame_step] = shifted(kv_column, "frame", -frame_step)
    window = []
    for frame_step in steps_three:
        for patch_step in steps_three:
            kv_block = kv_rows[frame_step][patch_step + 1]
            window.append(
                (
                    frame_step,
                    patch_step,
                    head_split(kv_block[:, :channels], tok_rows),
                    head_split(kv_block[:, channels:], tok_rows),
                )
            )
    run_max = jnp.full((HEADS, tok_rows), -jnp.inf, jnp.float32)
    run_total = jnp.zeros((HEADS, tok_rows), jnp.float32)
    for frame_step, patch_step, key_part, value_part in window:
        scores = score_tile(query_loc, key_part, scale_factor)
        new_max = jnp.maximum(run_max, jnp.max(scores, axis=-1))
        run_total = run_total * jnp.exp(run_max - new_max) + jnp.sum(
            jnp.exp(scores - new_max[:, :, None]), axis=-1
        )
        run_max = new_max
    log_total = run_max + jnp.log(run_total)
    forward_out = jnp.zeros((tok_rows, HEADS, HD), jnp.float32)
    for frame_step, patch_step, key_part, value_part in window:
        scores = score_tile(query_loc, key_part, scale_factor)
        prob_half = jnp.exp(scores - log_total[:, :, None]).astype(jnp.bfloat16)
        forward_out = forward_out + jnp.einsum(
            "hts,shd->thd", prob_half, value_part, preferred_element_type=jnp.float32
        )
    row_delta = jnp.sum(grad_loc.astype(jnp.float32) * forward_out, axis=-1).T
    query_acc = jnp.zeros((tok_rows, HEADS, HD), jnp.float32)
    for frame_step, patch_step, key_part, value_part in window:
        prob_half, dscore = tile_grads(
            query_loc, grad_loc, key_part, value_part, log_total, row_delta, scale_factor
        )
        query_acc = query_acc + jnp.einsum(
            "hts,shd->thd", dscore, key_part, preferred_element_type=jnp.float32
        )
    query_grad_local = jnp.concatenate(
        [queries.reshape(tok_rows, channels), out_grad.reshape(tok_rows, channels)], axis=1
    )
    query_column = with_halo(query_grad_local[None], (("patch", 0),), 1)
    query_rows = {0: query_column}
    for frame_step in (-1, 1):
        query_rows[frame_step] = shifted(query_column, "frame", -frame_step)
    stats_local = jnp.concatenate([log_total, row_delta], axis=0)[None, None]
    stats_near = with_halo(stats_local, (("frame", 0), ("patch", 1)), 1)
    key_acc = jnp.zeros((tok_rows, HEADS, HD), jnp.float32)
    value_acc = jnp.zeros((tok_rows, HEADS, HD), jnp.float32)
    for frame_step in steps_three:
        for patch_step in steps_three:
            query_block = query_rows[frame_step][patch_step + 1]
            query_part = head_split(query_block[:, :channels], tok_rows)
            grad_part = head_split(query_block[:, channels:], tok_rows)
            stats_part = stats_near[frame_step + 1, patch_step + 1]
            prob_half, dscore = tile_grads(
                query_part,
                grad_part,
                key_loc,
                value_loc,
                stats_part[:HEADS],
                stats_part[HEADS:],
                scale_factor,
            )
            key_acc = key_acc + jnp.einsum(
                "hts,thd->shd", dscore, query_part, preferred_element_type=jnp.float32
            )
            value_acc = value_acc + jnp.einsum(
                "hts,thd->shd", prob_half, grad_part, preferred_element_type=jnp.float32
            )
    key_value = jnp.concatenate(
        [key_acc.reshape(tok_rows, channels), value_acc.reshape(tok_rows, channels)], axis=1
    )
    grad_queries = (
        (query_acc * scale_factor).astype(jnp.bfloat16).reshape(frames_dev, patches_dev, channels)
    )
    grad_keys = (
        (key_value[:, :channels] * scale_factor)
        .astype(jnp.bfloat16)
        .reshape(frames_dev, patches_dev, channels)
    )
    grad_values = (
        key_value[:, channels:].astype(jnp.bfloat16).reshape(frames_dev, patches_dev, channels)
    )
    return (grad_queries, grad_keys, grad_values)


def solution(mesh):
    placed = (
        P("frame", "patch", None),
        P("frame", "patch", None),
        P("frame", "patch", None),
        P("frame", "patch", None),
    )
    return jax.shard_map(
        on_device,
        mesh=mesh,
        in_specs=placed,
        out_specs=(P("frame", "patch", None), P("frame", "patch", None), P("frame", "patch", None)),
        check_vma=False,
    )
```

profile of v0, /device:TPU:1, one launch (start us, length us, event | category | flops | bytes accessed | tf_op | source)
XLA Modules:
  0.0 216.8 jit_solution(11802532157225693479)
XLA Ops:
  0.6 1.2 copy.85
  3.8 3.2 %collective-permute-start.1 = (bf16[1,128,2048]{1,2,0:T(8,128)(2,1)}, bf16[1,128,2048]{1,2,0:T(8,128)(2,1)S(1)}, u32[]{:S(2)}, u32[]{:S(2)}) collective-permute-start(bf16[1,128,2048]{1,2,0:T(8,128)(2,1)} %maximum_bitcast_fusion), channel_id=1, source_target_pairs={{1,0},{2,1},{3,2},{4,3},{5,4},{6,5},{7,6},{8,7},{9,8},{10,9},{11,1... | collective-permute-start | bytes 1572872 | tf_op jit(solution)/shard_map/ppermute | solution.py:21
  7.4 6.3 %collective-permute-start.5 = (bf16[1,128,2048]{1,2,0:T(8,128)(2,1)S(1)}, bf16[1,128,2048]{1,2,0:T(8,128)(2,1)S(1)}, u32[]{:S(2)}, u32[]{:S(2)}) collective-permute-start(bf16[1,128,2048]{1,2,0:T(8,128)(2,1)S(1)} %maximum_bitcast_fusion.1), channel_id=1, source_target_pairs={{1,0},{2,1},{3,2},{4,3},{5,4},{6,5},{7,6},{8,7},{9,8},{10,9},{11,1... | collective-permute-start | bytes 1572872 | tf_op jit(solution)/shard_map/ppermute | solution.py:21
  14.8 1.2 pad_maximum_fusion
  16.1 2.7 %collective-permute-start.3 = (bf16[3,128,2048]{1,2,0:T(8,128)(2,1)S(1)}, bf16[3,128,2048]{1,2,0:T(8,128)(2,1)S(1)}, u32[]{:S(2)}, u32[]{:S(2)}) collective-permute-start(bf16[3,128,2048]{1,2,0:T(8,128)(2,1)S(1)} %pad_maximum_fusion), channel_id=1, source_target_pairs={{0,224},{32,0},{64,32},{96,64},{128,96},{160,128},{192,160},{224,1... | collective-permute-start | bytes 4718600 | tf_op jit(solution)/shard_map/ppermute | solution.py:29
  20.5 1.4 pad_maximum_fusion.1
  21.8 2.8 %collective-permute-start.11 = (bf16[3,128,2048]{1,2,0:T(8,128)(2,1)}, bf16[3,128,2048]{1,2,0:T(8,128)(2,1)}, u32[]{:S(2)}, u32[]{:S(2)}) collective-permute-start(bf16[3,128,2048]{1,2,0:T(8,128)(2,1)} %pad_maximum_fusion.1), channel_id=1, source_target_pairs={{0,224},{32,0},{64,32},{96,64},{128,96},{160,128},{192,160},{224,1... | collective-permute-start | bytes 4718600 | tf_op jit(solution)/shard_map/ppermute | solution.py:29
  27.2 103.0 %collective-permute-done.3 = bf16[3,128,2048]{1,2,0:T(8,128)(2,1)S(1)} collective-permute-done((bf16[3,128,2048]{1,2,0:T(8,128)(2,1)S(1)}, bf16[3,128,2048]{1,2,0:T(8,128)(2,1)S(1)}, u32[]{:S(2)}, u32[]{:S(2)}) %collective-permute-start.3) | collective-permute-done | bytes 1572896 | tf_op jit(solution)/shard_map/ppermute | solution.py:29
  137.4 1.5 collective-permute-start.8
  140.2 2.5 %fusion.98 = f32[8,128,128]{2,1,0:T(8,128)} fusion(bf16[128,8,128]{0,2,1:T(8,128)(2,1)} %bitcast.468, bf16[128,8,128]{0,2,1:T(8,128)(2,1)} %bitcast.440, bf16[128,8,128]{0,2,1:T(8,128)(2,1)S(1)} %bitcast.385, f32[8,128,128]{1,2,0:T(8,128)} %copy-done, f32[8,128]{1,0:T(8,128)S(1)} %bitcast.502, f32[8,128]{1,0:T(8,128)S(1)} %log_add_fusion), kind=kOutput, calls=%fused_computation.166 | convolution fusion | flops 67633152 | bytes 1843200 | tf_op jit(solution)/shard_map/hts,shd->thd/dot_general | solution.py:104
  142.6 2.6 %convolution_add_fusion.8 = f32[8,128,128]{2,1,0:T(8,128)} fusion(f32[8,128,128]{2,1,0:T(8,128)} %fusion.98, bf16[128,8,128]{0,2,1:T(8,128)(2,1)} %bitcast.486, bf16[128,8,128]{0,2,1:T(8,128)(2,1)} %bitcast.466, bf16[128,8,128]{0,2,1:T(8,128)(2,1)S(1)} %bitcast.386, f32[8,128,128]{1,2,0:T(8,128)} %copy-done.5, f32[8,128]{1,0:T(8,128)S(1)} %bitcast.503, ...), kind=kOutput, calls=%fused_computation.119 | convolution fusion | flops 67764224 | bytes 2367488 | tf_op jit(solution)/shard_map/hts,shd->thd/dot_general | solution.py:104
  145.2 2.6 %convolution_add_fusion.7 = f32[8,128,128]{2,1,0:T(8,128)} fusion(f32[8,128,128]{2,1,0:T(8,128)} %convolution_add_fusion.8, bf16[128,8,128]{0,2,1:T(8,128)(2,1)} %bitcast.482, bf16[128,8,128]{0,2,1:T(8,128)(2,1)} %bitcast.462, bf16[128,8,128]{0,2,1:T(8,128)(2,1)S(1)} %bitcast.387, f32[8,128,128]{1,2,0:T(8,128)} %copy-done.4, f32[8,128]{1,0:T(8,128)S(1)} %bitcast.504, ...), kind=kOutput, calls=%fused_computation.112 | convolution fusion | flops 67764224 | bytes 2367488 | tf_op jit(solution)/shard_map/hts,shd->thd/dot_general | solution.py:104
  147.8 2.6 %fusion.58 = f32[128,8,128]{0,2,1:T(8,128)} fusion(f32[8,128,128]{2,1,0:T(8,128)} %convolution_add_fusion.7, bf16[128,8,128]{0,2,1:T(8,128)(2,1)} %bitcast.450, bf16[128,8,128]{0,2,1:T(8,128)(2,1)} %bitcast.436, bf16[128,8,128]{0,2,1:T(8,128)(2,1)S(1)} %bitcast.388, f32[8,128,128]{1,2,0:T(8,128)} %copy-done.3, f32[8,128]{1,0:T(8,128)S(1)} %bitcast.505, ...), kind=kOutput, calls=%fused_computation.108 | convolution fusion | flops 67764224 | bytes 2367488 | tf_op jit(solution)/shard_map/hts,shd->thd/dot_general | solution.py:104
  150.4 13.8 %collective-permute-done.11 = bf16[3,128,2048]{1,2,0:T(8,128)(2,1)} collective-permute-done((bf16[3,128,2048]{1,2,0:T(8,128)(2,1)}, bf16[3,128,2048]{1,2,0:T(8,128)(2,1)}, u32[]{:S(2)}, u32[]{:S(2)}) %collective-permute-start.11) | collective-permute-done | bytes 1572896 | tf_op jit(solution)/shard_map/ppermute | solution.py:29
  164.3 1.5 slice_bitcast_fusion.2
  168.8 2.2 %convolution_bitcast_fusion.10 = f32[128,8,128]{0,2,1:T(8,128)} fusion(bf16[128,8,128]{0,2,1:T(8,128)(2,1)} %bitcast.448, bf16[128,8,128]{0,2,1:T(8,128)(2,1)} %bitcast.434, bf16[128,8,128]{0,2,1:T(8,128)(2,1)S(1)} %bitcast.389, f32[8,128,128]{1,2,0:T(8,128)S(1)} %get-tuple-element.78, f32[8,128]{1,0:T(8,128)S(1)} %bitcast.506, f32[8,128]{1,0:T(8,128)S(1)} %log_add_fusion), kind=kOutput, calls=%fused_computation.12 | convolution fusion | flops 67633152 | bytes 1843200 | tf_op jit(solution)/shard_map/hts,shd->thd/dot_general | solution.py:104
  171.0 2.3 %convolution_bitcast_fusion.11 = f32[128,8,128]{0,2,1:T(8,128)} fusion(bf16[128,8,128]{0,2,1:T(8,128)(2,1)} %bitcast.476, bf16[128,8,128]{0,2,1:T(8,128)(2,1)} %bitcast.454, bf16[128,8,128]{0,2,1:T(8,128)(2,1)S(1)} %bitcast.390, f32[8,128,128]{1,2,0:T(8,128)S(1)} %get-tuple-element.80, f32[8,128]{1,0:T(8,128)S(1)} %bitcast.507, f32[8,128]{1,0:T(8,128)S(1)} %log_add_fusion), kind=kOutput, calls=%fused_computation.13 | convolution fusion | flops 67633152 | bytes 1843200 | tf_op jit(solution)/shard_map/hts,shd->thd/dot_general | solution.py:104
  173.3 1.2 convolution_bitcast_fusion.12
  174.6 2.2 %slice_bitcast_fusion.3 = (bf16[128,2048]{0,1:T(8,128)(2,1)S(1)}, bf16[128,2048]{0,1:T(8,128)(2,1)}, bf16[128,2048]{0,1:T(8,128)(2,1)S(1)}) fusion(bf16[3,128,2048]{1,2,0:T(8,128)(2,1)} %collective-permute-done.6), kind=kLoop, calls=%fused_computation.170 | loop fusion | bytes 3145728 | tf_op jit(solution)/shard_map/squeeze | solution.py:120
  178.5 2.5 %fusion.95 = bf16[128,8,128]{0,2,1:T(8,128)(2,1)} fusion(f32[128,8,128]{0,2,1:T(8,128)} %convolution_bitcast_fusion.10, f32[128,8,128]{0,2,1:T(8,128)} %convolution_bitcast_fusion.11, f32[128,8,128]{0,2,1:T(8,128)} %convolution_bitcast_fusion.12, f32[128,8,128]{0,2,1:T(8,128)S(1)} %copy-done.39, bf16[128,8,128]{0,2,1:T(8,128)(2,1)S(1)} %bitcast.428, ...), kind=kOutput, calls=%fused_computation.163 | convolution fusion | flops 68419584 | bytes 3678208 | tf_op jit(solution)/shard_map/hts,shd->thd/dot_general | solution.py:104
  182.1 1.8 copy.146
  187.1 1.3 convolution_bitcast_fusion.7
  188.8 1.3 fusion.97
  191.5 1.3 convolution_bitcast_fusion.6
  195.2 1.3 convolution_bitcast_fusion.8
  196.9 1.3 fusion.42
  198.5 2.5 %convolution_add_fusion.5 = f32[8,128,128]{2,1,0:T(8,128)} fusion(f32[8,128,128]{2,1,0:T(8,128)} %fusion.97, bf16[128,8,128]{0,2,1:T(8,128)(2,1)} %bitcast.483, f32[8,128,128]{2,1,0:T(8,128)S(1)} %fusion.48, bf16[128,8,128]{0,2,1:T(8,128)(2,1)} %bitcast.457, f32[8,128]{1,0:T(8,128)S(1)} %get-tuple-element.71, bf16[128,8,128]{2,1,0:T(8,128)(2,1)S(1)} %bitcast.411), kind=kOutput, calls=%fused_computation.87 | convolution fusion | flops 67633152 | bytes 2363392 | tf_op jit(solution)/shard_map/hts,thd->shd/dot_general | solution.py:133
  201.0 2.6 %convolution_add_fusion.4 = f32[8,128,128]{2,1,0:T(8,128)} fusion(f32[8,128,128]{2,1,0:T(8,128)} %convolution_add_fusion.5, bf16[128,8,128]{0,2,1:T(8,128)(2,1)} %bitcast.480, f32[8,128,128]{2,1,0:T(8,128)S(1)} %fusion.42, bf16[128,8,128]{0,2,1:T(8,128)(2,1)} %bitcast.455, f32[8,128]{1,0:T(8,128)S(1)} %get-tuple-element.65, ...), kind=kOutput, calls=%fused_computation.76 | convolution fusion | flops 67633152 | bytes 2363392 | tf_op jit(solution)/shard_map/hts,thd->shd/dot_general | solution.py:133
  203.6 2.4 %fusion.36 = f32[128,8,128]{0,2,1:T(8,128)} fusion(f32[8,128,128]{2,1,0:T(8,128)} %convolution_add_fusion.4, bf16[128,8,128]{0,2,1:T(8,128)(2,1)} %bitcast.445, f32[8,128,128]{2,1,0:T(8,128)S(1)} %fusion.39, bf16[128,8,128]{0,2,1:T(8,128)(2,1)S(1)} %bitcast.431, f32[8,128]{1,0:T(8,128)S(1)} %get-tuple-element.67, bf16[128,8,128]{2,1,0:T(8,128)(2,1)S(1)} %bitcast.413), kind=kOutput, calls=%fused_computation.70 | convolution fusion | flops 67633152 | bytes 2363392 | tf_op jit(solution)/shard_map/hts,thd->shd/dot_general | solution.py:133
  206.0 2.2 %fusion.21 = f32[128,8,128]{0,2,1:T(8,128)} fusion(f32[128,8,128]{0,2,1:T(8,128)} %fusion.36, bf16[128,8,128]{0,2,1:T(8,128)(2,1)S(1)} %bitcast.404, bf16[8,128,128]{2,1,0:T(8,128)(2,1)} %fusion.80), kind=kOutput, calls=%fused_computation.43 | convolution fusion | flops 33685504 | bytes 1572864 | tf_op jit(solution)/shard_map/hts,thd->shd/dot_general | solution.py:133
  209.4 2.3 %fusion.94 = bf16[128,8,128]{0,2,1:T(8,128)(2,1)S(1)} fusion(f32[128,8,128]{0,2,1:T(8,128)} %convolution_bitcast_fusion.6, f32[128,8,128]{0,2,1:T(8,128)} %convolution_bitcast_fusion.7, f32[128,8,128]{0,2,1:T(8,128)} %convolution_bitcast_fusion.8, f32[128,8,128]{0,2,1:T(8,128)} %fusion.21, bf16[128,8,128]{0,2,1:T(8,128)(2,1)} %bitcast.443, ...), kind=kOutput, calls=%fused_computation.162 | convolution fusion | flops 68288512 | bytes 3674112 | tf_op jit(solution)/shard_map/hts,thd->shd/dot_general | solution.py:133
  212.5 1.4 convolution_add_fusion.2
  (188 shorter events, 34.1 us)
Async XLA Ops:
  0.6 6.4 %copy-start.46 = (bf16[1,128,1024]{2,1,0:T(8,128)(2,1)S(1)}, bf16[1,128,1024]{2,1,0:T(8,128)(2,1)}, u32[]{:S(2)}) copy-start(bf16[1,128,1024]{2,1,0:T(8,128)(2,1)} %param.7) | copy-start | bytes 786436
  0.6 6.6 %copy-start.47 = (bf16[1,128,1024]{2,1,0:T(8,128)(2,1)S(1)}, bf16[1,128,1024]{2,1,0:T(8,128)(2,1)}, u32[]{:S(2)}) copy-start(bf16[1,128,1024]{2,1,0:T(8,128)(2,1)} %param.4) | copy-start | bytes 786436
  3.0 10.8 %copy-start.44 = (bf16[1,128,1024]{2,1,0:T(8,128)(2,1)S(1)}, bf16[1,128,1024]{2,1,0:T(8,128)(2,1)}, u32[]{:S(2)}) copy-start(bf16[1,128,1024]{2,1,0:T(8,128)(2,1)} %param.5) | copy-start | bytes 786436
  3.8 10.0 %copy-start.45 = (bf16[1,128,1024]{2,1,0:T(8,128)(2,1)S(1)}, bf16[1,128,1024]{2,1,0:T(8,128)(2,1)}, u32[]{:S(2)}) copy-start(bf16[1,128,1024]{2,1,0:T(8,128)(2,1)} %param.6) | copy-start | bytes 786436
  3.8 10.5 %collective-permute-start.1 = (bf16[1,128,2048]{1,2,0:T(8,128)(2,1)}, bf16[1,128,2048]{1,2,0:T(8,128)(2,1)S(1)}, u32[]{:S(2)}, u32[]{:S(2)}) collective-permute-start(bf16[1,128,2048]{1,2,0:T(8,128)(2,1)} %maximum_bitcast_fusion), channel_id=1, source_target_pairs={{1,0},{2,1},{3,2},{4,3},{5,4},{6,5},{7,6},{8,7},{9,8},{10,9},{11,1... | collective-permute-start | bytes 1572872 | tf_op jit(solution)/shard_map/ppermute | solution.py:21
  7.0 7.8 %collective-permute-start = (bf16[1,128,2048]{1,2,0:T(8,128)(2,1)}, bf16[1,128,2048]{1,2,0:T(8,128)(2,1)S(1)}, u32[]{:S(2)}, u32[]{:S(2)}) collective-permute-start(bf16[1,128,2048]{1,2,0:T(8,128)(2,1)} %maximum_bitcast_fusion), channel_id=1, source_target_pairs={{0,1},{1,2},{2,3},{3,4},{4,5},{5,6},{6,7},{7,8},{8,9},{9,10},{10,1... | collective-permute-start | bytes 1572872 | tf_op jit(solution)/shard_map/ppermute | solution.py:18
  7.4 12.4 %collective-permute-start.5 = (bf16[1,128,2048]{1,2,0:T(8,128)(2,1)S(1)}, bf16[1,128,2048]{1,2,0:T(8,128)(2,1)S(1)}, u32[]{:S(2)}, u32[]{:S(2)}) collective-permute-start(bf16[1,128,2048]{1,2,0:T(8,128)(2,1)S(1)} %maximum_bitcast_fusion.1), channel_id=1, source_target_pairs={{1,0},{2,1},{3,2},{4,3},{5,4},{6,5},{7,6},{8,7},{9,8},{10,9},{11,1... | collective-permute-start | bytes 1572872 | tf_op jit(solution)/shard_map/ppermute | solution.py:21
  13.7 6.8 %collective-permute-start.4 = (bf16[1,128,2048]{1,2,0:T(8,128)(2,1)S(1)}, bf16[1,128,2048]{1,2,0:T(8,128)(2,1)S(1)}, u32[]{:S(2)}, u32[]{:S(2)}) collective-permute-start(bf16[1,128,2048]{1,2,0:T(8,128)(2,1)S(1)} %maximum_bitcast_fusion.1), channel_id=1, source_target_pairs={{0,1},{1,2},{2,3},{3,4},{4,5},{5,6},{6,7},{7,8},{8,9},{9,10},{10,1... | collective-permute-start | bytes 1572872 | tf_op jit(solution)/shard_map/ppermute | solution.py:18
  16.1 114.2 %collective-permute-start.3 = (bf16[3,128,2048]{1,2,0:T(8,128)(2,1)S(1)}, bf16[3,128,2048]{1,2,0:T(8,128)(2,1)S(1)}, u32[]{:S(2)}, u32[]{:S(2)}) collective-permute-start(bf16[3,128,2048]{1,2,0:T(8,128)(2,1)S(1)} %pad_maximum_fusion), channel_id=1, source_target_pairs={{0,224},{32,0},{64,32},{96,64},{128,96},{160,128},{192,160},{224,1... | collective-permute-start | bytes 4718600 | tf_op jit(solution)/shard_map/ppermute | solution.py:29
  18.7 113.5 %collective-permute-start.2 = (bf16[3,128,2048]{1,2,0:T(8,128)(2,1)S(1)}, bf16[3,128,2048]{1,2,0:T(8,128)(2,1)S(1)}, u32[]{:S(2)}, u32[]{:S(2)}) collective-permute-start(bf16[3,128,2048]{1,2,0:T(8,128)(2,1)S(1)} %pad_maximum_fusion), channel_id=1, source_target_pairs={{0,32},{32,64},{64,96},{96,128},{128,160},{160,192},{192,224},{224... | collective-permute-start | bytes 4718600 | tf_op jit(solution)/shard_map/ppermute | solution.py:29
  21.8 142.4 %collective-permute-start.11 = (bf16[3,128,2048]{1,2,0:T(8,128)(2,1)}, bf16[3,128,2048]{1,2,0:T(8,128)(2,1)}, u32[]{:S(2)}, u32[]{:S(2)}) collective-permute-start(bf16[3,128,2048]{1,2,0:T(8,128)(2,1)} %pad_maximum_fusion.1), channel_id=1, source_target_pairs={{0,224},{32,0},{64,32},{96,64},{128,96},{160,128},{192,160},{224,1... | collective-permute-start | bytes 4718600 | tf_op jit(solution)/shard_map/ppermute | solution.py:29
  24.7 149.9 %collective-permute-start.6 = (bf16[3,128,2048]{1,2,0:T(8,128)(2,1)}, bf16[3,128,2048]{1,2,0:T(8,128)(2,1)}, u32[]{:S(2)}, u32[]{:S(2)}) collective-permute-start(bf16[3,128,2048]{1,2,0:T(8,128)(2,1)} %pad_maximum_fusion.1), channel_id=1, source_target_pairs={{0,32},{32,64},{64,96},{96,128},{128,160},{160,192},{192,224},{224... | collective-permute-start | bytes 4718600 | tf_op jit(solution)/shard_map/ppermute | solution.py:29
  24.8 111.6 %copy-start.13 = (bf16[128,1024]{0,1:T(8,128)(2,1)}, bf16[128,1024]{0,1:T(8,128)(2,1)S(1)}, u32[]{:S(2)}) copy-start(bf16[128,1024]{0,1:T(8,128)(2,1)S(1)} %get-tuple-element.47) | copy-start | bytes 786436
  26.9 110.2 %copy-start.1 = (f32[8,128,128]{1,2,0:T(8,128)}, f32[8,128,128]{1,2,0:T(8,128)S(1)}, u32[]{:S(2)}) copy-start(f32[8,128,128]{1,2,0:T(8,128)S(1)} %get-tuple-element.84) | copy-start | bytes 1572868
  27.2 109.1 %copy-start.3 = (f32[8,128,128]{1,2,0:T(8,128)}, f32[8,128,128]{1,2,0:T(8,128)S(1)}, u32[]{:S(2)}) copy-start(f32[8,128,128]{1,2,0:T(8,128)S(1)} %get-tuple-element.88) | copy-start | bytes 1572868
  130.4 4.4 %copy-start.12 = (bf16[128,1024]{0,1:T(8,128)(2,1)}, bf16[128,1024]{0,1:T(8,128)(2,1)S(1)}, u32[]{:S(2)}) copy-start(bf16[128,1024]{0,1:T(8,128)(2,1)S(1)} %get-tuple-element.59) | copy-start | bytes 786436
  131.1 3.9 %copy-start.23 = (bf16[128,1024]{0,1:T(8,128)(2,1)}, bf16[128,1024]{0,1:T(8,128)(2,1)S(1)}, u32[]{:S(2)}) copy-start(bf16[128,1024]{0,1:T(8,128)(2,1)S(1)} %get-tuple-element.96) | copy-start | bytes 786436
  131.1 4.2 %copy-start.21 = (bf16[128,1024]{0,1:T(8,128)(2,1)}, bf16[128,1024]{0,1:T(8,128)(2,1)S(1)}, u32[]{:S(2)}) copy-start(bf16[128,1024]{0,1:T(8,128)(2,1)S(1)} %get-tuple-element.55) | copy-start | bytes 786436
  132.5 3.4 %copy-start.28 = (bf16[128,1024]{0,1:T(8,128)(2,1)}, bf16[128,1024]{0,1:T(8,128)(2,1)S(1)}, u32[]{:S(2)}) copy-start(bf16[128,1024]{0,1:T(8,128)(2,1)S(1)} %get-tuple-element.98) | copy-start | bytes 786436
  132.5 3.6 %copy-start.26 = (bf16[128,1024]{0,1:T(8,128)(2,1)}, bf16[128,1024]{0,1:T(8,128)(2,1)S(1)}, u32[]{:S(2)}) copy-start(bf16[128,1024]{0,1:T(8,128)(2,1)S(1)} %get-tuple-element.49) | copy-start | bytes 786436
  132.8 3.3 %copy-start.4 = (f32[8,128,128]{1,2,0:T(8,128)}, f32[8,128,128]{1,2,0:T(8,128)S(1)}, u32[]{:S(2)}) copy-start(f32[8,128,128]{1,2,0:T(8,128)S(1)} %get-tuple-element.90) | copy-start | bytes 1572868
  133.1 2.7 %copy-start.5 = (f32[8,128,128]{1,2,0:T(8,128)}, f32[8,128,128]{1,2,0:T(8,128)S(1)}, u32[]{:S(2)}) copy-start(f32[8,128,128]{1,2,0:T(8,128)S(1)} %get-tuple-element.92) | copy-start | bytes 1572868
  137.4 46.5 %collective-permute-start.8 = (f32[1,1,16,128]{3,2,1,0:T(8,128)S(1)}, f32[1,1,16,128]{3,2,1,0:T(8,128)S(1)}, u32[]{:S(2)}, u32[]{:S(2)}) collective-permute-start(f32[1,1,16,128]{3,2,1,0:T(8,128)S(1)} %maximum_bitcast_fusion.2), channel_id=1, source_target_pairs={{32,0},{64,32},{96,64},{128,96},{160,128},{192,160},{224,192},{0,2... | collective-permute-start | bytes 24584 | tf_op jit(solution)/shard_map/ppermute | solution.py:21
  139.0 45.0 %collective-permute-start.7 = (f32[1,1,16,128]{3,2,1,0:T(8,128)S(1)}, f32[1,1,16,128]{3,2,1,0:T(8,128)S(1)}, u32[]{:S(2)}, u32[]{:S(2)}) collective-permute-start(f32[1,1,16,128]{3,2,1,0:T(8,128)S(1)} %maximum_bitcast_fusion.2), channel_id=1, source_target_pairs={{0,32},{32,64},{64,96},{96,128},{128,160},{160,192},{192,224},{224... | collective-permute-start | bytes 24584 | tf_op jit(solution)/shard_map/ppermute | solution.py:18
  150.4 16.1 %copy-start.18 = (bf16[8,128,128]{2,1,0:T(8,128)(2,1)S(1)}, bf16[8,128,128]{2,1,0:T(8,128)(2,1)}, u32[]{:S(2)}) copy-start(bf16[8,128,128]{2,1,0:T(8,128)(2,1)} %fusion.80) | copy-start | bytes 786436
  150.4 16.1 %copy-start.40 = (f32[128,8,128]{0,2,1:T(8,128)S(1)}, f32[128,8,128]{0,2,1:T(8,128)}, u32[]{:S(2)}) copy-start(f32[128,8,128]{0,2,1:T(8,128)} %fusion.58) | copy-start | bytes 1572868
  181.0 4.8 %copy-start.38 = (bf16[128,1024]{0,1:T(8,128)(2,1)S(1)}, bf16[128,1024]{0,1:T(8,128)(2,1)}, u32[]{:S(2)}) copy-start(bf16[128,1024]{0,1:T(8,128)(2,1)} %get-tuple-element.99) | copy-start | bytes 786436
  181.0 5.1 %copy-start.30 = (bf16[128,1024]{0,1:T(8,128)(2,1)S(1)}, bf16[128,1024]{0,1:T(8,128)(2,1)}, u32[]{:S(2)}) copy-start(bf16[128,1024]{0,1:T(8,128)(2,1)} %get-tuple-element.100) | copy-start | bytes 786436
  183.9 7.2 %collective-permute-start.10 = (f32[3,1,16,128]{3,2,1,0:T(8,128)S(1)}, f32[3,1,16,128]{3,2,1,0:T(8,128)S(1)}, u32[]{:S(2)}, u32[]{:S(2)}) collective-permute-start(f32[3,1,16,128]{3,2,1,0:T(8,128)S(1)} %pad_maximum_fusion.2), channel_id=1, source_target_pairs={{1,0},{2,1},{3,2},{4,3},{5,4},{6,5},{7,6},{8,7},{9,8},{10,9},{11,1... | collective-permute-start | bytes 73736 | tf_op jit(solution)/shard_map/ppermute | solution.py:21
  184.6 9.2 %collective-permute-start.9 = (f32[3,1,16,128]{3,2,1,0:T(8,128)S(1)}, f32[3,1,16,128]{3,2,1,0:T(8,128)S(1)}, u32[]{:S(2)}, u32[]{:S(2)}) collective-permute-start(f32[3,1,16,128]{3,2,1,0:T(8,128)S(1)} %pad_maximum_fusion.2), channel_id=1, source_target_pairs={{0,1},{1,2},{2,3},{3,4},{4,5},{5,6},{6,7},{7,8},{8,9},{9,10},{10,1... | collective-permute-start | bytes 73736 | tf_op jit(solution)/shard_map/ppermute | solution.py:18
  195.2 2.9 %copy-start.17 = (bf16[128,1024]{0,1:T(8,128)(2,1)S(1)}, bf16[128,1024]{0,1:T(8,128)(2,1)}, u32[]{:S(2)}) copy-start(bf16[128,1024]{0,1:T(8,128)(2,1)} %get-tuple-element.32) | copy-start | bytes 786436
  206.0 3.3 %copy-start.9 = (bf16[128,1024]{0,1:T(8,128)(2,1)S(1)}, bf16[128,1024]{0,1:T(8,128)(2,1)}, u32[]{:S(2)}) copy-start(bf16[128,1024]{0,1:T(8,128)(2,1)} %get-tuple-element.29) | copy-start | bytes 786436
  (28 other events, 45.6 us)
where the time goes:
time: 217 us
  waiting for transfers between devices  119 us (55%)
  matrix products  54.2 us (25%)
  local copies, waits for them, and re-layouts  18.9 us (9%)
  starting transfers between devices  18.4 us (8%)
  other arithmetic  4.58 us (2%)
    ppermute x4, waiting for transfers between devices, shifted(): return lax.ppermute(value, axis, pairs)  117 us
    dot_general x9, matrix products, on_device(): jnp.einsum('hts,shd->thd', dscore, key_part, preferred_element_type=jnp.f...  19.7 us
    dot_general x9, matrix products, on_device(): jnp.einsum('hts,thd->shd', dscore, query_part, preferred_element_type=jnp...  17.2 us
    ppermute x4, starting transfers between devices, with_halo(): lax.ppermute(lax.slice_in_dim(block, 0, width, axis=dim), axis, backward)  11.7 us
    unnamed x104, local copies, waits for them, and re-layouts  8.73 us
    dot_general x17, matrix products, score_tile(): jnp.einsum('thd,shd->hts', query_part, key_part, preferred_element_type=j...  7.15 us
    dot_general x9, matrix products, on_device(): jnp.einsum('hts,thd->shd', prob_half, grad_part, preferred_element_type=j...  6.51 us
    slice x6, local copies, waits for them, and re-layouts, on_device(): grad_part = head_split(query_block[:, channels:], tok_rows)  5.81 us
  transfers between devices with their start and end apart: 12, of which 5 were waited for; matrix products, arithmetic and copies ran while one was open for 23% of the time, Pallas kernels for 0%

commit v1 on v0

v1 whole, which is shorter than its diff:
```python
import math

import jax
import jax.numpy as jnp
import numpy as np
from jax import lax
from jax.experimental import pallas as pl
from jax.experimental.pallas import tpu as pltpu
from jax.sharding import PartitionSpec as P

HD = 128
BLK = 128
WIDE = 2 * HD
AXES = ("x", "l", "h", "z", "c")
SIZES = (4, 2, 2, 8, 2)
SCALE = 1.0 / math.sqrt(HD)
EXP_SCALE = SCALE * math.log2(math.e)
BF = jnp.bfloat16
F32 = jnp.float32


def make_perm(target):
    pairs = []
    for index in range(math.prod(SIZES)):
        place = [int(v) for v in np.unravel_index(index, SIZES)]
        pairs.append((index, int(np.ravel_multi_index(target(*place), SIZES))))
    return pairs


def ring_z(x, l, h, z, c, step):
    near = z + step
    if 0 <= near < 8:
        return (x, l, h, near, c)
    return (x, 1 - l, 1 - h, near % 8, c)


def up(bit):
    return 2 * bit - 1


CORE = make_perm(lambda x, l, h, z, c: (x, l, h, z, 1 - c))
PAIR = make_perm(lambda x, l, h, z, c: (x, 1 - l, h, z, c))
X_OWN = make_perm(lambda x, l, h, z, c: ((x + up(l)) % 4, l, h, z, c))
X_FAR = make_perm(lambda x, l, h, z, c: ((x - up(l)) % 4, l, h, z, c))
Z_OWN = make_perm(lambda x, l, h, z, c: ring_z(x, l, h, z, c, up(c)))
Z_FAR = make_perm(lambda x, l, h, z, c: ring_z(x, l, h, z, c, -up(c)))


def move(value, perm):
    return lax.ppermute(value, AXES, perm)


KEYS = [(r, s) for r in range(4) for s in range(4)]


def query_runs(r, s):
    rows = [i for i in (1, 2) if abs(i - r) <= 1]
    cols = [j for j in (1, 2) if abs(j - s) <= 1]
    if len(cols) == 2:
        first = (rows[0] - 1) * 2
        return [(first, 2 * len(rows))]
    return [((i - 1) * 2 + cols[0] - 1, 1) for i in rows]


def dot_nt(a, b):
    return lax.dot_general(a, b, (((1,), (1,)), ((), ())), preferred_element_type=F32)


def dot_nn(a, b):
    return lax.dot_general(a, b, (((1,), (0,)), ((), ())), preferred_element_type=F32)


def fold(tile):
    return tile.reshape(BLK // 8, 8, BLK)


def attention_kernel(
    flip, qg1, qg2, kv1, kv2, kv3, kv0, za12, zb12, za30, zb30,
    dq1, dq2, p1, p2, p3, p0, pa12, pb12, pa30, pb30,
    qh, gh, kt, s_s, d_s, p_s, ds_s,
):
    fa = flip[0]
    fb = flip[1]

    def place(r, s, tile_refs, a12, b12, a30, b30):
        if s in (1, 2):
            return tile_refs[r], s - 1
        near, bit = (a12, fa) if s == 3 else (b12, fb)
        far = a30 if s == 3 else b30
        if r in (1, 2):
            return near, bit if r == 1 else 1 - bit
        return far, bit if r == 3 else 1 - bit

    def key_place(r, s):
        return place(r, s, (kv0, kv1, kv2, kv3), za12, zb12, za30, zb30)

    def grad_place(r, s):
        return place(r, s, (p0, p1, p2, p3), pa12, pb12, pa30, pb30)

    for head in range(2):
        lanes = slice(head * HD, (head + 1) * HD)
        for i, (ref, j) in enumerate(((qg1, 0), (qg1, 1), (qg2, 0), (qg2, 1))):
            rows = slice(i * BLK, (i + 1) * BLK)
            qh[rows, :] = ref[j, 0, :, lanes]
            gh[rows, :] = ref[j, 1, :, lanes]
        peak = [None] * 4
        for u, (r, s) in enumerate(KEYS):
            ref, index = key_place(r, s)
            key = ref[index, 0, :, lanes]
            value = ref[index, 1, :, lanes]
            kt[:, u * BLK : (u + 1) * BLK] = key.T
            urows = slice(u * BLK, (u + 1) * BLK)
            for first, count in query_runs(r, s):
                part = slice(first * BLK, (first + count) * BLK)
                scores = dot_nt(key, qh[part, :])
                s_s[urows, part] = scores
                d_s[urows, part] = dot_nt(value, gh[part, :])
                for k in range(count):
                    top = jnp.max(fold(scores[:, k * BLK : (k + 1) * BLK]), axis=0)
                    q = first + k
                    peak[q] = top if peak[q] is None else jnp.maximum(peak[q], top)
        for q in range(4):
            qr, qs = q // 2 + 1, q % 2 + 1
            part = slice(q * BLK, (q + 1) * BLK)
            window = [r * 4 + s for r in range(qr - 1, qr + 2) for s in range(qs - 1, qs + 2)]
            top = jnp.max(peak[q], axis=0, keepdims=True) * EXP_SCALE
            total8 = jnp.zeros((8, BLK), F32)
            delta8 = jnp.zeros((8, BLK), F32)
            for u in window:
                urows = slice(u * BLK, (u + 1) * BLK)
                e = jnp.exp2(s_s[urows, part] * EXP_SCALE - top)
                s_s[urows, part] = e
                total8 = total8 + jnp.sum(fold(e), axis=0)
                delta8 = delta8 + jnp.sum(fold(e * d_s[urows, part]), axis=0)
            inverse = 1.0 / jnp.sum(total8, axis=0, keepdims=True)
            delta = jnp.sum(delta8, axis=0, keepdims=True) * inverse
            for u in window:
                urows = slice(u * BLK, (u + 1) * BLK)
                prob = s_s[urows, part] * inverse
                p_s[urows, part] = prob.astype(BF)
                ds_s[urows, part] = (prob * (d_s[urows, part] - delta)).astype(BF)
        for u, (r, s) in enumerate(KEYS):
            urows = slice(u * BLK, (u + 1) * BLK)
            dkey = None
            for first, count in query_runs(r, s):
                part = slice(first * BLK, (first + count) * BLK)
                one = dot_nn(ds_s[urows, part], qh[part, :])
                two = dot_nn(p_s[urows, part], gh[part, :])
                dkey, dvalue = (one, two) if dkey is None else (dkey + one, dvalue + two)
            ref, index = grad_place(r, s)
            ref[index, 0, :, lanes] = (dkey * SCALE).astype(ref.dtype)
            ref[index, 1, :, lanes] = dvalue.astype(ref.dtype)
        for q in range(4):
            qr, qs = q // 2 + 1, q % 2 + 1
            part = slice(q * BLK, (q + 1) * BLK)
            acc = None
            for r in range(qr - 1, qr + 2):
                u = r * 4 + qs - 1
                long = slice(u * BLK, (u + 3) * BLK)
                one = dot_nn(kt[:, long], ds_s[long, part])
                acc = one if acc is None else acc + one
            out = dq1 if qr == 1 else dq2
            out[qs - 1, :, lanes] = (acc * SCALE).T.astype(BF)


def attention(flip, *arrays):
    vmem = pl.BlockSpec(memory_space=pltpu.VMEM)
    smem = pl.BlockSpec(memory_space=pltpu.SMEM)
    dq = jax.ShapeDtypeStruct((2, BLK, WIDE), BF)
    wide = jax.ShapeDtypeStruct((2, 2, BLK, WIDE), F32)
    half = jax.ShapeDtypeStruct((2, 2, BLK, WIDE), BF)
    return pl.pallas_call(
        attention_kernel,
        out_shape=[dq] * 2 + [wide] * 4 + [half] * 4,
        in_specs=[smem] + [vmem] * 10,
        out_specs=[vmem] * 10,
        scratch_shapes=[
            pltpu.VMEM((4 * BLK, HD), BF),
            pltpu.VMEM((4 * BLK, HD), BF),
            pltpu.VMEM((HD, 16 * BLK), BF),
            pltpu.VMEM((16 * BLK, 4 * BLK), F32),
            pltpu.VMEM((16 * BLK, 4 * BLK), F32),
            pltpu.VMEM((16 * BLK, 4 * BLK), BF),
            pltpu.VMEM((16 * BLK, 4 * BLK), BF),
        ],
        compiler_params=pltpu.CompilerParams(vmem_limit_bytes=48 * 1024 * 1024),
        cost_estimate=pl.CostEstimate(
            flops=1_500_000_000, bytes_accessed=8 * 1024 * 1024, transcendentals=1_200_000
        ),
    )(flip, *arrays)


def on_device(queries, key_states, value_states, out_grad):
    l = lax.axis_index("l")
    h = lax.axis_index("h")
    z = lax.axis_index("z")
    c = lax.axis_index("c")
    group = l ^ h
    low_end = z == 0
    high_end = z == 7
    flip = jnp.stack(
        [
            jnp.where(c == 1, low_end, high_end).astype(jnp.int32),
            jnp.where(c == 1, high_end, low_end).astype(jnp.int32),
        ]
    )

    def lanes(array, start, width):
        return lax.dynamic_slice_in_dim(array, start, width, axis=array.ndim - 1)

    def to_tile(first, second):
        both = (first[0], second[0])
        away = jnp.stack([lanes(a, (1 - c) * 512, 512) for a in both])
        came = move(away, CORE)
        other = jnp.stack(
            [
                jnp.stack([lanes(a, c * 512 + (1 - group) * WIDE, WIDE) for a in both]),
                lanes(came, (1 - group) * WIDE, WIDE),
            ]
        )
        mine = jnp.stack(
            [
                jnp.stack([lanes(a, c * 512 + group * WIDE, WIDE) for a in both]),
                lanes(came, group * WIDE, WIDE),
            ]
        )
        return mine, other

    kv1, kv_other = to_tile(key_states, value_states)
    kv2 = move(kv_other, PAIR)
    kv3 = move(kv1, X_OWN)
    qg1, qg_other = to_tile(queries, out_grad)
    qg2 = move(qg_other, PAIR)
    kv0 = move(kv2, X_FAR)
    za12 = move(jnp.stack([kv1[0], kv2[0]]), Z_OWN)
    zb12 = move(jnp.stack([kv1[1], kv2[1]]), Z_FAR)
    za30 = move(jnp.stack([kv3[0], kv0[0]]), Z_OWN)
    zb30 = move(jnp.stack([kv3[1], kv0[1]]), Z_FAR)

    dq1, dq2, p1, p2, p3, p0, pa12, pb12, pa30, pb30 = attention(
        flip, qg1, qg2, kv1, kv2, kv3, kv0, za12, zb12, za30, zb30
    )

    ra30 = move(pa30, Z_FAR)
    rb30 = move(pb30, Z_OWN)
    ra12 = move(pa12, Z_FAR)
    rb12 = move(pb12, Z_OWN)
    dq_pair = move(dq2, PAIR)

    def with_sides(part, near, far, row):
        return part + jnp.stack([near[row], far[row]]).astype(F32)

    r0 = move(with_sides(p0, ra30, rb30, 1).astype(BF), X_OWN)
    r3 = move(with_sides(p3, ra30, rb30, 0).astype(BF), X_FAR)
    row2 = (with_sides(p2, ra12, rb12, 1) + r0.astype(F32)).astype(BF)
    row1 = (with_sides(p1, ra12, rb12, 0) + r3.astype(F32)).astype(BF)
    row_pair = move(row2, PAIR)

    own = jnp.concatenate([dq1[:, None], row1], axis=1)
    pair = jnp.concatenate([dq_pair[:, None], row_pair], axis=1)
    quad = jnp.where(
        group == 0,
        jnp.concatenate([own, pair], axis=-1),
        jnp.concatenate([pair, own], axis=-1),
    )
    came = move(quad[1], CORE)
    kept = quad[0]
    full = jnp.where(
        c == 0,
        jnp.concatenate([kept, came], axis=-1),
        jnp.concatenate([came, kept], axis=-1),
    )
    return full[0][None], full[1][None], full[2][None]


def solution(mesh):
    fine = jax.sharding.Mesh(mesh.devices.reshape(SIZES), AXES)
    placed = P(("x", "l"), ("h", "z", "c"), None)
    return jax.shard_map(
        on_device,
        mesh=fine,
        in_specs=(placed,) * 4,
        out_specs=(placed,) * 3,
        check_vma=False,
    )
```

time: 217 us -> 78.6 us (0.36)
  waiting for transfers between devices: 119 us -> 28 us
  matrix products: 54.2 us -> 0 us
  starting transfers between devices: 18.4 us -> 39.1 us
  local copies, waits for them, and re-layouts: 18.9 us -> 2.29 us
  Pallas kernels: 0 us -> 7.04 us
  other arithmetic: 4.58 us -> 1.09 us
    ppermute x12 -> x19, waiting for transfers between devices: 119 us -> 28 us  [move(): return lax.ppermute(value, AXES, perm)]
    dot_general x54 -> x0, matrix products: 54.2 us -> none  [the longest x9 19.7 us: on_device(): jnp.einsum('hts,shd->thd', dscore, key_part, preferred_element_type=jnp.f...]
    ppermute x12 -> x19, starting transfers between devices: 18.4 us -> 39.1 us  [move(): return lax.ppermute(value, AXES, perm)]
    unnamed x104 -> x8, local copies, waits for them, and re-layouts: 8.73 us -> 0.02 us
    pallas_call x0 -> x1, Pallas kernels: none -> 7.04 us  [attention(): pl.pallas_call(attention_kernel, out_shape=[dq] * 2 + [wide] * 4 + [half]...]
    slice x12 -> x8, local copies, waits for them, and re-layouts: 6.09 us -> 1.02 us  [the longest x1 0.89 us: on_device(): return (full[0][None], full[1][None], full[2][None])]
    squeeze x4 -> x1, local copies, waits for them, and re-layouts: 3.91 us -> 0.05 us  [on_device(): kept = quad[0]]
    concatenate x3 -> x0, other arithmetic: 2.57 us -> none  [with_halo(): block = jnp.concatenate([low, block, high], axis=dim)]
  transfers between devices with their start and end apart: 12 -> 19, of which waited for: 5 -> 9; matrix products, arithmetic and copies ran while one was open for 23% -> 1% of each run, Pallas kernels for 0% -> 0%
where the time goes in v1:
time: 78.6 us; the launch traced here: 78.5 us
  starting transfers between devices  39.1 us (50%)
  waiting for transfers between devices  28 us (36%)
  Pallas kernels  7.04 us (9%)
  local copies, waits for them, and re-layouts  2.29 us (3%)
  other arithmetic  1.09 us (1%)
  between operations  0.96 us (1%)
    ppermute x19, starting transfers between devices, move(): return lax.ppermute(value, AXES, perm)  39.1 us
    ppermute x19, waiting for transfers between devices, move(): return lax.ppermute(value, AXES, perm)  28 us
    pallas_call x1, Pallas kernels, attention(): pl.pallas_call(attention_kernel, out_shape=[dq] * 2 + [wide] * 4 + [half]...  7.04 us
  transfers between devices with their start and end apart: 19, of which 9 were waited for; matrix products, arithmetic and copies ran while one was open for 1% of the time, Pallas kernels for 0%

profile of v1, /device:TPU:1, one launch (start us, length us, event | category | flops | bytes accessed | tf_op | source)
XLA Modules:
  0.0 78.5 jit_solution(3294908684149435319)
XLA Ops:
  0.7 1.0 %constant_dynamic-slice_fusion.2 = (bf16[1,128,512]{2,1,0:T(8,128)(2,1)S(1)}, bf16[1,128,512]{2,1,0:T(8,128)(2,1)S(1)}) fusion(bf16[1,128,1024]{2,1,0:T(8,128)(2,1)} %param.6, s32[]{:T(128)S(6)} %select_n.54, bf16[1,128,1024]{2,1,0:T(8,128)(2,1)} %param.5), kind=kLoop, calls=%fused_computation.28 | loop fusion | bytes 524292 | tf_op jit(solution)/shard_map/dynamic_slice | solution.py:209
  1.8 3.3 %collective-permute-start.2 = (bf16[2,128,512]{2,1,0:T(8,128)(2,1)S(1)}, bf16[2,128,512]{2,1,0:T(8,128)(2,1)S(1)}, u32[]{:S(2)}, u32[]{:S(2)}) collective-permute-start(bf16[2,128,512]{2,1,0:T(8,128)(2,1)S(1)} %pad_maximum_fusion.5), channel_id=1, source_target_pairs={{0,1},{1,0},{2,3},{3,2},{4,5},{5,4},{6,7},{7,6},{8,9},{9,8},{10,11... | collective-permute-start | bytes 786440 | tf_op jit(solution)/shard_map/ppermute | solution.py:50
  5.2 1.0 %collective-permute-done.2 = bf16[2,128,512]{2,1,0:T(8,128)(2,1)S(1)} collective-permute-done((bf16[2,128,512]{2,1,0:T(8,128)(2,1)S(1)}, bf16[2,128,512]{2,1,0:T(8,128)(2,1)S(1)}, u32[]{:S(2)}, u32[]{:S(2)}) %collective-permute-start.2) | collective-permute-done | bytes 262176 | tf_op jit(solution)/shard_map/ppermute | solution.py:50
  6.3 0.1 collective-permute-start.3
  6.4 0.5 collective-permute-start
  7.0 6.9 %collective-permute-done.3.kv2 = bf16[2,2,128,256]{3,2,1,0:T(8,128)(2,1)S(1)} collective-permute-done((bf16[2,2,128,256]{3,2,1,0:T(8,128)(2,1)S(1)}, bf16[2,2,128,256]{3,2,1,0:T(8,128)(2,1)S(1)}, u32[]{:S(2)}, u32[]{:S(2)}) %collective-permute-start.3) | collective-permute-done | bytes 262176 | tf_op jit(solution)/shard_map/ppermute | solution.py:50
  14.0 0.8 %collective-permute-start.4 = (bf16[2,2,128,256]{3,2,1,0:T(8,128)(2,1)S(1)}, bf16[2,2,128,256]{3,2,1,0:T(8,128)(2,1)S(1)}, u32[]{:S(2)}, u32[]{:S(2)}) collective-permute-start(bf16[2,2,128,256]{3,2,1,0:T(8,128)(2,1)S(1)} %get-tuple-element.55.kv1), channel_id=1, source_target_pairs={{0,192},{1,193},{2,194},{3,195},{4,196},{5,197},{6,198},{7,199},{8... | collective-permute-start | bytes 786440 | tf_op jit(solution)/shard_map/ppermute | solution.py:50
  14.9 0.8 %collective-permute-start.5 = (bf16[2,2,128,256]{3,2,1,0:T(8,128)(2,1)S(1)}, bf16[2,2,128,256]{3,2,1,0:T(8,128)(2,1)S(1)}, u32[]{:S(2)}, u32[]{:S(2)}) collective-permute-start(bf16[2,2,128,256]{3,2,1,0:T(8,128)(2,1)S(1)} %collective-permute-done.3.kv2), channel_id=1, source_target_pairs={{0,64},{1,65},{2,66},{3,67},{4,68},{5,69},{6,70},{7,71},{8,72},{9,... | collective-permute-start | bytes 786440 | tf_op jit(solution)/shard_map/ppermute | solution.py:50
  15.7 1.6 %collective-permute-start.1 = (bf16[2,2,128,256]{3,2,1,0:T(8,128)(2,1)S(1)}, bf16[2,2,128,256]{3,2,1,0:T(8,128)(2,1)S(1)}, u32[]{:S(2)}, u32[]{:S(2)}) collective-permute-start(bf16[2,2,128,256]{3,2,1,0:T(8,128)(2,1)S(1)} %pad_maximum_fusion.4), channel_id=1, source_target_pairs={{0,32},{1,33},{2,34},{3,35},{4,36},{5,37},{6,38},{7,39},{8,40},{9,... | collective-permute-start | bytes 786440 | tf_op jit(solution)/shard_map/ppermute | solution.py:50
  17.4 6.2 %collective-permute-start.7 = (bf16[2,2,128,256]{3,2,1,0:T(8,128)(2,1)S(1)}, bf16[2,2,128,256]{3,2,1,0:T(8,128)(2,1)S(1)}, u32[]{:S(2)}, u32[]{:S(2)}) collective-permute-start(bf16[2,2,128,256]{3,2,1,0:T(8,128)(2,1)S(1)} %get-tuple-element.54), channel_id=1, source_target_pairs={{0,2},{1,63},{2,4},{3,1},{4,6},{5,3},{6,8},{7,5},{8,10},{9,7},{10,... | collective-permute-start | bytes 786440 | tf_op jit(solution)/shard_map/ppermute | solution.py:50
  23.7 0.6 collective-permute-start.8
  24.3 4.6 %collective-permute-start.9 = (bf16[2,2,128,256]{3,2,1,0:T(8,128)(2,1)S(1)}, bf16[2,2,128,256]{3,2,1,0:T(8,128)(2,1)S(1)}, u32[]{:S(2)}, u32[]{:S(2)}) collective-permute-start(bf16[2,2,128,256]{3,2,1,0:T(8,128)(2,1)S(1)} %pad_maximum_fusion.9), channel_id=1, source_target_pairs={{0,2},{1,63},{2,4},{3,1},{4,6},{5,3},{6,8},{7,5},{8,10},{9,7},{10,... | collective-permute-start | bytes 786440 | tf_op jit(solution)/shard_map/ppermute | solution.py:50
  29.0 3.1 %collective-permute-done.6.za12 = bf16[2,2,128,256]{3,2,1,0:T(8,128)(2,1)S(1)} collective-permute-done((bf16[2,2,128,256]{3,2,1,0:T(8,128)(2,1)S(1)}, bf16[2,2,128,256]{3,2,1,0:T(8,128)(2,1)S(1)}, u32[]{:S(2)}, u32[]{:S(2)}) %collective-permute-start.6) | collective-permute-done | bytes 262176 | tf_op jit(solution)/shard_map/ppermute | solution.py:50
  32.1 2.8 %collective-permute-done.8.za30 = bf16[2,2,128,256]{3,2,1,0:T(8,128)(2,1)S(1)} collective-permute-done((bf16[2,2,128,256]{3,2,1,0:T(8,128)(2,1)S(1)}, bf16[2,2,128,256]{3,2,1,0:T(8,128)(2,1)S(1)}, u32[]{:S(2)}, u32[]{:S(2)}) %collective-permute-start.8) | collective-permute-done | bytes 262176 | tf_op jit(solution)/shard_map/ppermute | solution.py:50
  35.0 7.0 %shard_map.67 = (bf16[2,128,256]{2,1,0:T(8,128)(2,1)S(1)}, bf16[2,128,256]{2,1,0:T(8,128)(2,1)S(1)}, f32[2,2,128,256]{3,2,1,0:T(8,128)S(1)}, f32[2,2,128,256]{3,...) custom-call(s32[2]{0:T(128)S(1)} %add_convert_fusion.4.flip, ...), custom_call_target="tpu_custom_call" | custom-call | flops 1500000000 | bytes 8388608 | tf_op jit(solution)/shard_map/pallas_call | solution.py:172
  42.0 4.1 %collective-permute-start.12 = (bf16[2,2,128,256]{3,2,1,0:T(8,128)(2,1)S(1)}, bf16[2,2,128,256]{3,2,1,0:T(8,128)(2,1)S(1)}, u32[]{:S(2)}, u32[]{:S(2)}) collective-permute-start(bf16[2,2,128,256]{3,2,1,0:T(8,128)(2,1)S(1)} %get-tuple-element.18), channel_id=1, source_target_pairs={{0,2},{1,63},{2,4},{3,1},{4,6},{5,3},{6,8},{7,5},{8,10},{9,7},{10,... | collective-permute-start | bytes 786440 | tf_op jit(solution)/shard_map/ppermute | solution.py:50
  46.1 4.8 %collective-permute-start.10 = (bf16[2,2,128,256]{3,2,1,0:T(8,128)(2,1)S(1)}, bf16[2,2,128,256]{3,2,1,0:T(8,128)(2,1)S(1)}, u32[]{:S(2)}, u32[]{:S(2)}) collective-permute-start(bf16[2,2,128,256]{3,2,1,0:T(8,128)(2,1)S(1)} %get-tuple-element.15), channel_id=1, source_target_pairs={{0,2},{1,63},{2,4},{3,1},{4,6},{5,3},{6,8},{7,5},{8,10},{9,7},{10,... | collective-permute-start | bytes 786440 | tf_op jit(solution)/shard_map/ppermute | solution.py:50
  50.9 4.4 %collective-permute-done.13 = bf16[2,2,128,256]{3,2,1,0:T(8,128)(2,1)S(1)} collective-permute-done((bf16[2,2,128,256]{3,2,1,0:T(8,128)(2,1)S(1)}, bf16[2,2,128,256]{3,2,1,0:T(8,128)(2,1)S(1)}, u32[]{:S(2)}, u32[]{:S(2)}) %collective-permute-start.13) | collective-permute-done | bytes 262176 | tf_op jit(solution)/shard_map/ppermute | solution.py:50
  55.4 0.1 collective-permute-start.14
  55.6 2.7 %collective-permute-start.16 = (bf16[2,2,128,256]{3,2,1,0:T(8,128)(2,1)S(1)}, bf16[2,2,128,256]{3,2,1,0:T(8,128)(2,1)S(1)}, u32[]{:S(2)}, u32[]{:S(2)}) collective-permute-start(bf16[2,2,128,256]{3,2,1,0:T(8,128)(2,1)S(1)} %add_convert_fusion.1), channel_id=1, source_target_pairs={{0,192},{1,193},{2,194},{3,195},{4,196},{5,197},{6,198},{7,199},{8... | collective-permute-start | bytes 786440 | tf_op jit(solution)/shard_map/ppermute | solution.py:50
  58.3 2.9 %collective-permute-done.11 = bf16[2,2,128,256]{3,2,1,0:T(8,128)(2,1)S(1)} collective-permute-done((bf16[2,2,128,256]{3,2,1,0:T(8,128)(2,1)S(1)}, bf16[2,2,128,256]{3,2,1,0:T(8,128)(2,1)S(1)}, u32[]{:S(2)}, u32[]{:S(2)}) %collective-permute-start.11) | collective-permute-done | bytes 262176 | tf_op jit(solution)/shard_map/ppermute | solution.py:50
  61.2 0.4 collective-permute-done.16
  61.6 0.1 add_convert_fusion
  61.7 0.3 collective-permute-start.17
  62.0 1.2 %collective-permute-start.15 = (bf16[2,128,256]{2,1,0:T(8,128)(2,1)S(1)}, bf16[2,128,256]{2,1,0:T(8,128)(2,1)S(1)}, u32[]{:S(2)}, u32[]{:S(2)}) collective-permute-start(bf16[2,128,256]{2,1,0:T(8,128)(2,1)S(1)} %get-tuple-element.20), channel_id=1, source_target_pairs={{0,32},{1,33},{2,34},{3,35},{4,36},{5,37},{6,38},{7,39},{8,40},{9,... | collective-permute-start | bytes 393224 | tf_op jit(solution)/shard_map/ppermute | solution.py:50
  63.3 0.1 add_convert_fusion.2
  63.4 5.1 %collective-permute-done.15 = bf16[2,128,256]{2,1,0:T(8,128)(2,1)S(1)} collective-permute-done((bf16[2,128,256]{2,1,0:T(8,128)(2,1)S(1)}, bf16[2,128,256]{2,1,0:T(8,128)(2,1)S(1)}, u32[]{:S(2)}, u32[]{:S(2)}) %collective-permute-start.15) | collective-permute-done | bytes 131104 | tf_op jit(solution)/shard_map/ppermute | solution.py:50
  68.5 0.2 maximum_select_fusion
  68.7 7.3 %collective-permute-start.18 = (bf16[3,128,512]{2,1,0:T(8,128)(2,1)S(1)}, bf16[3,128,512]{2,1,0:T(8,128)(2,1)S(1)}, u32[]{:S(2)}, u32[]{:S(2)}) collective-permute-start(bf16[3,128,512]{2,1,0:T(8,128)(2,1)S(1)} %get-tuple-element.27), channel_id=1, source_target_pairs={{0,1},{1,0},{2,3},{3,2},{4,5},{5,4},{6,7},{7,6},{8,9},{9,8},{10,11... | collective-permute-start | bytes 1179656 | tf_op jit(solution)/shard_map/ppermute | solution.py:50
  76.0 1.3 %collective-permute-done.18 = bf16[3,128,512]{2,1,0:T(8,128)(2,1)S(1)} collective-permute-done((bf16[3,128,512]{2,1,0:T(8,128)(2,1)S(1)}, bf16[3,128,512]{2,1,0:T(8,128)(2,1)S(1)}, u32[]{:S(2)}, u32[]{:S(2)}) %collective-permute-start.18) | collective-permute-done | bytes 393248 | tf_op jit(solution)/shard_map/ppermute | solution.py:50
  77.4 0.2 maximum_select_fusion.1
  77.6 0.9 %fusion = (bf16[1,128,1024]{2,1,0:T(8,128)(2,1)}, bf16[1,128,1024]{2,1,0:T(8,128)(2,1)}, bf16[1,128,1024]{2,1,0:T(8,128)(2,1)}) fusion(bf16[3,128,1024]{2,1,0:T(8,128)(2,1)S(1)} %maximum_select_fusion.1), kind=kLoop, calls=%fused_computation.39 | loop fusion | bytes 1572864 | tf_op jit(solution)/shard_map/slice | solution.py:273
  (49 shorter events, 0.9 us)
Async XLA Ops:
  0.6 4.5 %copy-start = (bf16[1,128,1024]{2,1,0:T(8,128)(2,1)S(1)}, bf16[1,128,1024]{2,1,0:T(8,128)(2,1)}, u32[]{:S(2)}) copy-start(bf16[1,128,1024]{2,1,0:T(8,128)(2,1)} %param.6) | copy-start | bytes 786436
  0.6 4.5 %copy-start.1 = (bf16[1,128,1024]{2,1,0:T(8,128)(2,1)S(1)}, bf16[1,128,1024]{2,1,0:T(8,128)(2,1)}, u32[]{:S(2)}) copy-start(bf16[1,128,1024]{2,1,0:T(8,128)(2,1)} %param.5) | copy-start | bytes 786436
  1.7 3.5 %copy-start.2 = (bf16[1,128,1024]{2,1,0:T(8,128)(2,1)S(1)}, bf16[1,128,1024]{2,1,0:T(8,128)(2,1)}, u32[]{:S(2)}) copy-start(bf16[1,128,1024]{2,1,0:T(8,128)(2,1)} %param.7) | copy-start | bytes 786436
  1.7 3.5 %copy-start.3 = (bf16[1,128,1024]{2,1,0:T(8,128)(2,1)S(1)}, bf16[1,128,1024]{2,1,0:T(8,128)(2,1)}, u32[]{:S(2)}) copy-start(bf16[1,128,1024]{2,1,0:T(8,128)(2,1)} %param.4) | copy-start | bytes 786436
  1.8 4.5 %collective-permute-start.2 = (bf16[2,128,512]{2,1,0:T(8,128)(2,1)S(1)}, bf16[2,128,512]{2,1,0:T(8,128)(2,1)S(1)}, u32[]{:S(2)}, u32[]{:S(2)}) collective-permute-start(bf16[2,128,512]{2,1,0:T(8,128)(2,1)S(1)} %pad_maximum_fusion.5), channel_id=1, source_target_pairs={{0,1},{1,0},{2,3},{3,2},{4,5},{5,4},{6,7},{7,6},{8,9},{9,8},{10,11... | collective-permute-start | bytes 786440 | tf_op jit(solution)/shard_map/ppermute | solution.py:50
  6.3 7.6 %collective-permute-start.3 = (bf16[2,2,128,256]{3,2,1,0:T(8,128)(2,1)S(1)}, bf16[2,2,128,256]{3,2,1,0:T(8,128)(2,1)S(1)}, u32[]{:S(2)}, u32[]{:S(2)}) collective-permute-start(bf16[2,2,128,256]{3,2,1,0:T(8,128)(2,1)S(1)} %pad_maximum_fusion.6), channel_id=1, source_target_pairs={{0,32},{1,33},{2,34},{3,35},{4,36},{5,37},{6,38},{7,39},{8,40},{9,... | collective-permute-start | bytes 786440 | tf_op jit(solution)/shard_map/ppermute | solution.py:50
  6.4 8.4 %collective-permute-start = (bf16[2,128,512]{2,1,0:T(8,128)(2,1)S(1)}, bf16[2,128,512]{2,1,0:T(8,128)(2,1)S(1)}, u32[]{:S(2)}, u32[]{:S(2)}) collective-permute-start(bf16[2,128,512]{2,1,0:T(8,128)(2,1)S(1)} %pad_maximum_fusion.2), channel_id=1, source_target_pairs={{0,1},{1,0},{2,3},{3,2},{4,5},{5,4},{6,7},{7,6},{8,9},{9,8},{10,11... | collective-permute-start | bytes 786440 | tf_op jit(solution)/shard_map/ppermute | solution.py:50
  14.0 9.6 %collective-permute-start.4 = (bf16[2,2,128,256]{3,2,1,0:T(8,128)(2,1)S(1)}, bf16[2,2,128,256]{3,2,1,0:T(8,128)(2,1)S(1)}, u32[]{:S(2)}, u32[]{:S(2)}) collective-permute-start(bf16[2,2,128,256]{3,2,1,0:T(8,128)(2,1)S(1)} %get-tuple-element.55.kv1), channel_id=1, source_target_pairs={{0,192},{1,193},{2,194},{3,195},{4,196},{5,197},{6,198},{7,199},{8... | collective-permute-start | bytes 786440 | tf_op jit(solution)/shard_map/ppermute | solution.py:50
  14.9 8.7 %collective-permute-start.5 = (bf16[2,2,128,256]{3,2,1,0:T(8,128)(2,1)S(1)}, bf16[2,2,128,256]{3,2,1,0:T(8,128)(2,1)S(1)}, u32[]{:S(2)}, u32[]{:S(2)}) collective-permute-start(bf16[2,2,128,256]{3,2,1,0:T(8,128)(2,1)S(1)} %collective-permute-done.3.kv2), channel_id=1, source_target_pairs={{0,64},{1,65},{2,66},{3,67},{4,68},{5,69},{6,70},{7,71},{8,72},{9,... | collective-permute-start | bytes 786440 | tf_op jit(solution)/shard_map/ppermute | solution.py:50
  15.7 13.3 %collective-permute-start.1 = (bf16[2,2,128,256]{3,2,1,0:T(8,128)(2,1)S(1)}, bf16[2,2,128,256]{3,2,1,0:T(8,128)(2,1)S(1)}, u32[]{:S(2)}, u32[]{:S(2)}) collective-permute-start(bf16[2,2,128,256]{3,2,1,0:T(8,128)(2,1)S(1)} %pad_maximum_fusion.4), channel_id=1, source_target_pairs={{0,32},{1,33},{2,34},{3,35},{4,36},{5,37},{6,38},{7,39},{8,40},{9,... | collective-permute-start | bytes 786440 | tf_op jit(solution)/shard_map/ppermute | solution.py:50
  17.4 11.7 %collective-permute-start.7 = (bf16[2,2,128,256]{3,2,1,0:T(8,128)(2,1)S(1)}, bf16[2,2,128,256]{3,2,1,0:T(8,128)(2,1)S(1)}, u32[]{:S(2)}, u32[]{:S(2)}) collective-permute-start(bf16[2,2,128,256]{3,2,1,0:T(8,128)(2,1)S(1)} %get-tuple-element.54), channel_id=1, source_target_pairs={{0,2},{1,63},{2,4},{3,1},{4,6},{5,3},{6,8},{7,5},{8,10},{9,7},{10,... | collective-permute-start | bytes 786440 | tf_op jit(solution)/shard_map/ppermute | solution.py:50
  23.6 8.5 %collective-permute-start.6 = (bf16[2,2,128,256]{3,2,1,0:T(8,128)(2,1)S(1)}, bf16[2,2,128,256]{3,2,1,0:T(8,128)(2,1)S(1)}, u32[]{:S(2)}, u32[]{:S(2)}) collective-permute-start(bf16[2,2,128,256]{3,2,1,0:T(8,128)(2,1)S(1)} %get-tuple-element.56), channel_id=1, source_target_pairs={{0,62},{1,3},{2,0},{3,5},{4,2},{5,7},{6,4},{7,9},{8,6},{9,11},{10,... | collective-permute-start | bytes 786440 | tf_op jit(solution)/shard_map/ppermute | solution.py:50
  23.7 11.2 %collective-permute-start.8 = (bf16[2,2,128,256]{3,2,1,0:T(8,128)(2,1)S(1)}, bf16[2,2,128,256]{3,2,1,0:T(8,128)(2,1)S(1)}, u32[]{:S(2)}, u32[]{:S(2)}) collective-permute-start(bf16[2,2,128,256]{3,2,1,0:T(8,128)(2,1)S(1)} %pad_maximum_fusion.8), channel_id=1, source_target_pairs={{0,62},{1,3},{2,0},{3,5},{4,2},{5,7},{6,4},{7,9},{8,6},{9,11},{10,... | collective-permute-start | bytes 786440 | tf_op jit(solution)/shard_map/ppermute | solution.py:50
  24.3 10.6 %collective-permute-start.9 = (bf16[2,2,128,256]{3,2,1,0:T(8,128)(2,1)S(1)}, bf16[2,2,128,256]{3,2,1,0:T(8,128)(2,1)S(1)}, u32[]{:S(2)}, u32[]{:S(2)}) collective-permute-start(bf16[2,2,128,256]{3,2,1,0:T(8,128)(2,1)S(1)} %pad_maximum_fusion.9), channel_id=1, source_target_pairs={{0,2},{1,63},{2,4},{3,1},{4,6},{5,3},{6,8},{7,5},{8,10},{9,7},{10,... | collective-permute-start | bytes 786440 | tf_op jit(solution)/shard_map/ppermute | solution.py:50
  42.0 8.9 %collective-permute-start.12 = (bf16[2,2,128,256]{3,2,1,0:T(8,128)(2,1)S(1)}, bf16[2,2,128,256]{3,2,1,0:T(8,128)(2,1)S(1)}, u32[]{:S(2)}, u32[]{:S(2)}) collective-permute-start(bf16[2,2,128,256]{3,2,1,0:T(8,128)(2,1)S(1)} %get-tuple-element.18), channel_id=1, source_target_pairs={{0,2},{1,63},{2,4},{3,1},{4,6},{5,3},{6,8},{7,5},{8,10},{9,7},{10,... | collective-permute-start | bytes 786440 | tf_op jit(solution)/shard_map/ppermute | solution.py:50
  46.1 9.2 %collective-permute-start.13 = (bf16[2,2,128,256]{3,2,1,0:T(8,128)(2,1)S(1)}, bf16[2,2,128,256]{3,2,1,0:T(8,128)(2,1)S(1)}, u32[]{:S(2)}, u32[]{:S(2)}) collective-permute-start(bf16[2,2,128,256]{3,2,1,0:T(8,128)(2,1)S(1)} %get-tuple-element.19), channel_id=1, source_target_pairs={{0,62},{1,3},{2,0},{3,5},{4,2},{5,7},{6,4},{7,9},{8,6},{9,11},{10,... | collective-permute-start | bytes 786440 | tf_op jit(solution)/shard_map/ppermute | solution.py:50
  46.1 12.2 %collective-permute-start.10 = (bf16[2,2,128,256]{3,2,1,0:T(8,128)(2,1)S(1)}, bf16[2,2,128,256]{3,2,1,0:T(8,128)(2,1)S(1)}, u32[]{:S(2)}, u32[]{:S(2)}) collective-permute-start(bf16[2,2,128,256]{3,2,1,0:T(8,128)(2,1)S(1)} %get-tuple-element.15), channel_id=1, source_target_pairs={{0,2},{1,63},{2,4},{3,1},{4,6},{5,3},{6,8},{7,5},{8,10},{9,7},{10,... | collective-permute-start | bytes 786440 | tf_op jit(solution)/shard_map/ppermute | solution.py:50
  50.9 10.3 %collective-permute-start.11 = (bf16[2,2,128,256]{3,2,1,0:T(8,128)(2,1)S(1)}, bf16[2,2,128,256]{3,2,1,0:T(8,128)(2,1)S(1)}, u32[]{:S(2)}, u32[]{:S(2)}) collective-permute-start(bf16[2,2,128,256]{3,2,1,0:T(8,128)(2,1)S(1)} %get-tuple-element.16), channel_id=1, source_target_pairs={{0,62},{1,3},{2,0},{3,5},{4,2},{5,7},{6,4},{7,9},{8,6},{9,11},{10,... | collective-permute-start | bytes 786440 | tf_op jit(solution)/shard_map/ppermute | solution.py:50
  55.4 7.9 %collective-permute-start.14 = (bf16[2,2,128,256]{3,2,1,0:T(8,128)(2,1)S(1)}, bf16[2,2,128,256]{3,2,1,0:T(8,128)(2,1)S(1)}, u32[]{:S(2)}, u32[]{:S(2)}) collective-permute-start(bf16[2,2,128,256]{3,2,1,0:T(8,128)(2,1)S(1)} %add_convert_fusion.3), channel_id=1, source_target_pairs={{0,64},{1,65},{2,66},{3,67},{4,68},{5,69},{6,70},{7,71},{8,72},{9,... | collective-permute-start | bytes 786440 | tf_op jit(solution)/shard_map/ppermute | solution.py:50
  55.6 6.1 %collective-permute-start.16 = (bf16[2,2,128,256]{3,2,1,0:T(8,128)(2,1)S(1)}, bf16[2,2,128,256]{3,2,1,0:T(8,128)(2,1)S(1)}, u32[]{:S(2)}, u32[]{:S(2)}) collective-permute-start(bf16[2,2,128,256]{3,2,1,0:T(8,128)(2,1)S(1)} %add_convert_fusion.1), channel_id=1, source_target_pairs={{0,192},{1,193},{2,194},{3,195},{4,196},{5,197},{6,198},{7,199},{8... | collective-permute-start | bytes 786440 | tf_op jit(solution)/shard_map/ppermute | solution.py:50
  61.7 6.7 %collective-permute-start.17 = (bf16[2,2,128,256]{3,2,1,0:T(8,128)(2,1)S(1)}, bf16[2,2,128,256]{3,2,1,0:T(8,128)(2,1)S(1)}, u32[]{:S(2)}, u32[]{:S(2)}) collective-permute-start(bf16[2,2,128,256]{3,2,1,0:T(8,128)(2,1)S(1)} %add_convert_fusion), channel_id=1, source_target_pairs={{0,32},{1,33},{2,34},{3,35},{4,36},{5,37},{6,38},{7,39},{8,40},{9,... | collective-permute-start | bytes 786440 | tf_op jit(solution)/shard_map/ppermute | solution.py:50
  62.0 6.4 %collective-permute-start.15 = (bf16[2,128,256]{2,1,0:T(8,128)(2,1)S(1)}, bf16[2,128,256]{2,1,0:T(8,128)(2,1)S(1)}, u32[]{:S(2)}, u32[]{:S(2)}) collective-permute-start(bf16[2,128,256]{2,1,0:T(8,128)(2,1)S(1)} %get-tuple-element.20), channel_id=1, source_target_pairs={{0,32},{1,33},{2,34},{3,35},{4,36},{5,37},{6,38},{7,39},{8,40},{9,... | collective-permute-start | bytes 393224 | tf_op jit(solution)/shard_map/ppermute | solution.py:50
  68.7 8.7 %collective-permute-start.18 = (bf16[3,128,512]{2,1,0:T(8,128)(2,1)S(1)}, bf16[3,128,512]{2,1,0:T(8,128)(2,1)S(1)}, u32[]{:S(2)}, u32[]{:S(2)}) collective-permute-start(bf16[3,128,512]{2,1,0:T(8,128)(2,1)S(1)} %get-tuple-element.27), channel_id=1, source_target_pairs={{0,1},{1,0},{2,3},{3,2},{4,5},{5,4},{6,7},{7,6},{8,9},{9,8},{10,11... | collective-permute-start | bytes 1179656 | tf_op jit(solution)/shard_map/ppermute | solution.py:50

commit v2 on v0

v2 whole, which is shorter than its diff:
```python
import math

import jax
import jax.numpy as jnp
import numpy as np
from jax import lax
from jax.experimental import pallas as pl
from jax.experimental.pallas import tpu as pltpu
from jax.sharding import PartitionSpec as P

HD = 128
BLK = 128
FRAMES = 8
WIN = 3 * BLK
AXES = ("x", "l", "h", "z", "c")
SIZES = (4, 2, 2, 8, 2)
SCALE = 1.0 / math.sqrt(HD)
EXP_SCALE = SCALE * math.log2(math.e)
BF = jnp.bfloat16
F32 = jnp.float32
VMEM = pl.BlockSpec(memory_space=pltpu.VMEM)
HBM = pl.BlockSpec(memory_space=pltpu.HBM)
SMEM = pl.BlockSpec(memory_space=pltpu.SMEM)
Q, K, V, G = range(4)


def make_perm(target):
    pairs = []
    for index in range(math.prod(SIZES)):
        place = [int(v) for v in np.unravel_index(index, SIZES)]
        pairs.append((index, int(np.ravel_multi_index(target(*place), SIZES))))
    return pairs


def over_z(x, l, h, z, c):
    near = z + 2 * c - 1
    if 0 <= near < 8:
        return (x, l, h, near, 1 - c)
    return (x, 1 - l, 1 - h, near % 8, 1 - c)


CORE = make_perm(lambda x, l, h, z, c: (x, l, h, z, 1 - c))
OVER_Z = make_perm(over_z)


def move(value, perm):
    return lax.ppermute(value, AXES, perm)


def dot_nt(a, b):
    return lax.dot_general(a, b, (((1,), (1,)), ((), ())), preferred_element_type=F32)


def dot_nn(a, b):
    return lax.dot_general(a, b, (((1,), (0,)), ((), ())), preferred_element_type=F32)


def fold(tile):
    return tile.reshape(BLK // 8, 8, BLK)


def near(frame):
    return [(frame + step) % FRAMES for step in (-1, 0, 1)]


def bytes_of(shapes):
    return sum(math.prod(s.shape) * s.dtype.itemsize for s in shapes)


def call(kernel, outs, args, scratch=(), smem=0, flops=0, space=VMEM, limit=32):
    return pl.pallas_call(
        kernel,
        out_shape=outs,
        in_specs=[SMEM] * smem + [space] * (len(args) - smem),
        out_specs=[VMEM] * len(outs),
        scratch_shapes=list(scratch),
        compiler_params=pltpu.CompilerParams(vmem_limit_bytes=limit * 1024 * 1024 if limit else None),
        cost_estimate=pl.CostEstimate(
            flops=flops, bytes_accessed=bytes_of(args) + bytes_of(outs), transcendentals=0
        ),
    )(*args)


def pack_kernel(swap, q, k, v, g, out, held, sems):
    half = BLK // 2
    copies = {}
    for place, ref in enumerate((q, k, v, g)):
        for part in range(2):
            rows = pl.ds(part * half, half)
            copies[place, part] = pltpu.make_async_copy(
                ref.at[0, rows], held.at[place, rows], sems.at[place, part]
            )
            copies[place, part].start()
    for (place, part), copy in copies.items():
        copy.wait()
        rows = slice(part * half, (part + 1) * half)
        for head in range(FRAMES):
            out[head ^ swap[0], place, rows] = held[place, rows, head * HD : (head + 1) * HD]


def unpack_kernel(swap, tile, dq, dk, dv):
    for place, ref in enumerate((dq, dk, dv)):
        for head in range(FRAMES):
            ref[0, :, head * HD : (head + 1) * HD] = tile[head ^ swap[0], place]


def column_sums(tile, f, keys, values, before):
    query = tile[f, Q]
    grad = tile[f, G]
    scores = [dot_nt(key, query) for key in keys]
    top8 = None
    for s in scores:
        one = jnp.max(fold(s), axis=0)
        top8 = one if top8 is None else jnp.maximum(top8, one)
    top = jnp.max(top8, axis=0, keepdims=True) * EXP_SCALE
    if before is not None:
        top = jnp.maximum(top, before[0])
    total8 = jnp.zeros((8, BLK), F32)
    delta8 = jnp.zeros((8, BLK), F32)
    exps = []
    grads = []
    for value, s in zip(values, scores):
        e = jnp.exp2(s * EXP_SCALE - top)
        grad_prob = dot_nt(value, grad)
        total8 = total8 + jnp.sum(fold(e), axis=0)
        delta8 = delta8 + jnp.sum(fold(e * grad_prob), axis=0)
        exps.append(e)
        grads.append(grad_prob)
    total = jnp.sum(total8, axis=0, keepdims=True)
    delta = jnp.sum(delta8, axis=0, keepdims=True)
    if before is not None:
        shrink = jnp.exp2(before[0] - top)
        total = total + before[1] * shrink
        delta = delta + before[2] * shrink
    return (top, total, delta), exps, grads


def near_sums_kernel(tile, core, stats):
    for f in range(FRAMES):
        keys = [tile[u, K] for u in near(f)] + [core[u, 0] for u in near(f)]
        values = [tile[u, V] for u in near(f)] + [core[u, 1] for u in near(f)]
        sums, _, _ = column_sums(tile, f, keys, values, None)
        for i, row in enumerate(sums):
            stats[i, f : f + 1, :] = row


def wrap_queries(tile, qw, gw):
    for i in range(FRAMES + 2):
        rows = slice(i * BLK, (i + 1) * BLK)
        qw[rows, :] = tile[(i - 1) % FRAMES, Q]
        gw[rows, :] = tile[(i - 1) % FRAMES, G]


def far_column_kernel(tile, far, stats, part, ds_by_query, final, qw, gw, p_s, ds_s):
    wrap_queries(tile, qw, gw)
    for f in range(FRAMES):
        keys = [far[u, 0] for u in near(f)]
        values = [far[u, 1] for u in near(f)]
        rows = [stats[i, f : f + 1, :] for i in range(3)]
        (top, total, delta), exps, grads = column_sums(tile, f, keys, values, rows)
        inverse = 1.0 / total
        delta = delta * inverse
        final[0, f : f + 1, :] = top + jnp.log2(total)
        final[1, f : f + 1, :] = delta
        for i, u in enumerate(near(f)):
            lanes = slice((2 - i) * BLK, (3 - i) * BLK)
            prob = exps[i] * inverse
            dscore = (prob * (grads[i] - delta)).astype(BF)
            p_s[u, :, lanes] = prob.astype(BF)
            ds_s[u, :, lanes] = dscore
            ds_by_query[f, i * BLK : (i + 1) * BLK, :] = dscore
    for u in range(FRAMES):
        rows = slice(u * BLK, u * BLK + WIN)
        part[u, 0] = (dot_nn(ds_s[u], qw[rows, :]) * SCALE).astype(BF)
        part[u, 1] = dot_nn(p_s[u], gw[rows, :]).astype(BF)


def near_columns_kernel(
    tile, core, far, ds_far, final, own_part, core_part, dq, qw, gw, kt, p_s, ds_s, dsq
):
    wrap_queries(tile, qw, gw)
    for i in range(FRAMES + 2):
        rows = slice(i * BLK, (i + 1) * BLK)
        u = (i - 1) % FRAMES
        kt[0, :, rows] = tile[u, K].T
        kt[1, :, rows] = core[u, 0].T
        kt[2, :, rows] = far[u, 0].T
    for f in range(FRAMES):
        query = tile[f, Q]
        grad = tile[f, G]
        total = final[0, f : f + 1, :]
        delta = final[1, f : f + 1, :]
        for i, u in enumerate(near(f)):
            lanes = slice((2 - i) * BLK, (3 - i) * BLK)
            for j, (key, value) in enumerate(((tile[u, K], tile[u, V]), (core[u, 0], core[u, 1]))):
                prob = jnp.exp2(dot_nt(key, query) * EXP_SCALE - total)
                dscore = (prob * (dot_nt(value, grad) - delta)).astype(BF)
                p_s[j, u, :, lanes] = prob.astype(BF)
                ds_s[j, u, :, lanes] = dscore
                dsq[j, f, i * BLK : (i + 1) * BLK, :] = dscore
    for u in range(FRAMES):
        rows = slice(u * BLK, u * BLK + WIN)
        for j, out in enumerate((own_part, core_part)):
            out[u, 0] = (dot_nn(ds_s[j, u], qw[rows, :]) * SCALE).astype(out.dtype)
            out[u, 1] = dot_nn(p_s[j, u], gw[rows, :]).astype(out.dtype)
    for f in range(FRAMES):
        rows = slice(f * BLK, f * BLK + WIN)
        acc = dot_nn(kt[0, :, rows], dsq[0, f]) + dot_nn(kt[1, :, rows], dsq[1, f])
        acc = acc + dot_nn(kt[2, :, rows], ds_far[f])
        dq[f] = (acc * SCALE).T.astype(BF)


def add_far_kernel(own_part, far_back, out):
    for u in range(FRAMES):
        for place in range(2):
            out[u, place] = own_part[u, place] + far_back[u, place].astype(F32)


def gather_kernel(part, core_back, dq, out):
    for u in range(FRAMES):
        out[u, 0] = dq[u]
        for place in range(2):
            out[u, 1 + place] = (part[u, place] + core_back[u, place].astype(F32)).astype(BF)


def on_device(queries, key_states, value_states, out_grad):
    swap = lax.axis_index("h").astype(jnp.int32).reshape(1)
    shape = jax.ShapeDtypeStruct
    pair = (FRAMES, 2, BLK, HD)
    window = (FRAMES, BLK, WIN)
    wrapped = pltpu.VMEM(((FRAMES + 2) * BLK, HD), BF)
    mats = 2 * BLK * BLK * HD * FRAMES * 3

    packed = call(
        pack_kernel,
        [shape((FRAMES, 4, BLK, HD), BF)],
        (swap, queries, key_states, value_states, out_grad),
        scratch=(pltpu.VMEM((4, BLK, FRAMES * HD), BF), pltpu.SemaphoreType.DMA((4, 2))),
        smem=1,
        space=HBM,
        limit=0,
    )[0]
    tile = lax.all_to_all(packed, ("x", "l"), 0, 0)
    keys_values = tile[:, K : V + 1]
    far = move(keys_values, OVER_Z)
    core = move(keys_values, CORE)
    stats = call(
        near_sums_kernel, [shape((3, FRAMES, BLK), F32)], (tile, core), flops=4 * mats
    )[0]
    far_part, ds_far, final = call(
        far_column_kernel,
        [
            shape(pair, BF),
            shape((FRAMES, WIN, BLK), BF),
            shape((2, FRAMES, BLK), F32),
        ],
        (tile, far, stats),
        scratch=(wrapped, wrapped, pltpu.VMEM(window, BF), pltpu.VMEM(window, BF)),
        flops=4 * mats,
    )
    far_back = move(far_part, OVER_Z)
    own_part, core_part, dq = call(
        near_columns_kernel,
        [shape(pair, F32), shape(pair, BF), shape((FRAMES, BLK, HD), BF)],
        (tile, core, far, ds_far, final),
        scratch=(
            wrapped,
            wrapped,
            pltpu.VMEM((3, HD, (FRAMES + 2) * BLK), BF),
            pltpu.VMEM((2,) + window, BF),
            pltpu.VMEM((2,) + window, BF),
            pltpu.VMEM((2, FRAMES, WIN, BLK), BF),
        ),
        flops=11 * mats,
    )
    core_back = move(core_part, CORE)
    part = call(add_far_kernel, [shape(pair, F32)], (own_part, far_back), flops=10 * mats)[0]
    grads = call(
        gather_kernel, [shape((FRAMES, 3, BLK, HD), BF)], (part, core_back, dq)
    )[0]
    back = lax.all_to_all(grads, ("x", "l"), 0, 0)
    flat = shape((1, BLK, FRAMES * HD), BF)
    return tuple(call(unpack_kernel, [flat] * 3, (swap, back), smem=1))


def solution(mesh):
    fine = jax.sharding.Mesh(mesh.devices.reshape(SIZES), AXES)
    placed = P(("x", "l"), ("h", "z", "c"), None)
    return jax.shard_map(
        on_device,
        mesh=fine,
        in_specs=(placed,) * 4,
        out_specs=(placed,) * 3,
        check_vma=False,
    )
```

time: 217 us -> 68.5 us (0.32)
  the two profiles are of different devices: /device:TPU:1 before, /device:TPU:8 now
where the time goes in v2:
time: 68.5 us; the launch traced here: 68.3 us
  blocking collectives  37.2 us (54%)
  Pallas kernels  11.8 us (17%)
  starting transfers between devices  11 us (16%)
  waiting for transfers between devices  7.4 us (11%)
  between operations  0.7 us (1%)
    all_to_all x1, blocking collectives, on_device(): tile = lax.all_to_all(packed, ('x', 'l'), 0, 0)  20.4 us
    all_to_all x1, blocking collectives, on_device(): back = lax.all_to_all(grads, ('x', 'l'), 0, 0)  16.8 us
    pallas_call x7, Pallas kernels, call(): pl.pallas_call(kernel, out_shape=outs, in_specs=[SMEM] * smem + [space] *...  11.8 us
    ppermute x4, starting transfers between devices, move(): return lax.ppermute(value, AXES, perm)  11 us
    ppermute x4, waiting for transfers between devices, move(): return lax.ppermute(value, AXES, perm)  7.4 us
  transfers between devices with their start and end apart: 4, of which 2 were waited for; matrix products, arithmetic and copies ran while one was open for 0% of the time, Pallas kernels for 9%

profile of v2, /device:TPU:8, one launch (start us, length us, event | category | flops | bytes accessed | tf_op | source)
XLA Modules:
  0.0 68.3 jit_solution(15510193856832402887)
XLA Ops:
  0.6 2.3 %shard_map.67 = bf16[8,4,128,128]{3,2,1,0:T(8,128)(2,1)} custom-call(s32[1]{0:T(128)} %bitcast.swap, bf16[1,128,1024]{2,1,0:T(8,128)(2,1)} %q.1, bf16[1,128,1024]{2,1,0:T(8,128)(2,1)} %k.1, bf16[1,128,1024]{2,1,0:T(8,128)(2,1)} %v.1, bf16[1,128,1024]{2,1,0:T(8,128)(2,1)} %g.1), custom_call_target="tpu_custom_call" | custom-call | bytes 2097156 | tf_op jit(solution)/shard_map/pallas_call | solution.py:71
  3.0 20.4 %all_to_all.10.tile = bf16[8,4,128,128]{3,2,1,0:T(8,128)(2,1)S(1)} all-to-all(bf16[8,4,128,128]{3,2,1,0:T(8,128)(2,1)} %shard_map.67), channel_id=1, replica_groups=mesh['x'=4,'l'=2,'h'=2,'z'=8,'c'=2] {'x','l'}, dimensions={0} | all-to-all | bytes 2097152 | tf_op jit(solution)/shard_map/all_to_all | solution.py:243
  23.5 0.1 collective-permute-start
  23.6 6.9 %collective-permute-start.1 = (bf16[8,2,128,128]{3,2,1,0:T(8,128)(2,1)S(1)}, bf16[8,2,128,128]{3,2,1,0:T(8,128)(2,1)S(1)}, u32[]{:S(2)}, u32[]{:S(2)}) collective-permute-start(bf16[8,2,128,128]{3,2,1,0:T(8,128)(2,1)S(1)} %slice.4), channel_id=1, source_target_pairs={{0,63},{1,2},{2,1},{3,4},{4,3},{5,6},{6,5},{7,8},{8,7},{9,10},{10,... | collective-permute-start | bytes 1572872 | tf_op jit(solution)/shard_map/ppermute | solution.py:47
  30.5 0.0 collective-permute-done.core
  30.5 2.3 %shard_map.68.stats = f32[3,8,128]{2,1,0:T(8,128)S(1)} custom-call(bf16[8,4,128,128]{3,2,1,0:T(8,128)(2,1)S(1)} %all_to_all.10.tile, bf16[8,2,128,128]{3,2,1,0:T(8,128)(2,1)S(1)} %collective-permute-done.core), custom_call_target="tpu_custom_call" | custom-call | flops 402653184 | bytes 1585152 | tf_op jit(solution)/shard_map/pallas_call | solution.py:71
  32.8 4.5 %collective-permute-done.1.far = bf16[8,2,128,128]{3,2,1,0:T(8,128)(2,1)S(1)} collective-permute-done((bf16[8,2,128,128]{3,2,1,0:T(8,128)(2,1)S(1)}, bf16[8,2,128,128]{3,2,1,0:T(8,128)(2,1)S(1)}, u32[]{:S(2)}, u32[]{:S(2)}) %collective-permute-start.1) | collective-permute-done | bytes 524320 | tf_op jit(solution)/shard_map/ppermute | solution.py:47
  37.3 2.0 %shard_map.69 = (bf16[8,2,128,128]{3,2,1,0:T(8,128)(2,1)S(1)}, bf16[8,384,128]{2,1,0:T(8,128)(2,1)S(1)}, f32[2,8,128]{2,1,0:T(8,128)S(1)}) custom-call(bf16[8,4,128,128]{3,2,1,0:T(8,128)(2,1)S(1)} %all_to_all.10.tile, bf16[8,2,128,128]{3,2,1,0:T(8,128)(2,1)S(1)} %collective-permute-done.1.far, f32[3,8,128]{2,1,0:T(8,128)S(1)} %shard_map.68.stats), custom_call_target="tpu_custom_call" | custom-call | flops 402653184 | bytes 2904064 | tf_op jit(solution)/shard_map/pallas_call | solution.py:71
  39.4 3.9 %collective-permute-start.2 = (bf16[8,2,128,128]{3,2,1,0:T(8,128)(2,1)S(1)}, bf16[8,2,128,128]{3,2,1,0:T(8,128)(2,1)S(1)}, u32[]{:S(2)}, u32[]{:S(2)}) collective-permute-start(bf16[8,2,128,128]{3,2,1,0:T(8,128)(2,1)S(1)} %get-tuple-element.12), channel_id=1, source_target_pairs={{0,63},{1,2},{2,1},{3,4},{4,3},{5,6},{6,5},{7,8},{8,7},{9,10},{10,... | collective-permute-start | bytes 1572872 | tf_op jit(solution)/shard_map/ppermute | solution.py:47
  43.3 3.9 %shard_map.70 = (f32[8,2,128,128]{3,2,1,0:T(8,128)S(1)}, bf16[8,2,128,128]{3,2,1,0:T(8,128)(2,1)S(1)}, bf16[8,128,128]{2,1,0:T(8,128)(2,1)S(1)}) custom-call(bf16[8,4,128,128]{3,2,1,0:T(8,128)(2,1)S(1)} %all_to_all.10.tile, bf16[8,2,128,128]{3,2,1,0:T(8,128)(2,1)S(1)} %collective-permute-done.core, bf16[8,2,128,128]{3,2,1,0:T(8,128)(2,1)S(1)} %collective-permute-done.1.far, ...), custom_call_target="tpu_custom_call" | custom-call | flops 1107296256 | bytes 4726784 | tf_op jit(solution)/shard_map/pallas_call | solution.py:71
  47.2 0.1 collective-permute-start.3
  47.3 2.9 %collective-permute-done.2.far_back = bf16[8,2,128,128]{3,2,1,0:T(8,128)(2,1)S(1)} collective-permute-done((bf16[8,2,128,128]{3,2,1,0:T(8,128)(2,1)S(1)}, bf16[8,2,128,128]{3,2,1,0:T(8,128)(2,1)S(1)}, u32[]{:S(2)}, u32[]{:S(2)}) %collective-permute-start.2) | collective-permute-done | bytes 524320 | tf_op jit(solution)/shard_map/ppermute | solution.py:47
  50.2 0.1 shard_map.71.part
  50.3 0.0 collective-permute-done.3.core_back
  50.3 0.1 shard_map.72
  50.4 16.8 %all_to_all.11.tile = bf16[8,3,128,128]{3,2,1,0:T(8,128)(2,1)S(1)} all-to-all(bf16[8,3,128,128]{3,2,1,0:T(8,128)(2,1)S(1)} %shard_map.72), channel_id=1, replica_groups=mesh['x'=4,'l'=2,'h'=2,'z'=8,'c'=2] {'x','l'}, dimensions={0} | all-to-all | bytes 1572864 | tf_op jit(solution)/shard_map/all_to_all | solution.py:281
  67.2 1.1 %shard_map.73 = (bf16[1,128,1024]{2,1,0:T(8,128)(2,1)}, bf16[1,128,1024]{2,1,0:T(8,128)(2,1)}, bf16[1,128,1024]{2,1,0:T(8,128)(2,1)}) custom-call(s32[1]{0:T(128)} %bitcast.swap, bf16[8,3,128,128]{3,2,1,0:T(8,128)(2,1)S(1)} %all_to_all.11.tile), custom_call_target="tpu_custom_call" | custom-call | bytes 1572868 | tf_op jit(solution)/shard_map/pallas_call | solution.py:71
  (1 shorter events, 0.0 us)
Async XLA Ops:
  23.5 7.0 %collective-permute-start = (bf16[8,2,128,128]{3,2,1,0:T(8,128)(2,1)S(1)}, bf16[8,2,128,128]{3,2,1,0:T(8,128)(2,1)S(1)}, u32[]{:S(2)}, u32[]{:S(2)}) collective-permute-start(bf16[8,2,128,128]{3,2,1,0:T(8,128)(2,1)S(1)} %slice.4), channel_id=1, source_target_pairs={{0,1},{1,0},{2,3},{3,2},{4,5},{5,4},{6,7},{7,6},{8,9},{9,8},{10,11... | collective-permute-start | bytes 1572872 | tf_op jit(solution)/shard_map/ppermute | solution.py:47
  23.6 13.8 %collective-permute-start.1 = (bf16[8,2,128,128]{3,2,1,0:T(8,128)(2,1)S(1)}, bf16[8,2,128,128]{3,2,1,0:T(8,128)(2,1)S(1)}, u32[]{:S(2)}, u32[]{:S(2)}) collective-permute-start(bf16[8,2,128,128]{3,2,1,0:T(8,128)(2,1)S(1)} %slice.4), channel_id=1, source_target_pairs={{0,63},{1,2},{2,1},{3,4},{4,3},{5,6},{6,5},{7,8},{8,7},{9,10},{10,... | collective-permute-start | bytes 1572872 | tf_op jit(solution)/shard_map/ppermute | solution.py:47
  39.4 10.8 %collective-permute-start.2 = (bf16[8,2,128,128]{3,2,1,0:T(8,128)(2,1)S(1)}, bf16[8,2,128,128]{3,2,1,0:T(8,128)(2,1)S(1)}, u32[]{:S(2)}, u32[]{:S(2)}) collective-permute-start(bf16[8,2,128,128]{3,2,1,0:T(8,128)(2,1)S(1)} %get-tuple-element.12), channel_id=1, source_target_pairs={{0,63},{1,2},{2,1},{3,4},{4,3},{5,6},{6,5},{7,8},{8,7},{9,10},{10,... | collective-permute-start | bytes 1572872 | tf_op jit(solution)/shard_map/ppermute | solution.py:47
  47.2 3.0 %collective-permute-start.3 = (bf16[8,2,128,128]{3,2,1,0:T(8,128)(2,1)S(1)}, bf16[8,2,128,128]{3,2,1,0:T(8,128)(2,1)S(1)}, u32[]{:S(2)}, u32[]{:S(2)}) collective-permute-start(bf16[8,2,128,128]{3,2,1,0:T(8,128)(2,1)S(1)} %get-tuple-element.13), channel_id=1, source_target_pairs={{0,1},{1,0},{2,3},{3,2},{4,5},{5,4},{6,7},{7,6},{8,9},{9,8},{10,11... | collective-permute-start | bytes 1572872 | tf_op jit(solution)/shard_map/ppermute | solution.py:47

commit v3 on v2

v3 whole, which is shorter than its diff:
```python
import math

import jax
import jax.numpy as jnp
import numpy as np
from jax import lax
from jax.experimental import pallas as pl
from jax.experimental.pallas import tpu as pltpu
from jax.sharding import PartitionSpec as P

HD = 128
BLK = 128
FRAMES = 8
WIN = 3 * BLK
AXES = ("x", "l", "h", "z", "c")
SIZES = (4, 2, 2, 8, 2)
SCALE = 1.0 / math.sqrt(HD)
EXP_SCALE = SCALE * math.log2(math.e)
BF = jnp.bfloat16
F32 = jnp.float32
VMEM = pl.BlockSpec(memory_space=pltpu.VMEM)
HBM = pl.BlockSpec(memory_space=pltpu.HBM)
SMEM = pl.BlockSpec(memory_space=pltpu.SMEM)


def make_perm(target):
    pairs = []
    for index in range(math.prod(SIZES)):
        place = [int(v) for v in np.unravel_index(index, SIZES)]
        pairs.append((index, int(np.ravel_multi_index(target(*place), SIZES))))
    return pairs


def over_z(x, l, h, z, c):
    near = z + 2 * c - 1
    if 0 <= near < 8:
        return (x, l, h, near, 1 - c)
    return (x, 1 - l, 1 - h, near % 8, 1 - c)


CORE = make_perm(lambda x, l, h, z, c: (x, l, h, z, 1 - c))
OVER_Z = make_perm(over_z)


def move(value, perm):
    return lax.ppermute(value, AXES, perm)


def dot_nt(a, b):
    return lax.dot_general(a, b, (((1,), (1,)), ((), ())), preferred_element_type=F32)


def dot_nn(a, b):
    return lax.dot_general(a, b, (((1,), (0,)), ((), ())), preferred_element_type=F32)


def bytes_of(shapes):
    return sum(math.prod(s.shape) * s.dtype.itemsize for s in shapes)


def call(kernel, outs, args, scratch=(), smem=0, flops=0, space=VMEM, limit=32):
    return pl.pallas_call(
        kernel,
        out_shape=outs,
        in_specs=[SMEM] * smem + [space] * (len(args) - smem),
        out_specs=[VMEM] * len(outs),
        scratch_shapes=list(scratch),
        compiler_params=pltpu.CompilerParams(vmem_limit_bytes=limit * 1024 * 1024 if limit else None),
        cost_estimate=pl.CostEstimate(
            flops=flops, bytes_accessed=bytes_of(args) + bytes_of(outs), transcendentals=0
        ),
    )(*args)


def pack_kernel(swap, q, g, k, v, out, held, sems):
    half = BLK // 2
    copies = {}
    for place, ref in enumerate((q, g, k, v)):
        for part in range(2):
            rows = pl.ds(part * half, half)
            copies[place, part] = pltpu.make_async_copy(
                ref.at[0, rows], held.at[place, rows], sems.at[place, part]
            )
            copies[place, part].start()
    for (place, part), copy in copies.items():
        copy.wait()
        rows = slice(part * half, (part + 1) * half)
        lanes = slice((place % 2) * HD, (place % 2 + 1) * HD)
        for head in range(FRAMES):
            out[head ^ swap[0], place // 2, rows, lanes] = held[
                place, rows, head * HD : (head + 1) * HD
            ]


def unpack_kernel(swap, tile, dq, dk, dv):
    for place, ref in enumerate((dq, dk, dv)):
        for head in range(FRAMES):
            ref[0, :, head * HD : (head + 1) * HD] = tile[head ^ swap[0], place]


def block_diagonal(read, diag):
    diag[...] = jnp.zeros(diag.shape, BF)
    for f in range(FRAMES):
        both = read(f)
        diag[f, :BLK, :HD] = both[:, :HD]
        diag[f, BLK:, HD:] = both[:, HD:]


def wrap_frames(read, wrapped):
    for i in range(FRAMES + 2):
        wrapped[i * BLK : (i + 1) * BLK, :] = read((i - 1) % FRAMES)


def window(f):
    return slice(f * BLK, f * BLK + WIN)


def fold(tile):
    return tile.reshape(WIN // 8, 8, BLK)


def column_sums(columns, diag, f, before):
    both = [dot_nt(wrapped[window(f), :], diag[f]) for wrapped in columns]
    top8 = None
    for x in both:
        one = jnp.max(fold(x[:, :BLK]), axis=0)
        top8 = one if top8 is None else jnp.maximum(top8, one)
    top = jnp.max(top8, axis=0, keepdims=True) * EXP_SCALE
    if before is not None:
        top = jnp.maximum(top, before[0])
    total8 = jnp.zeros((8, BLK), F32)
    delta8 = jnp.zeros((8, BLK), F32)
    for x in both:
        e = jnp.exp2(x[:, :BLK] * EXP_SCALE - top)
        total8 = total8 + jnp.sum(fold(e), axis=0)
        delta8 = delta8 + jnp.sum(fold(e * x[:, BLK:]), axis=0)
    total = jnp.sum(total8, axis=0, keepdims=True)
    delta = jnp.sum(delta8, axis=0, keepdims=True)
    if before is not None:
        shrink = jnp.exp2(before[0] - top)
        total = total + before[1] * shrink
        delta = delta + before[2] * shrink
    return top, total, delta


def own_sums_kernel(tile, stats, queries, diag, kv_own):
    block_diagonal(lambda f: tile[f, 0], diag)
    wrap_frames(lambda f: tile[f, 1], kv_own)
    for f in range(FRAMES):
        queries[f] = tile[f, 0]
        for i, row in enumerate(column_sums((kv_own,), diag, f, None)):
            stats[i, f : f + 1, :] = row


def side_sums_kernel(tile, core, far, before, final, diag, kv_far, kv_core):
    block_diagonal(lambda f: tile[f, 0], diag)
    wrap_frames(lambda f: far[f], kv_far)
    wrap_frames(lambda f: core[f], kv_core)
    for f in range(FRAMES):
        rows = [before[i, f : f + 1, :] for i in range(3)]
        top, total, delta = column_sums((kv_far, kv_core), diag, f, rows)
        final[0, f : f + 1, :] = top + jnp.log2(total)
        final[1, f : f + 1, :] = delta / total


def prob_and_dscore(keys_values, diag, final, f):
    both = dot_nt(keys_values[window(f), :], diag[f])
    prob = jnp.exp2(both[:, :BLK] * EXP_SCALE - final[0, f : f + 1, :])
    dscore = prob * (both[:, BLK:] - final[1, f : f + 1, :])
    return prob.astype(BF), dscore.astype(BF)


def add_key_grads(dscore, prob, diag, f, total):
    both = jnp.concatenate([dscore, prob], axis=1)
    total[window(f), :] += dot_nn(both, diag[f])


def key_grads(total, u):
    got = total[(u + 1) * BLK : (u + 2) * BLK, :]
    if u == FRAMES - 1:
        got = got + total[:BLK, :]
    if u == 0:
        got = got + total[(FRAMES + 1) * BLK :, :]
    return got


def own_queries_kernel(
    tile, core, far, final, part, dq, diag, kv_own, kv_core, kv_far, kt, total
):
    columns = (kv_own, kv_core, kv_far)
    block_diagonal(lambda f: tile[f, 0], diag)
    wrap_frames(lambda f: tile[f, 1], kv_own)
    wrap_frames(lambda f: core[f], kv_core)
    wrap_frames(lambda f: far[f], kv_far)
    for j, wrapped in enumerate(columns):
        for i in range(FRAMES + 2):
            rows = slice(i * BLK, (i + 1) * BLK)
            kt[j, :, rows] = wrapped[rows, :HD].T
    total[...] = jnp.zeros(total.shape, F32)
    for f in range(FRAMES):
        acc = None
        for j, wrapped in enumerate(columns):
            prob, dscore = prob_and_dscore(wrapped, diag, final, f)
            one = dot_nn(kt[j, :, window(f)], dscore)
            acc = one if acc is None else acc + one
            if j == 0:
                add_key_grads(dscore, prob, diag, f, total)
        dq[f] = (acc * SCALE).T.astype(BF)
    for u in range(FRAMES):
        part[u] = key_grads(total, u)


def side_queries(tile, side, final, diag, kv_own, total):
    block_diagonal(lambda f: side[f], diag)
    wrap_frames(lambda f: tile[f, 1], kv_own)
    total[...] = jnp.zeros(total.shape, F32)
    for f in range(FRAMES):
        prob, dscore = prob_and_dscore(kv_own, diag, final, f)
        add_key_grads(dscore, prob, diag, f, total)


def core_queries_kernel(tile, side, final, before, part, diag, kv_own, total):
    side_queries(tile, side, final, diag, kv_own, total)
    for u in range(FRAMES):
        part[u] = before[u] + key_grads(total, u)


def far_queries_kernel(tile, side, final, before, dq, out, diag, kv_own, total):
    side_queries(tile, side, final, diag, kv_own, total)
    for u in range(FRAMES):
        both = before[u] + key_grads(total, u)
        out[u, 0] = dq[u]
        out[u, 1] = (both[:, :HD] * SCALE).astype(BF)
        out[u, 2] = both[:, HD:].astype(BF)


def on_device(queries, key_states, value_states, out_grad):
    swap = lax.axis_index("h").astype(jnp.int32).reshape(1)
    shape = jax.ShapeDtypeStruct
    both = (FRAMES, BLK, 2 * HD)
    wrapped = pltpu.VMEM(((FRAMES + 2) * BLK, 2 * HD), BF)
    summed = pltpu.VMEM(((FRAMES + 2) * BLK, 2 * HD), F32)
    diag = pltpu.VMEM((FRAMES, 2 * BLK, 2 * HD), BF)
    mats = 2 * BLK * BLK * HD * FRAMES * 3

    packed = call(
        pack_kernel,
        [shape((FRAMES, 2, BLK, 2 * HD), BF)],
        (swap, queries, out_grad, key_states, value_states),
        scratch=(pltpu.VMEM((4, BLK, FRAMES * HD), BF), pltpu.SemaphoreType.DMA((4, 2))),
        smem=1,
        space=HBM,
        limit=0,
    )[0]
    tile = lax.all_to_all(packed, ("x", "l"), 0, 0)
    keys_values = tile[:, 1]
    far_keys = move(keys_values, OVER_Z)
    core_keys = move(keys_values, CORE)
    sums, queries_grads = call(
        own_sums_kernel,
        [shape((3, FRAMES, BLK), F32), shape(both, BF)],
        (tile,),
        scratch=(diag, wrapped),
        flops=2 * mats,
    )
    far_queries = move(queries_grads, OVER_Z)
    core_queries = move(queries_grads, CORE)
    final = call(
        side_sums_kernel,
        [shape((2, FRAMES, BLK), F32)],
        (tile, core_keys, far_keys, sums),
        scratch=(diag, wrapped, wrapped),
        flops=4 * mats,
    )[0]
    far_final = move(final, OVER_Z)
    core_final = move(final, CORE)
    own_part, dq = call(
        own_queries_kernel,
        [shape(both, F32), shape((FRAMES, BLK, HD), BF)],
        (tile, core_keys, far_keys, final),
        scratch=(
            diag,
            wrapped,
            wrapped,
            wrapped,
            pltpu.VMEM((3, HD, (FRAMES + 2) * BLK), BF),
            summed,
        ),
        flops=11 * mats,
    )
    part = call(
        core_queries_kernel,
        [shape(both, F32)],
        (tile, core_queries, core_final, own_part),
        scratch=(diag, wrapped, summed),
        flops=4 * mats,
    )[0]
    grads = call(
        far_queries_kernel,
        [shape((FRAMES, 3, BLK, HD), BF)],
        (tile, far_queries, far_final, part, dq),
        scratch=(diag, wrapped, summed),
        flops=4 * mats,
    )[0]
    back = lax.all_to_all(grads, ("x", "l"), 0, 0)
    flat = shape((1, BLK, FRAMES * HD), BF)
    return tuple(call(unpack_kernel, [flat] * 3, (swap, back), smem=1))


def solution(mesh):
    fine = jax.sharding.Mesh(mesh.devices.reshape(SIZES), AXES)
    placed = P(("x", "l"), ("h", "z", "c"), None)
    return jax.shard_map(
        on_device,
        mesh=fine,
        in_specs=(placed,) * 4,
        out_specs=(placed,) * 3,
        check_vma=False,
    )
```

time: 68.5 us -> 63.5 us (0.927)
  waiting for transfers between devices: 7.4 us -> 3.66 us
  blocking collectives: 37.2 us -> 35 us
  Pallas kernels: 11.8 us -> 12.5 us
    ppermute x4 -> x6, waiting for transfers between devices: 7.4 us -> 3.66 us  [move(): return lax.ppermute(value, AXES, perm)]
    all_to_all x1, blocking collectives: 16.8 us -> 14.6 us  [on_device(): back = lax.all_to_all(grads, ('x', 'l'), 0, 0)]
    ppermute x4 -> x6, starting transfers between devices: 11 us -> 11.3 us  [move(): return lax.ppermute(value, AXES, perm)]
  transfers between devices with their start and end apart: 4 -> 6, of which waited for: 2 -> 1; matrix products, arithmetic and copies ran while one was open for 0% -> 0% of each run, Pallas kernels for 9% -> 12%
where the time goes in v3:
time: 63.5 us; the launch traced here: 63.3 us
  blocking collectives  35 us (55%)
  Pallas kernels  12.5 us (20%)
  starting transfers between devices  11.3 us (18%)
  waiting for transfers between devices  3.66 us (6%)
  between operations  0.72 us (1%)
    all_to_all x1, blocking collectives, on_device(): tile = lax.all_to_all(packed, ('x', 'l'), 0, 0)  20.4 us
    all_to_all x1, blocking collectives, on_device(): back = lax.all_to_all(grads, ('x', 'l'), 0, 0)  14.6 us
    pallas_call x7, Pallas kernels, call(): pl.pallas_call(kernel, out_shape=outs, in_specs=[SMEM] * smem + [space] *...  12.5 us
    ppermute x6, starting transfers between devices, move(): return lax.ppermute(value, AXES, perm)  11.3 us
    ppermute x6, waiting for transfers between devices, move(): return lax.ppermute(value, AXES, perm)  3.66 us
  transfers between devices with their start and end apart: 6, of which 1 were waited for; matrix products, arithmetic and copies ran while one was open for 0% of the time, Pallas kernels for 12%

profile of v3, /device:TPU:8, one launch (start us, length us, event | category | flops | bytes accessed | tf_op | source)
XLA Modules:
  0.0 63.3 jit_solution(5460730702792221870)
XLA Ops:
  0.6 2.3 %shard_map.67 = bf16[8,2,128,256]{3,2,1,0:T(8,128)(2,1)} custom-call(s32[1]{0:T(128)} %bitcast.swap, bf16[1,128,1024]{2,1,0:T(8,128)(2,1)} %q.1, bf16[1,128,1024]{2,1,0:T(8,128)(2,1)} %g.1, bf16[1,128,1024]{2,1,0:T(8,128)(2,1)} %k.1, bf16[1,128,1024]{2,1,0:T(8,128)(2,1)} %v.1), custom_call_target="tpu_custom_call" | custom-call | bytes 2097156 | tf_op jit(solution)/shard_map/pallas_call | solution.py:62
  3.0 20.4 %all_to_all.10.tile = bf16[8,2,128,256]{3,2,1,0:T(8,128)(2,1)S(1)} all-to-all(bf16[8,2,128,256]{3,2,1,0:T(8,128)(2,1)} %shard_map.67), channel_id=1, replica_groups=mesh['x'=4,'l'=2,'h'=2,'z'=8,'c'=2] {'x','l'}, dimensions={0} | all-to-all | bytes 2097152 | tf_op jit(solution)/shard_map/all_to_all | solution.py:255
  23.5 5.0 %collective-permute-start.2 = (bf16[8,128,256]{2,1,0:T(8,128)(2,1)S(1)}, bf16[8,128,256]{2,1,0:T(8,128)(2,1)S(1)}, u32[]{:S(2)}, u32[]{:S(2)}) collective-permute-start(bf16[8,128,256]{2,1,0:T(8,128)(2,1)S(1)} %slice_bitcast_fusion), channel_id=1, source_target_pairs={{0,63},{1,2},{2,1},{3,4},{4,3},{5,6},{6,5},{7,8},{8,7},{9,10},{10,... | collective-permute-start | bytes 1572872 | tf_op jit(solution)/shard_map/ppermute | solution.py:46
  28.5 0.0 collective-permute-start.1
  28.5 0.9 %shard_map.68 = (f32[3,8,128]{2,1,0:T(8,128)S(1)}, bf16[8,128,256]{2,1,0:T(8,128)(2,1)S(1)}) custom-call(bf16[8,2,128,256]{3,2,1,0:T(8,128)(2,1)S(1)} %all_to_all.10.tile), custom_call_target="tpu_custom_call" | custom-call | flops 201326592 | bytes 1585152 | tf_op jit(solution)/shard_map/pallas_call | solution.py:62
  29.4 0.6 collective-permute-start.4
  30.0 1.7 %collective-permute-start = (bf16[8,128,256]{2,1,0:T(8,128)(2,1)S(1)}, bf16[8,128,256]{2,1,0:T(8,128)(2,1)S(1)}, u32[]{:S(2)}, u32[]{:S(2)}) collective-permute-start(bf16[8,128,256]{2,1,0:T(8,128)(2,1)S(1)} %get-tuple-element.7), channel_id=1, source_target_pairs={{0,63},{1,2},{2,1},{3,4},{4,3},{5,6},{6,5},{7,8},{8,7},{9,10},{10,... | collective-permute-start | bytes 1572872 | tf_op jit(solution)/shard_map/ppermute | solution.py:46
  31.7 3.6 %collective-permute-done.2.far = bf16[8,128,256]{2,1,0:T(8,128)(2,1)S(1)} collective-permute-done((bf16[8,128,256]{2,1,0:T(8,128)(2,1)S(1)}, bf16[8,128,256]{2,1,0:T(8,128)(2,1)S(1)}, u32[]{:S(2)}, u32[]{:S(2)}) %collective-permute-start.2) | collective-permute-done | bytes 524320 | tf_op jit(solution)/shard_map/ppermute | solution.py:46
  35.3 0.0 collective-permute-done.1.core
  35.4 1.7 %shard_map.69.final = f32[2,8,128]{2,1,0:T(8,128)S(1)} custom-call(bf16[8,2,128,256]{3,2,1,0:T(8,128)(2,1)S(1)} %all_to_all.10.tile, bf16[8,128,256]{2,1,0:T(8,128)(2,1)S(1)} %collective-permute-done.1.core, bf16[8,128,256]{2,1,0:T(8,128)(2,1)S(1)} %collective-permute-done.2.far, f32[3,8,128]{2,1,0:T(8,128)S(1)} %get-tuple-element.8.before), custom_call_target="tpu_custom_call" | custom-call | flops 402653184 | bytes 2117632 | tf_op jit(solution)/shard_map/pallas_call | solution.py:62
  37.1 0.1 collective-permute-start.5
  37.2 3.9 %collective-permute-start.3 = (f32[2,8,128]{2,1,0:T(8,128)S(1)}, f32[2,8,128]{2,1,0:T(8,128)S(1)}, u32[]{:S(2)}, u32[]{:S(2)}) collective-permute-start(f32[2,8,128]{2,1,0:T(8,128)S(1)} %shard_map.69.final), channel_id=1, source_target_pairs={{0,63},{1,2},{2,1},{3,4},{4,3},{5,6},{6,5},{7,8},{8,7},{9,10},{10,... | collective-permute-start | bytes 24584 | tf_op jit(solution)/shard_map/ppermute | solution.py:46
  41.1 3.9 %shard_map.70 = (f32[8,128,256]{2,1,0:T(8,128)S(1)}, bf16[8,128,128]{2,1,0:T(8,128)(2,1)S(1)}) custom-call(bf16[8,2,128,256]{3,2,1,0:T(8,128)(2,1)S(1)} %all_to_all.10.tile, bf16[8,128,256]{2,1,0:T(8,128)(2,1)S(1)} %collective-permute-done.1.core, bf16[8,128,256]{2,1,0:T(8,128)(2,1)S(1)} %collective-permute-done.2.far, f32[2,8,128]{2,1,0:T(8,128)S(1)} %shard_map.69.final), custom_call_target="tpu_custom_call" | custom-call | flops 1107296256 | bytes 3416064 | tf_op jit(solution)/shard_map/pallas_call | solution.py:62
  45.0 0.0 collective-permute-done.4.side
  45.0 0.0 collective-permute-done.5.final
  45.0 1.3 %shard_map.71.before = f32[8,128,256]{2,1,0:T(8,128)S(1)} custom-call(bf16[8,2,128,256]{3,2,1,0:T(8,128)(2,1)S(1)} %all_to_all.10.tile, bf16[8,128,256]{2,1,0:T(8,128)(2,1)S(1)} %collective-permute-done.4.side, f32[2,8,128]{2,1,0:T(8,128)S(1)} %collective-permute-done.5.final, f32[8,128,256]{2,1,0:T(8,128)S(1)} %get-tuple-element.9.before), custom_call_target="tpu_custom_call" | custom-call | flops 402653184 | bytes 3678208 | tf_op jit(solution)/shard_map/pallas_call | solution.py:62
  46.3 0.0 collective-permute-done.side
  46.3 0.0 collective-permute-done.3.final
  46.3 1.3 %shard_map.72 = bf16[8,3,128,128]{3,2,1,0:T(8,128)(2,1)S(1)} custom-call(bf16[8,2,128,256]{3,2,1,0:T(8,128)(2,1)S(1)} %all_to_all.10.tile, bf16[8,128,256]{2,1,0:T(8,128)(2,1)S(1)} %collective-permute-done.side, f32[2,8,128]{2,1,0:T(8,128)S(1)} %collective-permute-done.3.final, f32[8,128,256]{2,1,0:T(8,128)S(1)} %shard_map.71.before, ...), custom_call_target="tpu_custom_call" | custom-call | flops 402653184 | bytes 3678208 | tf_op jit(solution)/shard_map/pallas_call | solution.py:62
  47.6 14.6 %all_to_all.11.tile = bf16[8,3,128,128]{3,2,1,0:T(8,128)(2,1)S(1)} all-to-all(bf16[8,3,128,128]{3,2,1,0:T(8,128)(2,1)S(1)} %shard_map.72), channel_id=1, replica_groups=mesh['x'=4,'l'=2,'h'=2,'z'=8,'c'=2] {'x','l'}, dimensions={0} | all-to-all | bytes 1572864 | tf_op jit(solution)/shard_map/all_to_all | solution.py:305
  62.2 1.1 %shard_map.73 = (bf16[1,128,1024]{2,1,0:T(8,128)(2,1)}, bf16[1,128,1024]{2,1,0:T(8,128)(2,1)}, bf16[1,128,1024]{2,1,0:T(8,128)(2,1)}) custom-call(s32[1]{0:T(128)} %bitcast.swap, bf16[8,3,128,128]{3,2,1,0:T(8,128)(2,1)S(1)} %all_to_all.11.tile), custom_call_target="tpu_custom_call" | custom-call | bytes 1572868 | tf_op jit(solution)/shard_map/pallas_call | solution.py:62
  (1 shorter events, 0.0 us)
Async XLA Ops:
  23.5 11.9 %collective-permute-start.2 = (bf16[8,128,256]{2,1,0:T(8,128)(2,1)S(1)}, bf16[8,128,256]{2,1,0:T(8,128)(2,1)S(1)}, u32[]{:S(2)}, u32[]{:S(2)}) collective-permute-start(bf16[8,128,256]{2,1,0:T(8,128)(2,1)S(1)} %slice_bitcast_fusion), channel_id=1, source_target_pairs={{0,63},{1,2},{2,1},{3,4},{4,3},{5,6},{6,5},{7,8},{8,7},{9,10},{10,... | collective-permute-start | bytes 1572872 | tf_op jit(solution)/shard_map/ppermute | solution.py:46
  28.5 6.9 %collective-permute-start.1 = (bf16[8,128,256]{2,1,0:T(8,128)(2,1)S(1)}, bf16[8,128,256]{2,1,0:T(8,128)(2,1)S(1)}, u32[]{:S(2)}, u32[]{:S(2)}) collective-permute-start(bf16[8,128,256]{2,1,0:T(8,128)(2,1)S(1)} %slice_bitcast_fusion), channel_id=1, source_target_pairs={{0,1},{1,0},{2,3},{3,2},{4,5},{5,4},{6,7},{7,6},{8,9},{9,8},{10,11... | collective-permute-start | bytes 1572872 | tf_op jit(solution)/shard_map/ppermute | solution.py:46
  29.4 15.6 %collective-permute-start.4 = (bf16[8,128,256]{2,1,0:T(8,128)(2,1)S(1)}, bf16[8,128,256]{2,1,0:T(8,128)(2,1)S(1)}, u32[]{:S(2)}, u32[]{:S(2)}) collective-permute-start(bf16[8,128,256]{2,1,0:T(8,128)(2,1)S(1)} %get-tuple-element.7), channel_id=1, source_target_pairs={{0,1},{1,0},{2,3},{3,2},{4,5},{5,4},{6,7},{7,6},{8,9},{9,8},{10,11... | collective-permute-start | bytes 1572872 | tf_op jit(solution)/shard_map/ppermute | solution.py:46
  30.0 16.3 %collective-permute-start = (bf16[8,128,256]{2,1,0:T(8,128)(2,1)S(1)}, bf16[8,128,256]{2,1,0:T(8,128)(2,1)S(1)}, u32[]{:S(2)}, u32[]{:S(2)}) collective-permute-start(bf16[8,128,256]{2,1,0:T(8,128)(2,1)S(1)} %get-tuple-element.7), channel_id=1, source_target_pairs={{0,63},{1,2},{2,1},{3,4},{4,3},{5,6},{6,5},{7,8},{8,7},{9,10},{10,... | collective-permute-start | bytes 1572872 | tf_op jit(solution)/shard_map/ppermute | solution.py:46
  37.1 7.9 %collective-permute-start.5 = (f32[2,8,128]{2,1,0:T(8,128)S(1)}, f32[2,8,128]{2,1,0:T(8,128)S(1)}, u32[]{:S(2)}, u32[]{:S(2)}) collective-permute-start(f32[2,8,128]{2,1,0:T(8,128)S(1)} %shard_map.69.final), channel_id=1, source_target_pairs={{0,1},{1,0},{2,3},{3,2},{4,5},{5,4},{6,7},{7,6},{8,9},{9,8},{10,11... | collective-permute-start | bytes 24584 | tf_op jit(solution)/shard_map/ppermute | solution.py:46
  37.2 9.1 %collective-permute-start.3 = (f32[2,8,128]{2,1,0:T(8,128)S(1)}, f32[2,8,128]{2,1,0:T(8,128)S(1)}, u32[]{:S(2)}, u32[]{:S(2)}) collective-permute-start(f32[2,8,128]{2,1,0:T(8,128)S(1)} %shard_map.69.final), channel_id=1, source_target_pairs={{0,63},{1,2},{2,1},{3,4},{4,3},{5,6},{6,5},{7,8},{8,7},{9,10},{10,... | collective-permute-start | bytes 24584 | tf_op jit(solution)/shard_map/ppermute | solution.py:46

commit v4 on v3

--- a/solution.py
+++ b/solution.py
@@ -73,10 +73,10 @@
 
 
 def pack_kernel(swap, q, g, k, v, out, held, sems):
-    half = BLK // 2
+    half = BLK // 4
     copies = {}
     for place, ref in enumerate((q, g, k, v)):
-        for part in range(2):
+        for part in range(4):
             rows = pl.ds(part * half, half)
             copies[place, part] = pltpu.make_async_copy(
                 ref.at[0, rows], held.at[place, rows], sems.at[place, part]
@@ -245,9 +245,9 @@
 
     packed = call(
         pack_kernel,
-        [shape((FRAMES, 2, BLK, 2 * HD), BF)],
+        [pltpu.VMEM((FRAMES, 2, BLK, 2 * HD), BF)],
         (swap, queries, out_grad, key_states, value_states),
-        scratch=(pltpu.VMEM((4, BLK, FRAMES * HD), BF), pltpu.SemaphoreType.DMA((4, 2))),
+        scratch=(pltpu.VMEM((4, BLK, FRAMES * HD), BF), pltpu.SemaphoreType.DMA((4, 4))),
         smem=1,
         space=HBM,
         limit=0,

time: 63.5 us -> 62.4 us (0.983)
  Pallas kernels: 12.5 us -> 11.7 us
    pallas_call x7, Pallas kernels: 12.5 us -> 11.7 us  [call(): pl.pallas_call(kernel, out_shape=outs, in_specs=[SMEM] * smem + [space] *...]
  transfers between devices with their start and end apart: 6 -> 6, of which waited for: 1 -> 1; matrix products, arithmetic and copies ran while one was open for 0% -> 0% of each run, Pallas kernels for 12% -> 13%
where the time goes in v4:
time: 62.4 us; the launch traced here: 62.2 us
  blocking collectives  34.8 us (56%)
  Pallas kernels  11.7 us (19%)
  starting transfers between devices  11.3 us (18%)
  waiting for transfers between devices  3.63 us (6%)
  between operations  0.72 us (1%)
    all_to_all x1, blocking collectives, on_device(): tile = lax.all_to_all(packed, ('x', 'l'), 0, 0)  20.2 us
    all_to_all x1, blocking collectives, on_device(): back = lax.all_to_all(grads, ('x', 'l'), 0, 0)  14.6 us
    pallas_call x7, Pallas kernels, call(): pl.pallas_call(kernel, out_shape=outs, in_specs=[SMEM] * smem + [space] *...  11.7 us
    ppermute x6, starting transfers between devices, move(): return lax.ppermute(value, AXES, perm)  11.3 us
    ppermute x6, waiting for transfers between devices, move(): return lax.ppermute(value, AXES, perm)  3.63 us
  transfers between devices with their start and end apart: 6, of which 1 were waited for; matrix products, arithmetic and copies ran while one was open for 0% of the time, Pallas kernels for 13%

profile of v4, /device:TPU:8, one launch (start us, length us, event | category | flops | bytes accessed | tf_op | source)
XLA Modules:
  0.0 62.2 jit_solution(2038835426421244248)
XLA Ops:
  0.6 1.4 %shard_map.67 = bf16[8,2,128,256]{3,2,1,0:T(8,128)(2,1)S(1)} custom-call(s32[1]{0:T(128)} %bitcast.swap, bf16[1,128,1024]{2,1,0:T(8,128)(2,1)} %q.1, bf16[1,128,1024]{2,1,0:T(8,128)(2,1)} %g.1, bf16[1,128,1024]{2,1,0:T(8,128)(2,1)} %k.1, bf16[1,128,1024]{2,1,0:T(8,128)(2,1)} %v.1), custom_call_target="tpu_custom_call" | custom-call | bytes 2097156 | tf_op jit(solution)/shard_map/pallas_call | solution.py:62
  2.0 20.2 %all_to_all.10.tile = bf16[8,2,128,256]{3,2,1,0:T(8,128)(2,1)S(1)} all-to-all(bf16[8,2,128,256]{3,2,1,0:T(8,128)(2,1)S(1)} %shard_map.67), channel_id=1, replica_groups=mesh['x'=4,'l'=2,'h'=2,'z'=8,'c'=2] {'x','l'}, dimensions={0} | all-to-all | bytes 2097152 | tf_op jit(solution)/shard_map/all_to_all | solution.py:255
  22.3 5.0 %collective-permute-start.2 = (bf16[8,128,256]{2,1,0:T(8,128)(2,1)S(1)}, bf16[8,128,256]{2,1,0:T(8,128)(2,1)S(1)}, u32[]{:S(2)}, u32[]{:S(2)}) collective-permute-start(bf16[8,128,256]{2,1,0:T(8,128)(2,1)S(1)} %slice_bitcast_fusion), channel_id=1, source_target_pairs={{0,63},{1,2},{2,1},{3,4},{4,3},{5,6},{6,5},{7,8},{8,7},{9,10},{10,... | collective-permute-start | bytes 1572872 | tf_op jit(solution)/shard_map/ppermute | solution.py:46
  27.3 0.0 collective-permute-start.1
  27.3 1.0 %shard_map.68 = (f32[3,8,128]{2,1,0:T(8,128)S(1)}, bf16[8,128,256]{2,1,0:T(8,128)(2,1)S(1)}) custom-call(bf16[8,2,128,256]{3,2,1,0:T(8,128)(2,1)S(1)} %all_to_all.10.tile), custom_call_target="tpu_custom_call" | custom-call | flops 201326592 | bytes 1585152 | tf_op jit(solution)/shard_map/pallas_call | solution.py:62
  28.3 0.6 collective-permute-start.4
  28.9 1.7 %collective-permute-start = (bf16[8,128,256]{2,1,0:T(8,128)(2,1)S(1)}, bf16[8,128,256]{2,1,0:T(8,128)(2,1)S(1)}, u32[]{:S(2)}, u32[]{:S(2)}) collective-permute-start(bf16[8,128,256]{2,1,0:T(8,128)(2,1)S(1)} %get-tuple-element.7), channel_id=1, source_target_pairs={{0,63},{1,2},{2,1},{3,4},{4,3},{5,6},{6,5},{7,8},{8,7},{9,10},{10,... | collective-permute-start | bytes 1572872 | tf_op jit(solution)/shard_map/ppermute | solution.py:46
  30.6 3.6 %collective-permute-done.2.far = bf16[8,128,256]{2,1,0:T(8,128)(2,1)S(1)} collective-permute-done((bf16[8,128,256]{2,1,0:T(8,128)(2,1)S(1)}, bf16[8,128,256]{2,1,0:T(8,128)(2,1)S(1)}, u32[]{:S(2)}, u32[]{:S(2)}) %collective-permute-start.2) | collective-permute-done | bytes 524320 | tf_op jit(solution)/shard_map/ppermute | solution.py:46
  34.2 0.0 collective-permute-done.1.core
  34.2 1.7 %shard_map.69.final = f32[2,8,128]{2,1,0:T(8,128)S(1)} custom-call(bf16[8,2,128,256]{3,2,1,0:T(8,128)(2,1)S(1)} %all_to_all.10.tile, bf16[8,128,256]{2,1,0:T(8,128)(2,1)S(1)} %collective-permute-done.1.core, bf16[8,128,256]{2,1,0:T(8,128)(2,1)S(1)} %collective-permute-done.2.far, f32[3,8,128]{2,1,0:T(8,128)S(1)} %get-tuple-element.8.before), custom_call_target="tpu_custom_call" | custom-call | flops 402653184 | bytes 2117632 | tf_op jit(solution)/shard_map/pallas_call | solution.py:62
  35.9 0.1 collective-permute-start.5
  36.0 3.9 %collective-permute-start.3 = (f32[2,8,128]{2,1,0:T(8,128)S(1)}, f32[2,8,128]{2,1,0:T(8,128)S(1)}, u32[]{:S(2)}, u32[]{:S(2)}) collective-permute-start(f32[2,8,128]{2,1,0:T(8,128)S(1)} %shard_map.69.final), channel_id=1, source_target_pairs={{0,63},{1,2},{2,1},{3,4},{4,3},{5,6},{6,5},{7,8},{8,7},{9,10},{10,... | collective-permute-start | bytes 24584 | tf_op jit(solution)/shard_map/ppermute | solution.py:46
  40.0 3.9 %shard_map.70 = (f32[8,128,256]{2,1,0:T(8,128)S(1)}, bf16[8,128,128]{2,1,0:T(8,128)(2,1)S(1)}) custom-call(bf16[8,2,128,256]{3,2,1,0:T(8,128)(2,1)S(1)} %all_to_all.10.tile, bf16[8,128,256]{2,1,0:T(8,128)(2,1)S(1)} %collective-permute-done.1.core, bf16[8,128,256]{2,1,0:T(8,128)(2,1)S(1)} %collective-permute-done.2.far, f32[2,8,128]{2,1,0:T(8,128)S(1)} %shard_map.69.final), custom_call_target="tpu_custom_call" | custom-call | flops 1107296256 | bytes 3416064 | tf_op jit(solution)/shard_map/pallas_call | solution.py:62
  43.9 0.0 collective-permute-done.4.side
  43.9 0.0 collective-permute-done.5.final
  43.9 1.3 %shard_map.71.before = f32[8,128,256]{2,1,0:T(8,128)S(1)} custom-call(bf16[8,2,128,256]{3,2,1,0:T(8,128)(2,1)S(1)} %all_to_all.10.tile, bf16[8,128,256]{2,1,0:T(8,128)(2,1)S(1)} %collective-permute-done.4.side, f32[2,8,128]{2,1,0:T(8,128)S(1)} %collective-permute-done.5.final, f32[8,128,256]{2,1,0:T(8,128)S(1)} %get-tuple-element.9.before), custom_call_target="tpu_custom_call" | custom-call | flops 402653184 | bytes 3678208 | tf_op jit(solution)/shard_map/pallas_call | solution.py:62
  45.2 0.0 collective-permute-done.side
  45.2 0.0 collective-permute-done.3.final
  45.2 1.3 %shard_map.72 = bf16[8,3,128,128]{3,2,1,0:T(8,128)(2,1)S(1)} custom-call(bf16[8,2,128,256]{3,2,1,0:T(8,128)(2,1)S(1)} %all_to_all.10.tile, bf16[8,128,256]{2,1,0:T(8,128)(2,1)S(1)} %collective-permute-done.side, f32[2,8,128]{2,1,0:T(8,128)S(1)} %collective-permute-done.3.final, f32[8,128,256]{2,1,0:T(8,128)S(1)} %shard_map.71.before, ...), custom_call_target="tpu_custom_call" | custom-call | flops 402653184 | bytes 3678208 | tf_op jit(solution)/shard_map/pallas_call | solution.py:62
  46.5 14.6 %all_to_all.11.tile = bf16[8,3,128,128]{3,2,1,0:T(8,128)(2,1)S(1)} all-to-all(bf16[8,3,128,128]{3,2,1,0:T(8,128)(2,1)S(1)} %shard_map.72), channel_id=1, replica_groups=mesh['x'=4,'l'=2,'h'=2,'z'=8,'c'=2] {'x','l'}, dimensions={0} | all-to-all | bytes 1572864 | tf_op jit(solution)/shard_map/all_to_all | solution.py:305
  61.1 1.1 %shard_map.73 = (bf16[1,128,1024]{2,1,0:T(8,128)(2,1)}, bf16[1,128,1024]{2,1,0:T(8,128)(2,1)}, bf16[1,128,1024]{2,1,0:T(8,128)(2,1)}) custom-call(s32[1]{0:T(128)} %bitcast.swap, bf16[8,3,128,128]{3,2,1,0:T(8,128)(2,1)S(1)} %all_to_all.11.tile), custom_call_target="tpu_custom_call" | custom-call | bytes 1572868 | tf_op jit(solution)/shard_map/pallas_call | solution.py:62
  (1 shorter events, 0.0 us)
Async XLA Ops:
  22.3 11.9 %collective-permute-start.2 = (bf16[8,128,256]{2,1,0:T(8,128)(2,1)S(1)}, bf16[8,128,256]{2,1,0:T(8,128)(2,1)S(1)}, u32[]{:S(2)}, u32[]{:S(2)}) collective-permute-start(bf16[8,128,256]{2,1,0:T(8,128)(2,1)S(1)} %slice_bitcast_fusion), channel_id=1, source_target_pairs={{0,63},{1,2},{2,1},{3,4},{4,3},{5,6},{6,5},{7,8},{8,7},{9,10},{10,... | collective-permute-start | bytes 1572872 | tf_op jit(solution)/shard_map/ppermute | solution.py:46
  27.3 6.9 %collective-permute-start.1 = (bf16[8,128,256]{2,1,0:T(8,128)(2,1)S(1)}, bf16[8,128,256]{2,1,0:T(8,128)(2,1)S(1)}, u32[]{:S(2)}, u32[]{:S(2)}) collective-permute-start(bf16[8,128,256]{2,1,0:T(8,128)(2,1)S(1)} %slice_bitcast_fusion), channel_id=1, source_target_pairs={{0,1},{1,0},{2,3},{3,2},{4,5},{5,4},{6,7},{7,6},{8,9},{9,8},{10,11... | collective-permute-start | bytes 1572872 | tf_op jit(solution)/shard_map/ppermute | solution.py:46
  28.3 15.6 %collective-permute-start.4 = (bf16[8,128,256]{2,1,0:T(8,128)(2,1)S(1)}, bf16[8,128,256]{2,1,0:T(8,128)(2,1)S(1)}, u32[]{:S(2)}, u32[]{:S(2)}) collective-permute-start(bf16[8,128,256]{2,1,0:T(8,128)(2,1)S(1)} %get-tuple-element.7), channel_id=1, source_target_pairs={{0,1},{1,0},{2,3},{3,2},{4,5},{5,4},{6,7},{7,6},{8,9},{9,8},{10,11... | collective-permute-start | bytes 1572872 | tf_op jit(solution)/shard_map/ppermute | solution.py:46
  28.9 16.3 %collective-permute-start = (bf16[8,128,256]{2,1,0:T(8,128)(2,1)S(1)}, bf16[8,128,256]{2,1,0:T(8,128)(2,1)S(1)}, u32[]{:S(2)}, u32[]{:S(2)}) collective-permute-start(bf16[8,128,256]{2,1,0:T(8,128)(2,1)S(1)} %get-tuple-element.7), channel_id=1, source_target_pairs={{0,63},{1,2},{2,1},{3,4},{4,3},{5,6},{6,5},{7,8},{8,7},{9,10},{10,... | collective-permute-start | bytes 1572872 | tf_op jit(solution)/shard_map/ppermute | solution.py:46
  35.9 8.0 %collective-permute-start.5 = (f32[2,8,128]{2,1,0:T(8,128)S(1)}, f32[2,8,128]{2,1,0:T(8,128)S(1)}, u32[]{:S(2)}, u32[]{:S(2)}) collective-permute-start(f32[2,8,128]{2,1,0:T(8,128)S(1)} %shard_map.69.final), channel_id=1, source_target_pairs={{0,1},{1,0},{2,3},{3,2},{4,5},{5,4},{6,7},{7,6},{8,9},{9,8},{10,11... | collective-permute-start | bytes 24584 | tf_op jit(solution)/shard_map/ppermute | solution.py:46
  36.0 9.2 %collective-permute-start.3 = (f32[2,8,128]{2,1,0:T(8,128)S(1)}, f32[2,8,128]{2,1,0:T(8,128)S(1)}, u32[]{:S(2)}, u32[]{:S(2)}) collective-permute-start(f32[2,8,128]{2,1,0:T(8,128)S(1)} %shard_map.69.final), channel_id=1, source_target_pairs={{0,63},{1,2},{2,1},{3,4},{4,3},{5,6},{6,5},{7,8},{8,7},{9,10},{10,... | collective-permute-start | bytes 24584 | tf_op jit(solution)/shard_map/ppermute | solution.py:46

commit v5 on v4

--- a/solution.py
+++ b/solution.py
@@ -143,17 +143,19 @@
     return top, total, delta
 
 
-def own_sums_kernel(tile, stats, queries, diag, kv_own):
+def own_sums_kernel(tile, stats, queries, diag, kv_own, kt_own):
     block_diagonal(lambda f: tile[f, 0], diag)
     wrap_frames(lambda f: tile[f, 1], kv_own)
+    for i in range(FRAMES + 2):
+        rows = slice(i * BLK, (i + 1) * BLK)
+        kt_own[:, rows] = kv_own[rows, :HD].T
     for f in range(FRAMES):
         queries[f] = tile[f, 0]
         for i, row in enumerate(column_sums((kv_own,), diag, f, None)):
             stats[i, f : f + 1, :] = row
 
 
-def side_sums_kernel(tile, core, far, before, final, diag, kv_far, kv_core):
-    block_diagonal(lambda f: tile[f, 0], diag)
+def side_sums_kernel(diag, far, core, before, final, kv_far, kv_core):
     wrap_frames(lambda f: far[f], kv_far)
     wrap_frames(lambda f: core[f], kv_core)
     for f in range(FRAMES):
@@ -184,49 +186,41 @@
     return got
 
 
-def own_queries_kernel(
-    tile, core, far, final, part, dq, diag, kv_own, kv_core, kv_far, kt, total
+def near_queries_kernel(
+    diag, kv_own, kt_own, core, far, final, side, side_final, part, dq,
+    side_diag, kv_core, kv_far, kt, total,
 ):
     columns = (kv_own, kv_core, kv_far)
-    block_diagonal(lambda f: tile[f, 0], diag)
-    wrap_frames(lambda f: tile[f, 1], kv_own)
+    block_diagonal(lambda f: side[f], side_diag)
     wrap_frames(lambda f: core[f], kv_core)
     wrap_frames(lambda f: far[f], kv_far)
-    for j, wrapped in enumerate(columns):
+    turned = (kt_own, kt.at[0], kt.at[1])
+    for keys, wrapped in zip(turned[1:], columns[1:]):
         for i in range(FRAMES + 2):
             rows = slice(i * BLK, (i + 1) * BLK)
-            kt[j, :, rows] = wrapped[rows, :HD].T
+            keys[:, rows] = wrapped[rows, :HD].T
     total[...] = jnp.zeros(total.shape, F32)
     for f in range(FRAMES):
         acc = None
         for j, wrapped in enumerate(columns):
             prob, dscore = prob_and_dscore(wrapped, diag, final, f)
-            one = dot_nn(kt[j, :, window(f)], dscore)
+            one = dot_nn(turned[j][:, window(f)], dscore)
             acc = one if acc is None else acc + one
             if j == 0:
                 add_key_grads(dscore, prob, diag, f, total)
         dq[f] = (acc * SCALE).T.astype(BF)
+        prob, dscore = prob_and_dscore(kv_own, side_diag, side_final, f)
+        add_key_grads(dscore, prob, side_diag, f, total)
     for u in range(FRAMES):
         part[u] = key_grads(total, u)
 
 
-def side_queries(tile, side, final, diag, kv_own, total):
+def far_queries_kernel(kv_own, side, final, before, dq, out, diag, total):
     block_diagonal(lambda f: side[f], diag)
-    wrap_frames(lambda f: tile[f, 1], kv_own)
     total[...] = jnp.zeros(total.shape, F32)
     for f in range(FRAMES):
         prob, dscore = prob_and_dscore(kv_own, diag, final, f)
         add_key_grads(dscore, prob, diag, f, total)
-
-
-def core_queries_kernel(tile, side, final, before, part, diag, kv_own, total):
-    side_queries(tile, side, final, diag, kv_own, total)
-    for u in range(FRAMES):
-        part[u] = before[u] + key_grads(total, u)
-
-
-def far_queries_kernel(tile, side, final, before, dq, out, diag, kv_own, total):
-    side_queries(tile, side, final, diag, kv_own, total)
     for u in range(FRAMES):
         both = before[u] + key_grads(total, u)
         out[u, 0] = dq[u]
@@ -256,11 +250,16 @@
     keys_values = tile[:, 1]
     far_keys = move(keys_values, OVER_Z)
     core_keys = move(keys_values, CORE)
-    sums, queries_grads = call(
+    sums, queries_grads, own_diag, own_wrap, own_kt = call(
         own_sums_kernel,
-        [shape((3, FRAMES, BLK), F32), shape(both, BF)],
+        [
+            shape((3, FRAMES, BLK), F32),
+            shape(both, BF),
+            shape((FRAMES, 2 * BLK, 2 * HD), BF),
+            shape(((FRAMES + 2) * BLK, 2 * HD), BF),
+            shape((HD, (FRAMES + 2) * BLK), BF),
+        ],
         (tile,),
-        scratch=(diag, wrapped),
         flops=2 * mats,
     )
     far_queries = move(queries_grads, OVER_Z)
@@ -268,38 +267,30 @@
     final = call(
         side_sums_kernel,
         [shape((2, FRAMES, BLK), F32)],
-        (tile, core_keys, far_keys, sums),
-        scratch=(diag, wrapped, wrapped),
+        (own_diag, far_keys, core_keys, sums),
+        scratch=(wrapped, wrapped),
         flops=4 * mats,
     )[0]
     far_final = move(final, OVER_Z)
     core_final = move(final, CORE)
-    own_part, dq = call(
-        own_queries_kernel,
+    part, dq = call(
+        near_queries_kernel,
         [shape(both, F32), shape((FRAMES, BLK, HD), BF)],
-        (tile, core_keys, far_keys, final),
+        (own_diag, own_wrap, own_kt, core_keys, far_keys, final, core_queries, core_final),
         scratch=(
             diag,
             wrapped,
             wrapped,
-            wrapped,
-            pltpu.VMEM((3, HD, (FRAMES + 2) * BLK), BF),
+            pltpu.VMEM((2, HD, (FRAMES + 2) * BLK), BF),
             summed,
         ),
-        flops=11 * mats,
+        flops=15 * mats,
     )
-    part = call(
-        core_queries_kernel,
-        [shape(both, F32)],
-        (tile, core_queries, core_final, own_part),
-        scratch=(diag, wrapped, summed),
-        flops=4 * mats,
-    )[0]
     grads = call(
         far_queries_kernel,
         [shape((FRAMES, 3, BLK, HD), BF)],
-        (tile, far_queries, far_final, part, dq),
-        scratch=(diag, wrapped, summed),
+        (own_wrap, far_queries, far_final, part, dq),
+        scratch=(diag, summed),
         flops=4 * mats,
     )[0]
     back = lax.all_to_all(grads, ("x", "l"), 0, 0)

time: 62.4 us -> 61.5 us (0.986)
  Pallas kernels: 11.7 us -> 10.9 us
    pallas_call x7 -> x6, Pallas kernels: 11.7 us -> 10.9 us  [call(): pl.pallas_call(kernel, out_shape=outs, in_specs=[SMEM] * smem + [space] *...]
  transfers between devices with their start and end apart: 6 -> 6, of which waited for: 1 -> 1; matrix products, arithmetic and copies ran while one was open for 0% -> 0% of each run, Pallas kernels for 13% -> 12%
where the time goes in v5:
time: 61.5 us; the launch traced here: 61.3 us
  blocking collectives  34.8 us (57%)
  starting transfers between devices  11.3 us (18%)
  Pallas kernels  10.9 us (18%)
  waiting for transfers between devices  3.6 us (6%)
  between operations  0.69 us (1%)
    all_to_all x1, blocking collectives, on_device(): tile = lax.all_to_all(packed, ('x', 'l'), 0, 0)  20.2 us
    all_to_all x1, blocking collectives, on_device(): back = lax.all_to_all(grads, ('x', 'l'), 0, 0)  14.5 us
    ppermute x6, starting transfers between devices, move(): return lax.ppermute(value, AXES, perm)  11.3 us
    pallas_call x6, Pallas kernels, call(): pl.pallas_call(kernel, out_shape=outs, in_specs=[SMEM] * smem + [space] *...  10.9 us
    ppermute x6, waiting for transfers between devices, move(): return lax.ppermute(value, AXES, perm)  3.6 us
  transfers between devices with their start and end apart: 6, of which 1 were waited for; matrix products, arithmetic and copies ran while one was open for 0% of the time, Pallas kernels for 12%

profile of v5, /device:TPU:8, one launch (start us, length us, event | category | flops | bytes accessed | tf_op | source)
XLA Modules:
  0.0 61.3 jit_solution(298353780774341320)
XLA Ops:
  0.6 1.4 %shard_map.67 = bf16[8,2,128,256]{3,2,1,0:T(8,128)(2,1)S(1)} custom-call(s32[1]{0:T(128)} %bitcast.swap, bf16[1,128,1024]{2,1,0:T(8,128)(2,1)} %q.1, bf16[1,128,1024]{2,1,0:T(8,128)(2,1)} %g.1, bf16[1,128,1024]{2,1,0:T(8,128)(2,1)} %k.1, bf16[1,128,1024]{2,1,0:T(8,128)(2,1)} %v.1), custom_call_target="tpu_custom_call" | custom-call | bytes 2097156 | tf_op jit(solution)/shard_map/pallas_call | solution.py:62
  2.0 20.2 %all_to_all.10.tile = bf16[8,2,128,256]{3,2,1,0:T(8,128)(2,1)S(1)} all-to-all(bf16[8,2,128,256]{3,2,1,0:T(8,128)(2,1)S(1)} %shard_map.67), channel_id=1, replica_groups=mesh['x'=4,'l'=2,'h'=2,'z'=8,'c'=2] {'x','l'}, dimensions={0} | all-to-all | bytes 2097152 | tf_op jit(solution)/shard_map/all_to_all | solution.py:249
  22.3 5.0 %collective-permute-start.1 = (bf16[8,128,256]{2,1,0:T(8,128)(2,1)S(1)}, bf16[8,128,256]{2,1,0:T(8,128)(2,1)S(1)}, u32[]{:S(2)}, u32[]{:S(2)}) collective-permute-start(bf16[8,128,256]{2,1,0:T(8,128)(2,1)S(1)} %slice_bitcast_fusion), channel_id=1, source_target_pairs={{0,63},{1,2},{2,1},{3,4},{4,3},{5,6},{6,5},{7,8},{8,7},{9,10},{10,... | collective-permute-start | bytes 1572872 | tf_op jit(solution)/shard_map/ppermute | solution.py:46
  27.3 0.0 collective-permute-start.2
  27.3 1.0 %shard_map.68 = (f32[3,8,128]{2,1,0:T(8,128)S(1)}, bf16[8,128,256]{2,1,0:T(8,128)(2,1)S(1)}, bf16[8,256,256]{2,1,0:T(8,128)(2,1)S(1)}, bf16[1280,256]{1,0:T(8,128)(2,1)S(1)}, bf16[128,1280]{1,0:T(8,128)(2,1)S(1)}) custom-call(bf16[8,2,128,256]{3,2,1,0:T(8,128)(2,1)S(1)} %all_to_all.10.tile), custom_call_target="tpu_custom_call" | custom-call | flops 201326592 | bytes 3616768 | tf_op jit(solution)/shard_map/pallas_call | solution.py:62
  28.3 0.6 collective-permute-start.4
  28.9 1.7 %collective-permute-start = (bf16[8,128,256]{2,1,0:T(8,128)(2,1)S(1)}, bf16[8,128,256]{2,1,0:T(8,128)(2,1)S(1)}, u32[]{:S(2)}, u32[]{:S(2)}) collective-permute-start(bf16[8,128,256]{2,1,0:T(8,128)(2,1)S(1)} %get-tuple-element.11), channel_id=1, source_target_pairs={{0,63},{1,2},{2,1},{3,4},{4,3},{5,6},{6,5},{7,8},{8,7},{9,10},{10,... | collective-permute-start | bytes 1572872 | tf_op jit(solution)/shard_map/ppermute | solution.py:46
  30.6 3.6 %collective-permute-done.1.far = bf16[8,128,256]{2,1,0:T(8,128)(2,1)S(1)} collective-permute-done((bf16[8,128,256]{2,1,0:T(8,128)(2,1)S(1)}, bf16[8,128,256]{2,1,0:T(8,128)(2,1)S(1)}, u32[]{:S(2)}, u32[]{:S(2)}) %collective-permute-start.1) | collective-permute-done | bytes 524320 | tf_op jit(solution)/shard_map/ppermute | solution.py:46
  34.2 0.0 collective-permute-done.2.core
  34.2 1.5 %shard_map.69.final = f32[2,8,128]{2,1,0:T(8,128)S(1)} custom-call(bf16[8,256,256]{2,1,0:T(8,128)(2,1)S(1)} %get-tuple-element.12.diag, bf16[8,128,256]{2,1,0:T(8,128)(2,1)S(1)} %collective-permute-done.1.far, bf16[8,128,256]{2,1,0:T(8,128)(2,1)S(1)} %collective-permute-done.2.core, f32[3,8,128]{2,1,0:T(8,128)S(1)} %get-tuple-element.13.before), custom_call_target="tpu_custom_call" | custom-call | flops 402653184 | bytes 2117632 | tf_op jit(solution)/shard_map/pallas_call | solution.py:62
  35.7 0.1 collective-permute-start.5
  35.8 4.0 %collective-permute-start.3 = (f32[2,8,128]{2,1,0:T(8,128)S(1)}, f32[2,8,128]{2,1,0:T(8,128)S(1)}, u32[]{:S(2)}, u32[]{:S(2)}) collective-permute-start(f32[2,8,128]{2,1,0:T(8,128)S(1)} %shard_map.69.final), channel_id=1, source_target_pairs={{0,63},{1,2},{2,1},{3,4},{4,3},{5,6},{6,5},{7,8},{8,7},{9,10},{10,... | collective-permute-start | bytes 24584 | tf_op jit(solution)/shard_map/ppermute | solution.py:46
  39.7 0.0 collective-permute-done.4.side
  39.7 0.0 collective-permute-done.5.side_final
  39.8 4.6 %shard_map.70 = (f32[8,128,256]{2,1,0:T(8,128)S(1)}, bf16[8,128,128]{2,1,0:T(8,128)(2,1)S(1)}) custom-call(bf16[8,256,256]{2,1,0:T(8,128)(2,1)S(1)} %get-tuple-element.12.diag, bf16[1280,256]{1,0:T(8,128)(2,1)S(1)} %get-tuple-element.10.kv_own, bf16[128,1280]{1,0:T(8,128)(2,1)S(1)} %get-tuple-element.14.kt_own, ...), custom_call_target="tpu_custom_call" | custom-call | flops 1509949440 | bytes 4931584 | tf_op jit(solution)/shard_map/pallas_call | solution.py:62
  44.4 0.0 collective-permute-done.side
  44.4 0.0 collective-permute-done.3.final
  44.4 1.3 %shard_map.71 = bf16[8,3,128,128]{3,2,1,0:T(8,128)(2,1)S(1)} custom-call(bf16[1280,256]{1,0:T(8,128)(2,1)S(1)} %get-tuple-element.10.kv_own, bf16[8,128,256]{2,1,0:T(8,128)(2,1)S(1)} %collective-permute-done.side, f32[2,8,128]{2,1,0:T(8,128)S(1)} %collective-permute-done.3.final, f32[8,128,256]{2,1,0:T(8,128)S(1)} %get-tuple-element.15.before, ...), custom_call_target="tpu_custom_call" | custom-call | flops 402653184 | bytes 3284992 | tf_op jit(solution)/shard_map/pallas_call | solution.py:62
  45.7 14.5 %all_to_all.11.tile = bf16[8,3,128,128]{3,2,1,0:T(8,128)(2,1)S(1)} all-to-all(bf16[8,3,128,128]{3,2,1,0:T(8,128)(2,1)S(1)} %shard_map.71), channel_id=1, replica_groups=mesh['x'=4,'l'=2,'h'=2,'z'=8,'c'=2] {'x','l'}, dimensions={0} | all-to-all | bytes 1572864 | tf_op jit(solution)/shard_map/all_to_all | solution.py:296
  60.2 1.1 %shard_map.72 = (bf16[1,128,1024]{2,1,0:T(8,128)(2,1)}, bf16[1,128,1024]{2,1,0:T(8,128)(2,1)}, bf16[1,128,1024]{2,1,0:T(8,128)(2,1)}) custom-call(s32[1]{0:T(128)} %bitcast.swap, bf16[8,3,128,128]{3,2,1,0:T(8,128)(2,1)S(1)} %all_to_all.11.tile), custom_call_target="tpu_custom_call" | custom-call | bytes 1572868 | tf_op jit(solution)/shard_map/pallas_call | solution.py:62
  (1 shorter events, 0.0 us)
Async XLA Ops:
  22.3 11.9 %collective-permute-start.1 = (bf16[8,128,256]{2,1,0:T(8,128)(2,1)S(1)}, bf16[8,128,256]{2,1,0:T(8,128)(2,1)S(1)}, u32[]{:S(2)}, u32[]{:S(2)}) collective-permute-start(bf16[8,128,256]{2,1,0:T(8,128)(2,1)S(1)} %slice_bitcast_fusion), channel_id=1, source_target_pairs={{0,63},{1,2},{2,1},{3,4},{4,3},{5,6},{6,5},{7,8},{8,7},{9,10},{10,... | collective-permute-start | bytes 1572872 | tf_op jit(solution)/shard_map/ppermute | solution.py:46
  27.3 6.9 %collective-permute-start.2 = (bf16[8,128,256]{2,1,0:T(8,128)(2,1)S(1)}, bf16[8,128,256]{2,1,0:T(8,128)(2,1)S(1)}, u32[]{:S(2)}, u32[]{:S(2)}) collective-permute-start(bf16[8,128,256]{2,1,0:T(8,128)(2,1)S(1)} %slice_bitcast_fusion), channel_id=1, source_target_pairs={{0,1},{1,0},{2,3},{3,2},{4,5},{5,4},{6,7},{7,6},{8,9},{9,8},{10,11... | collective-permute-start | bytes 1572872 | tf_op jit(solution)/shard_map/ppermute | solution.py:46
  28.3 11.4 %collective-permute-start.4 = (bf16[8,128,256]{2,1,0:T(8,128)(2,1)S(1)}, bf16[8,128,256]{2,1,0:T(8,128)(2,1)S(1)}, u32[]{:S(2)}, u32[]{:S(2)}) collective-permute-start(bf16[8,128,256]{2,1,0:T(8,128)(2,1)S(1)} %get-tuple-element.11), channel_id=1, source_target_pairs={{0,1},{1,0},{2,3},{3,2},{4,5},{5,4},{6,7},{7,6},{8,9},{9,8},{10,11... | collective-permute-start | bytes 1572872 | tf_op jit(solution)/shard_map/ppermute | solution.py:46
  28.9 15.5 %collective-permute-start = (bf16[8,128,256]{2,1,0:T(8,128)(2,1)S(1)}, bf16[8,128,256]{2,1,0:T(8,128)(2,1)S(1)}, u32[]{:S(2)}, u32[]{:S(2)}) collective-permute-start(bf16[8,128,256]{2,1,0:T(8,128)(2,1)S(1)} %get-tuple-element.11), channel_id=1, source_target_pairs={{0,63},{1,2},{2,1},{3,4},{4,3},{5,6},{6,5},{7,8},{8,7},{9,10},{10,... | collective-permute-start | bytes 1572872 | tf_op jit(solution)/shard_map/ppermute | solution.py:46
  35.7 4.1 %collective-permute-start.5 = (f32[2,8,128]{2,1,0:T(8,128)S(1)}, f32[2,8,128]{2,1,0:T(8,128)S(1)}, u32[]{:S(2)}, u32[]{:S(2)}) collective-permute-start(f32[2,8,128]{2,1,0:T(8,128)S(1)} %shard_map.69.final), channel_id=1, source_target_pairs={{0,1},{1,0},{2,3},{3,2},{4,5},{5,4},{6,7},{7,6},{8,9},{9,8},{10,11... | collective-permute-start | bytes 24584 | tf_op jit(solution)/shard_map/ppermute | solution.py:46
  35.8 8.6 %collective-permute-start.3 = (f32[2,8,128]{2,1,0:T(8,128)S(1)}, f32[2,8,128]{2,1,0:T(8,128)S(1)}, u32[]{:S(2)}, u32[]{:S(2)}) collective-permute-start(f32[2,8,128]{2,1,0:T(8,128)S(1)} %shard_map.69.final), channel_id=1, source_target_pairs={{0,63},{1,2},{2,1},{3,4},{4,3},{5,6},{6,5},{7,8},{8,7},{9,10},{10,... | collective-permute-start | bytes 24584 | tf_op jit(solution)/shard_map/ppermute | solution.py:46

commit v6 on v5

--- a/solution.py
+++ b/solution.py
@@ -58,12 +58,12 @@
     return sum(math.prod(s.shape) * s.dtype.itemsize for s in shapes)
 
 
-def call(kernel, outs, args, scratch=(), smem=0, flops=0, space=VMEM, limit=32):
+def call(kernel, outs, args, scratch=(), smem=0, flops=0, space=VMEM, limit=32, out_space=VMEM):
     return pl.pallas_call(
         kernel,
         out_shape=outs,
         in_specs=[SMEM] * smem + [space] * (len(args) - smem),
-        out_specs=[VMEM] * len(outs),
+        out_specs=[out_space] * len(outs),
         scratch_shapes=list(scratch),
         compiler_params=pltpu.CompilerParams(vmem_limit_bytes=limit * 1024 * 1024 if limit else None),
         cost_estimate=pl.CostEstimate(
@@ -92,10 +92,23 @@
             ]
 
 
-def unpack_kernel(swap, tile, dq, dk, dv):
+def unpack_kernel(swap, tile, dq, dk, dv, held, sems):
+    step = BLK // 4
+    copies = []
     for place, ref in enumerate((dq, dk, dv)):
-        for head in range(FRAMES):
-            ref[0, :, head * HD : (head + 1) * HD] = tile[head ^ swap[0], place]
+        for part in range(4):
+            rows = slice(part * step, (part + 1) * step)
+            for head in range(FRAMES):
+                lanes = slice(head * HD, (head + 1) * HD)
+                held[place, rows, lanes] = tile[head ^ swap[0], place, rows]
+            span = pl.ds(part * step, step)
+            copy = pltpu.make_async_copy(
+                held.at[place, span], ref.at[0, span], sems.at[place, part]
+            )
+            copy.start()
+            copies.append(copy)
+    for copy in copies:
+        copy.wait()
 
 
 def block_diagonal(read, diag):
@@ -120,27 +133,20 @@
 
 
 def column_sums(columns, diag, f, before):
-    both = [dot_nt(wrapped[window(f), :], diag[f]) for wrapped in columns]
-    top8 = None
-    for x in both:
-        one = jnp.max(fold(x[:, :BLK]), axis=0)
-        top8 = one if top8 is None else jnp.maximum(top8, one)
-    top = jnp.max(top8, axis=0, keepdims=True) * EXP_SCALE
-    if before is not None:
-        top = jnp.maximum(top, before[0])
-    total8 = jnp.zeros((8, BLK), F32)
-    delta8 = jnp.zeros((8, BLK), F32)
-    for x in both:
+    for wrapped in columns:
+        x = dot_nt(wrapped[window(f), :], diag[f])
+        top = jnp.max(jnp.max(fold(x[:, :BLK]), axis=0), axis=0, keepdims=True) * EXP_SCALE
+        if before is not None:
+            top = jnp.maximum(top, before[0])
         e = jnp.exp2(x[:, :BLK] * EXP_SCALE - top)
-        total8 = total8 + jnp.sum(fold(e), axis=0)
-        delta8 = delta8 + jnp.sum(fold(e * x[:, BLK:]), axis=0)
-    total = jnp.sum(total8, axis=0, keepdims=True)
-    delta = jnp.sum(delta8, axis=0, keepdims=True)
-    if before is not None:
-        shrink = jnp.exp2(before[0] - top)
-        total = total + before[1] * shrink
-        delta = delta + before[2] * shrink
-    return top, total, delta
+        total = jnp.sum(jnp.sum(fold(e), axis=0), axis=0, keepdims=True)
+        delta = jnp.sum(jnp.sum(fold(e * x[:, BLK:]), axis=0), axis=0, keepdims=True)
+        if before is not None:
+            shrink = jnp.exp2(before[0] - top)
+            total = total + before[1] * shrink
+            delta = delta + before[2] * shrink
+        before = (top, total, delta)
+    return before
 
 
 def own_sums_kernel(tile, stats, queries, diag, kv_own, kt_own):
@@ -295,7 +301,16 @@
     )[0]
     back = lax.all_to_all(grads, ("x", "l"), 0, 0)
     flat = shape((1, BLK, FRAMES * HD), BF)
-    return tuple(call(unpack_kernel, [flat] * 3, (swap, back), smem=1))
+    return tuple(
+        call(
+            unpack_kernel,
+            [flat] * 3,
+            (swap, back),
+            scratch=(pltpu.VMEM((3, BLK, FRAMES * HD), BF), pltpu.SemaphoreType.DMA((3, 4))),
+            smem=1,
+            out_space=HBM,
+        )
+    )
 
 
 def solution(mesh):

time: 61.5 us -> 61.3 us (level)
  no operation moved by 1% of the time
where the time goes in v6:
time: 61.3 us; the launch traced here: 61.1 us
  blocking collectives  34.8 us (57%)
  starting transfers between devices  11.3 us (18%)
  Pallas kernels  10.7 us (17%)
  waiting for transfers between devices  3.6 us (6%)
  between operations  0.7 us (1%)
    all_to_all x1, blocking collectives, on_device(): tile = lax.all_to_all(packed, ('x', 'l'), 0, 0)  20.2 us
    all_to_all x1, blocking collectives, on_device(): back = lax.all_to_all(grads, ('x', 'l'), 0, 0)  14.6 us
    ppermute x6, starting transfers between devices, move(): return lax.ppermute(value, AXES, perm)  11.3 us
    pallas_call x6, Pallas kernels, call(): pl.pallas_call(kernel, out_shape=outs, in_specs=[SMEM] * smem + [space] *...  10.7 us
    ppermute x6, waiting for transfers between devices, move(): return lax.ppermute(value, AXES, perm)  3.6 us
  transfers between devices with their start and end apart: 6, of which 1 were waited for; matrix products, arithmetic and copies ran while one was open for 0% of the time, Pallas kernels for 12%

profile of v6, /device:TPU:8, one launch (start us, length us, event | category | flops | bytes accessed | tf_op | source)
XLA Modules:
  0.0 61.1 jit_solution(4107357529382055563)
XLA Ops:
  0.6 1.4 %shard_map.67 = bf16[8,2,128,256]{3,2,1,0:T(8,128)(2,1)S(1)} custom-call(s32[1]{0:T(128)} %bitcast.swap, bf16[1,128,1024]{2,1,0:T(8,128)(2,1)} %q.1, bf16[1,128,1024]{2,1,0:T(8,128)(2,1)} %g.1, bf16[1,128,1024]{2,1,0:T(8,128)(2,1)} %k.1, bf16[1,128,1024]{2,1,0:T(8,128)(2,1)} %v.1), custom_call_target="tpu_custom_call" | custom-call | bytes 2097156 | tf_op jit(solution)/shard_map/pallas_call | solution.py:62
  2.0 20.2 %all_to_all.10.tile = bf16[8,2,128,256]{3,2,1,0:T(8,128)(2,1)S(1)} all-to-all(bf16[8,2,128,256]{3,2,1,0:T(8,128)(2,1)S(1)} %shard_map.67), channel_id=1, replica_groups=mesh['x'=4,'l'=2,'h'=2,'z'=8,'c'=2] {'x','l'}, dimensions={0} | all-to-all | bytes 2097152 | tf_op jit(solution)/shard_map/all_to_all | solution.py:255
  22.3 5.0 %collective-permute-start.1 = (bf16[8,128,256]{2,1,0:T(8,128)(2,1)S(1)}, bf16[8,128,256]{2,1,0:T(8,128)(2,1)S(1)}, u32[]{:S(2)}, u32[]{:S(2)}) collective-permute-start(bf16[8,128,256]{2,1,0:T(8,128)(2,1)S(1)} %slice_bitcast_fusion), channel_id=1, source_target_pairs={{0,63},{1,2},{2,1},{3,4},{4,3},{5,6},{6,5},{7,8},{8,7},{9,10},{10,... | collective-permute-start | bytes 1572872 | tf_op jit(solution)/shard_map/ppermute | solution.py:46
  27.3 0.0 collective-permute-start.2
  27.3 1.0 %shard_map.68 = (f32[3,8,128]{2,1,0:T(8,128)S(1)}, bf16[8,128,256]{2,1,0:T(8,128)(2,1)S(1)}, bf16[8,256,256]{2,1,0:T(8,128)(2,1)S(1)}, bf16[1280,256]{1,0:T(8,128)(2,1)S(1)}, bf16[128,1280]{1,0:T(8,128)(2,1)S(1)}) custom-call(bf16[8,2,128,256]{3,2,1,0:T(8,128)(2,1)S(1)} %all_to_all.10.tile), custom_call_target="tpu_custom_call" | custom-call | flops 201326592 | bytes 3616768 | tf_op jit(solution)/shard_map/pallas_call | solution.py:62
  28.3 0.6 collective-permute-start.4
  28.9 1.7 %collective-permute-start = (bf16[8,128,256]{2,1,0:T(8,128)(2,1)S(1)}, bf16[8,128,256]{2,1,0:T(8,128)(2,1)S(1)}, u32[]{:S(2)}, u32[]{:S(2)}) collective-permute-start(bf16[8,128,256]{2,1,0:T(8,128)(2,1)S(1)} %get-tuple-element.11), channel_id=1, source_target_pairs={{0,63},{1,2},{2,1},{3,4},{4,3},{5,6},{6,5},{7,8},{8,7},{9,10},{10,... | collective-permute-start | bytes 1572872 | tf_op jit(solution)/shard_map/ppermute | solution.py:46
  30.6 3.6 %collective-permute-done.1.far = bf16[8,128,256]{2,1,0:T(8,128)(2,1)S(1)} collective-permute-done((bf16[8,128,256]{2,1,0:T(8,128)(2,1)S(1)}, bf16[8,128,256]{2,1,0:T(8,128)(2,1)S(1)}, u32[]{:S(2)}, u32[]{:S(2)}) %collective-permute-start.1) | collective-permute-done | bytes 524320 | tf_op jit(solution)/shard_map/ppermute | solution.py:46
  34.2 0.0 collective-permute-done.2.core
  34.2 1.4 %shard_map.69.final = f32[2,8,128]{2,1,0:T(8,128)S(1)} custom-call(bf16[8,256,256]{2,1,0:T(8,128)(2,1)S(1)} %get-tuple-element.12.diag, bf16[8,128,256]{2,1,0:T(8,128)(2,1)S(1)} %collective-permute-done.1.far, bf16[8,128,256]{2,1,0:T(8,128)(2,1)S(1)} %collective-permute-done.2.core, f32[3,8,128]{2,1,0:T(8,128)S(1)} %get-tuple-element.13.before), custom_call_target="tpu_custom_call" | custom-call | flops 402653184 | bytes 2117632 | tf_op jit(solution)/shard_map/pallas_call | solution.py:62
  35.6 0.1 collective-permute-start.5
  35.7 3.9 %collective-permute-start.3 = (f32[2,8,128]{2,1,0:T(8,128)S(1)}, f32[2,8,128]{2,1,0:T(8,128)S(1)}, u32[]{:S(2)}, u32[]{:S(2)}) collective-permute-start(f32[2,8,128]{2,1,0:T(8,128)S(1)} %shard_map.69.final), channel_id=1, source_target_pairs={{0,63},{1,2},{2,1},{3,4},{4,3},{5,6},{6,5},{7,8},{8,7},{9,10},{10,... | collective-permute-start | bytes 24584 | tf_op jit(solution)/shard_map/ppermute | solution.py:46
  39.6 0.0 collective-permute-done.4.side
  39.6 0.0 collective-permute-done.5.side_final
  39.6 4.6 %shard_map.70 = (f32[8,128,256]{2,1,0:T(8,128)S(1)}, bf16[8,128,128]{2,1,0:T(8,128)(2,1)S(1)}) custom-call(bf16[8,256,256]{2,1,0:T(8,128)(2,1)S(1)} %get-tuple-element.12.diag, bf16[1280,256]{1,0:T(8,128)(2,1)S(1)} %get-tuple-element.10.kv_own, bf16[128,1280]{1,0:T(8,128)(2,1)S(1)} %get-tuple-element.14.kt_own, ...), custom_call_target="tpu_custom_call" | custom-call | flops 1509949440 | bytes 4931584 | tf_op jit(solution)/shard_map/pallas_call | solution.py:62
  44.3 0.0 collective-permute-done.side
  44.3 0.0 collective-permute-done.3.final
  44.3 1.3 %shard_map.71 = bf16[8,3,128,128]{3,2,1,0:T(8,128)(2,1)S(1)} custom-call(bf16[1280,256]{1,0:T(8,128)(2,1)S(1)} %get-tuple-element.10.kv_own, bf16[8,128,256]{2,1,0:T(8,128)(2,1)S(1)} %collective-permute-done.side, f32[2,8,128]{2,1,0:T(8,128)S(1)} %collective-permute-done.3.final, f32[8,128,256]{2,1,0:T(8,128)S(1)} %get-tuple-element.15.before, ...), custom_call_target="tpu_custom_call" | custom-call | flops 402653184 | bytes 3284992 | tf_op jit(solution)/shard_map/pallas_call | solution.py:62
  45.6 14.6 %all_to_all.11.tile = bf16[8,3,128,128]{3,2,1,0:T(8,128)(2,1)S(1)} all-to-all(bf16[8,3,128,128]{3,2,1,0:T(8,128)(2,1)S(1)} %shard_map.71), channel_id=1, replica_groups=mesh['x'=4,'l'=2,'h'=2,'z'=8,'c'=2] {'x','l'}, dimensions={0} | all-to-all | bytes 1572864 | tf_op jit(solution)/shard_map/all_to_all | solution.py:302
  60.1 1.0 %shard_map.72 = (bf16[1,128,1024]{2,1,0:T(8,128)(2,1)}, bf16[1,128,1024]{2,1,0:T(8,128)(2,1)}, bf16[1,128,1024]{2,1,0:T(8,128)(2,1)}) custom-call(s32[1]{0:T(128)} %bitcast.swap, bf16[8,3,128,128]{3,2,1,0:T(8,128)(2,1)S(1)} %all_to_all.11.tile), custom_call_target="tpu_custom_call" | custom-call | bytes 1572868 | tf_op jit(solution)/shard_map/pallas_call | solution.py:62
  (1 shorter events, 0.0 us)
Async XLA Ops:
  22.3 11.9 %collective-permute-start.1 = (bf16[8,128,256]{2,1,0:T(8,128)(2,1)S(1)}, bf16[8,128,256]{2,1,0:T(8,128)(2,1)S(1)}, u32[]{:S(2)}, u32[]{:S(2)}) collective-permute-start(bf16[8,128,256]{2,1,0:T(8,128)(2,1)S(1)} %slice_bitcast_fusion), channel_id=1, source_target_pairs={{0,63},{1,2},{2,1},{3,4},{4,3},{5,6},{6,5},{7,8},{8,7},{9,10},{10,... | collective-permute-start | bytes 1572872 | tf_op jit(solution)/shard_map/ppermute | solution.py:46
  27.3 6.9 %collective-permute-start.2 = (bf16[8,128,256]{2,1,0:T(8,128)(2,1)S(1)}, bf16[8,128,256]{2,1,0:T(8,128)(2,1)S(1)}, u32[]{:S(2)}, u32[]{:S(2)}) collective-permute-start(bf16[8,128,256]{2,1,0:T(8,128)(2,1)S(1)} %slice_bitcast_fusion), channel_id=1, source_target_pairs={{0,1},{1,0},{2,3},{3,2},{4,5},{5,4},{6,7},{7,6},{8,9},{9,8},{10,11... | collective-permute-start | bytes 1572872 | tf_op jit(solution)/shard_map/ppermute | solution.py:46
  28.3 11.3 %collective-permute-start.4 = (bf16[8,128,256]{2,1,0:T(8,128)(2,1)S(1)}, bf16[8,128,256]{2,1,0:T(8,128)(2,1)S(1)}, u32[]{:S(2)}, u32[]{:S(2)}) collective-permute-start(bf16[8,128,256]{2,1,0:T(8,128)(2,1)S(1)} %get-tuple-element.11), channel_id=1, source_target_pairs={{0,1},{1,0},{2,3},{3,2},{4,5},{5,4},{6,7},{7,6},{8,9},{9,8},{10,11... | collective-permute-start | bytes 1572872 | tf_op jit(solution)/shard_map/ppermute | solution.py:46
  28.9 15.4 %collective-permute-start = (bf16[8,128,256]{2,1,0:T(8,128)(2,1)S(1)}, bf16[8,128,256]{2,1,0:T(8,128)(2,1)S(1)}, u32[]{:S(2)}, u32[]{:S(2)}) collective-permute-start(bf16[8,128,256]{2,1,0:T(8,128)(2,1)S(1)} %get-tuple-element.11), channel_id=1, source_target_pairs={{0,63},{1,2},{2,1},{3,4},{4,3},{5,6},{6,5},{7,8},{8,7},{9,10},{10,... | collective-permute-start | bytes 1572872 | tf_op jit(solution)/shard_map/ppermute | solution.py:46
  35.6 4.1 %collective-permute-start.5 = (f32[2,8,128]{2,1,0:T(8,128)S(1)}, f32[2,8,128]{2,1,0:T(8,128)S(1)}, u32[]{:S(2)}, u32[]{:S(2)}) collective-permute-start(f32[2,8,128]{2,1,0:T(8,128)S(1)} %shard_map.69.final), channel_id=1, source_target_pairs={{0,1},{1,0},{2,3},{3,2},{4,5},{5,4},{6,7},{7,6},{8,9},{9,8},{10,11... | collective-permute-start | bytes 24584 | tf_op jit(solution)/shard_map/ppermute | solution.py:46
  35.7 8.6 %collective-permute-start.3 = (f32[2,8,128]{2,1,0:T(8,128)S(1)}, f32[2,8,128]{2,1,0:T(8,128)S(1)}, u32[]{:S(2)}, u32[]{:S(2)}) collective-permute-start(f32[2,8,128]{2,1,0:T(8,128)S(1)} %shard_map.69.final), channel_id=1, source_target_pairs={{0,63},{1,2},{2,1},{3,4},{4,3},{5,6},{6,5},{7,8},{8,7},{9,10},{10,... | collective-permute-start | bytes 24584 | tf_op jit(solution)/shard_map/ppermute | solution.py:46

commit v7 on v6

--- a/solution.py
+++ b/solution.py
@@ -178,9 +178,14 @@
     return prob.astype(BF), dscore.astype(BF)
 
 
-def add_key_grads(dscore, prob, diag, f, total):
-    both = jnp.concatenate([dscore, prob], axis=1)
-    total[window(f), :] += dot_nn(both, diag[f])
+def add_key_grads(dscore, prob, diag, f, total, fresh):
+    got = dot_nn(jnp.concatenate([dscore, prob], axis=1), diag[f])
+    old = 0 if fresh and f == 0 else 2 * BLK if fresh else WIN
+    start = f * BLK
+    if old:
+        total[start : start + old, :] += got[:old, :]
+    if old < WIN:
+        total[start + old : start + WIN, :] = got[old:, :]
 
 
 def key_grads(total, u):
@@ -205,7 +210,6 @@
         for i in range(FRAMES + 2):
             rows = slice(i * BLK, (i + 1) * BLK)
             keys[:, rows] = wrapped[rows, :HD].T
-    total[...] = jnp.zeros(total.shape, F32)
     for f in range(FRAMES):
         acc = None
         for j, wrapped in enumerate(columns):
@@ -213,20 +217,19 @@
             one = dot_nn(turned[j][:, window(f)], dscore)
             acc = one if acc is None else acc + one
             if j == 0:
-                add_key_grads(dscore, prob, diag, f, total)
+                add_key_grads(dscore, prob, diag, f, total, True)
         dq[f] = (acc * SCALE).T.astype(BF)
         prob, dscore = prob_and_dscore(kv_own, side_diag, side_final, f)
-        add_key_grads(dscore, prob, side_diag, f, total)
+        add_key_grads(dscore, prob, side_diag, f, total, False)
     for u in range(FRAMES):
         part[u] = key_grads(total, u)
 
 
 def far_queries_kernel(kv_own, side, final, before, dq, out, diag, total):
     block_diagonal(lambda f: side[f], diag)
-    total[...] = jnp.zeros(total.shape, F32)
     for f in range(FRAMES):
         prob, dscore = prob_and_dscore(kv_own, diag, final, f)
-        add_key_grads(dscore, prob, diag, f, total)
+        add_key_grads(dscore, prob, diag, f, total, True)
     for u in range(FRAMES):
         both = before[u] + key_grads(total, u)
         out[u, 0] = dq[u]

time: 61.3 us -> 61.3 us (level)
  no operation moved by 1% of the time
where the time goes in v7:
time: 61.3 us; the launch traced here: 61.1 us
  blocking collectives  34.8 us (57%)
  starting transfers between devices  11.3 us (18%)
  Pallas kernels  10.7 us (17%)
  waiting for transfers between devices  3.6 us (6%)
  between operations  0.7 us (1%)
    all_to_all x1, blocking collectives, on_device(): tile = lax.all_to_all(packed, ('x', 'l'), 0, 0)  20.2 us
    all_to_all x1, blocking collectives, on_device(): back = lax.all_to_all(grads, ('x', 'l'), 0, 0)  14.6 us
    ppermute x6, starting transfers between devices, move(): return lax.ppermute(value, AXES, perm)  11.3 us
    pallas_call x6, Pallas kernels, call(): pl.pallas_call(kernel, out_shape=outs, in_specs=[SMEM] * smem + [space] *...  10.7 us
    ppermute x6, waiting for transfers between devices, move(): return lax.ppermute(value, AXES, perm)  3.6 us
  transfers between devices with their start and end apart: 6, of which 1 were waited for; matrix products, arithmetic and copies ran while one was open for 0% of the time, Pallas kernels for 12%

profile of v7, /device:TPU:8, one launch (start us, length us, event | category | flops | bytes accessed | tf_op | source)
XLA Modules:
  0.0 61.1 jit_solution(4107357529382055563)
XLA Ops:
  0.6 1.4 %shard_map.67 = bf16[8,2,128,256]{3,2,1,0:T(8,128)(2,1)S(1)} custom-call(s32[1]{0:T(128)} %bitcast.swap, bf16[1,128,1024]{2,1,0:T(8,128)(2,1)} %q.1, bf16[1,128,1024]{2,1,0:T(8,128)(2,1)} %g.1, bf16[1,128,1024]{2,1,0:T(8,128)(2,1)} %k.1, bf16[1,128,1024]{2,1,0:T(8,128)(2,1)} %v.1), custom_call_target="tpu_custom_call" | custom-call | bytes 2097156 | tf_op jit(solution)/shard_map/pallas_call | solution.py:62
  2.0 20.2 %all_to_all.10.tile = bf16[8,2,128,256]{3,2,1,0:T(8,128)(2,1)S(1)} all-to-all(bf16[8,2,128,256]{3,2,1,0:T(8,128)(2,1)S(1)} %shard_map.67), channel_id=1, replica_groups=mesh['x'=4,'l'=2,'h'=2,'z'=8,'c'=2] {'x','l'}, dimensions={0} | all-to-all | bytes 2097152 | tf_op jit(solution)/shard_map/all_to_all | solution.py:258
  22.3 5.0 %collective-permute-start.1 = (bf16[8,128,256]{2,1,0:T(8,128)(2,1)S(1)}, bf16[8,128,256]{2,1,0:T(8,128)(2,1)S(1)}, u32[]{:S(2)}, u32[]{:S(2)}) collective-permute-start(bf16[8,128,256]{2,1,0:T(8,128)(2,1)S(1)} %slice_bitcast_fusion), channel_id=1, source_target_pairs={{0,63},{1,2},{2,1},{3,4},{4,3},{5,6},{6,5},{7,8},{8,7},{9,10},{10,... | collective-permute-start | bytes 1572872 | tf_op jit(solution)/shard_map/ppermute | solution.py:46
  27.3 0.0 collective-permute-start.2
  27.3 1.0 %shard_map.68 = (f32[3,8,128]{2,1,0:T(8,128)S(1)}, bf16[8,128,256]{2,1,0:T(8,128)(2,1)S(1)}, bf16[8,256,256]{2,1,0:T(8,128)(2,1)S(1)}, bf16[1280,256]{1,0:T(8,128)(2,1)S(1)}, bf16[128,1280]{1,0:T(8,128)(2,1)S(1)}) custom-call(bf16[8,2,128,256]{3,2,1,0:T(8,128)(2,1)S(1)} %all_to_all.10.tile), custom_call_target="tpu_custom_call" | custom-call | flops 201326592 | bytes 3616768 | tf_op jit(solution)/shard_map/pallas_call | solution.py:62
  28.3 0.6 collective-permute-start.4
  28.9 1.7 %collective-permute-start = (bf16[8,128,256]{2,1,0:T(8,128)(2,1)S(1)}, bf16[8,128,256]{2,1,0:T(8,128)(2,1)S(1)}, u32[]{:S(2)}, u32[]{:S(2)}) collective-permute-start(bf16[8,128,256]{2,1,0:T(8,128)(2,1)S(1)} %get-tuple-element.11), channel_id=1, source_target_pairs={{0,63},{1,2},{2,1},{3,4},{4,3},{5,6},{6,5},{7,8},{8,7},{9,10},{10,... | collective-permute-start | bytes 1572872 | tf_op jit(solution)/shard_map/ppermute | solution.py:46
  30.6 3.6 %collective-permute-done.1.far = bf16[8,128,256]{2,1,0:T(8,128)(2,1)S(1)} collective-permute-done((bf16[8,128,256]{2,1,0:T(8,128)(2,1)S(1)}, bf16[8,128,256]{2,1,0:T(8,128)(2,1)S(1)}, u32[]{:S(2)}, u32[]{:S(2)}) %collective-permute-start.1) | collective-permute-done | bytes 524320 | tf_op jit(solution)/shard_map/ppermute | solution.py:46
  34.2 0.0 collective-permute-done.2.core
  34.2 1.4 %shard_map.69.final = f32[2,8,128]{2,1,0:T(8,128)S(1)} custom-call(bf16[8,256,256]{2,1,0:T(8,128)(2,1)S(1)} %get-tuple-element.12.diag, bf16[8,128,256]{2,1,0:T(8,128)(2,1)S(1)} %collective-permute-done.1.far, bf16[8,128,256]{2,1,0:T(8,128)(2,1)S(1)} %collective-permute-done.2.core, f32[3,8,128]{2,1,0:T(8,128)S(1)} %get-tuple-element.13.before), custom_call_target="tpu_custom_call" | custom-call | flops 402653184 | bytes 2117632 | tf_op jit(solution)/shard_map/pallas_call | solution.py:62
  35.6 0.1 collective-permute-start.5
  35.7 3.9 %collective-permute-start.3 = (f32[2,8,128]{2,1,0:T(8,128)S(1)}, f32[2,8,128]{2,1,0:T(8,128)S(1)}, u32[]{:S(2)}, u32[]{:S(2)}) collective-permute-start(f32[2,8,128]{2,1,0:T(8,128)S(1)} %shard_map.69.final), channel_id=1, source_target_pairs={{0,63},{1,2},{2,1},{3,4},{4,3},{5,6},{6,5},{7,8},{8,7},{9,10},{10,... | collective-permute-start | bytes 24584 | tf_op jit(solution)/shard_map/ppermute | solution.py:46
  39.6 0.0 collective-permute-done.4.side
  39.6 0.0 collective-permute-done.5.side_final
  39.6 4.6 %shard_map.70 = (f32[8,128,256]{2,1,0:T(8,128)S(1)}, bf16[8,128,128]{2,1,0:T(8,128)(2,1)S(1)}) custom-call(bf16[8,256,256]{2,1,0:T(8,128)(2,1)S(1)} %get-tuple-element.12.diag, bf16[1280,256]{1,0:T(8,128)(2,1)S(1)} %get-tuple-element.10.kv_own, bf16[128,1280]{1,0:T(8,128)(2,1)S(1)} %get-tuple-element.14.kt_own, ...), custom_call_target="tpu_custom_call" | custom-call | flops 1509949440 | bytes 4931584 | tf_op jit(solution)/shard_map/pallas_call | solution.py:62
  44.3 0.0 collective-permute-done.side
  44.3 0.0 collective-permute-done.3.final
  44.3 1.3 %shard_map.71 = bf16[8,3,128,128]{3,2,1,0:T(8,128)(2,1)S(1)} custom-call(bf16[1280,256]{1,0:T(8,128)(2,1)S(1)} %get-tuple-element.10.kv_own, bf16[8,128,256]{2,1,0:T(8,128)(2,1)S(1)} %collective-permute-done.side, f32[2,8,128]{2,1,0:T(8,128)S(1)} %collective-permute-done.3.final, f32[8,128,256]{2,1,0:T(8,128)S(1)} %get-tuple-element.15.before, ...), custom_call_target="tpu_custom_call" | custom-call | flops 402653184 | bytes 3284992 | tf_op jit(solution)/shard_map/pallas_call | solution.py:62
  45.6 14.6 %all_to_all.11.tile = bf16[8,3,128,128]{3,2,1,0:T(8,128)(2,1)S(1)} all-to-all(bf16[8,3,128,128]{3,2,1,0:T(8,128)(2,1)S(1)} %shard_map.71), channel_id=1, replica_groups=mesh['x'=4,'l'=2,'h'=2,'z'=8,'c'=2] {'x','l'}, dimensions={0} | all-to-all | bytes 1572864 | tf_op jit(solution)/shard_map/all_to_all | solution.py:305
  60.1 1.0 %shard_map.72 = (bf16[1,128,1024]{2,1,0:T(8,128)(2,1)}, bf16[1,128,1024]{2,1,0:T(8,128)(2,1)}, bf16[1,128,1024]{2,1,0:T(8,128)(2,1)}) custom-call(s32[1]{0:T(128)} %bitcast.swap, bf16[8,3,128,128]{3,2,1,0:T(8,128)(2,1)S(1)} %all_to_all.11.tile), custom_call_target="tpu_custom_call" | custom-call | bytes 1572868 | tf_op jit(solution)/shard_map/pallas_call | solution.py:62
  (1 shorter events, 0.0 us)
Async XLA Ops:
  22.3 11.9 %collective-permute-start.1 = (bf16[8,128,256]{2,1,0:T(8,128)(2,1)S(1)}, bf16[8,128,256]{2,1,0:T(8,128)(2,1)S(1)}, u32[]{:S(2)}, u32[]{:S(2)}) collective-permute-start(bf16[8,128,256]{2,1,0:T(8,128)(2,1)S(1)} %slice_bitcast_fusion), channel_id=1, source_target_pairs={{0,63},{1,2},{2,1},{3,4},{4,3},{5,6},{6,5},{7,8},{8,7},{9,10},{10,... | collective-permute-start | bytes 1572872 | tf_op jit(solution)/shard_map/ppermute | solution.py:46
  27.3 6.9 %collective-permute-start.2 = (bf16[8,128,256]{2,1,0:T(8,128)(2,1)S(1)}, bf16[8,128,256]{2,1,0:T(8,128)(2,1)S(1)}, u32[]{:S(2)}, u32[]{:S(2)}) collective-permute-start(bf16[8,128,256]{2,1,0:T(8,128)(2,1)S(1)} %slice_bitcast_fusion), channel_id=1, source_target_pairs={{0,1},{1,0},{2,3},{3,2},{4,5},{5,4},{6,7},{7,6},{8,9},{9,8},{10,11... | collective-permute-start | bytes 1572872 | tf_op jit(solution)/shard_map/ppermute | solution.py:46
  28.3 11.3 %collective-permute-start.4 = (bf16[8,128,256]{2,1,0:T(8,128)(2,1)S(1)}, bf16[8,128,256]{2,1,0:T(8,128)(2,1)S(1)}, u32[]{:S(2)}, u32[]{:S(2)}) collective-permute-start(bf16[8,128,256]{2,1,0:T(8,128)(2,1)S(1)} %get-tuple-element.11), channel_id=1, source_target_pairs={{0,1},{1,0},{2,3},{3,2},{4,5},{5,4},{6,7},{7,6},{8,9},{9,8},{10,11... | collective-permute-start | bytes 1572872 | tf_op jit(solution)/shard_map/ppermute | solution.py:46
  28.9 15.4 %collective-permute-start = (bf16[8,128,256]{2,1,0:T(8,128)(2,1)S(1)}, bf16[8,128,256]{2,1,0:T(8,128)(2,1)S(1)}, u32[]{:S(2)}, u32[]{:S(2)}) collective-permute-start(bf16[8,128,256]{2,1,0:T(8,128)(2,1)S(1)} %get-tuple-element.11), channel_id=1, source_target_pairs={{0,63},{1,2},{2,1},{3,4},{4,3},{5,6},{6,5},{7,8},{8,7},{9,10},{10,... | collective-permute-start | bytes 1572872 | tf_op jit(solution)/shard_map/ppermute | solution.py:46
  35.6 4.1 %collective-permute-start.5 = (f32[2,8,128]{2,1,0:T(8,128)S(1)}, f32[2,8,128]{2,1,0:T(8,128)S(1)}, u32[]{:S(2)}, u32[]{:S(2)}) collective-permute-start(f32[2,8,128]{2,1,0:T(8,128)S(1)} %shard_map.69.final), channel_id=1, source_target_pairs={{0,1},{1,0},{2,3},{3,2},{4,5},{5,4},{6,7},{7,6},{8,9},{9,8},{10,11... | collective-permute-start | bytes 24584 | tf_op jit(solution)/shard_map/ppermute | solution.py:46
  35.7 8.6 %collective-permute-start.3 = (f32[2,8,128]{2,1,0:T(8,128)S(1)}, f32[2,8,128]{2,1,0:T(8,128)S(1)}, u32[]{:S(2)}, u32[]{:S(2)}) collective-permute-start(f32[2,8,128]{2,1,0:T(8,128)S(1)} %shard_map.69.final), channel_id=1, source_target_pairs={{0,63},{1,2},{2,1},{3,4},{4,3},{5,6},{6,5},{7,8},{8,7},{9,10},{10,... | collective-permute-start | bytes 24584 | tf_op jit(solution)/shard_map/ppermute | solution.py:46
